TPU v7x, 256 devices: a whole 4x4x8 slice. The times are simulated.
256 devices in a mesh: dp: 128 (over z, y, x), ep: 2 (over core).
Axes of the slice: x: 4, y: 4, z: 8, core: 2. Of those that a mesh axis runs over, the one named last changes fastest.
Arguments:
- queries: bfloat16 [2048, 64, 576], P('dp'), may hold values from -65 to 65
- latent_cache: bfloat16 [2048, 256, 576], P('dp', 'ep'), may hold values from -6 to 6
- cache_lens: int32 [2048], P('dp'), may hold values from 2 to 256
- movers: int32 [128, 4], P('dp'), may hold values from 0 to 16, as said below
- hidden: bfloat16 [2048, 7168], P('dp'), may hold values from -6 to 6
- norm_gain: float32 [7168], replicated, may hold values from 0.1 to 1.9
- routes: int32 [2048, 8], P('dp'), may hold values from 0 to 31, all different within a row; in each aligned block of 16 rows (0 to 15, 16 to 31, ...) at most 8 rows name the same one
- gate_weights: bfloat16 [2048, 8], P('dp'), may hold values from 0.19921875 to 1
- gate_proj: bfloat16 [128, 7168, 256], P('dp', None, 'ep'), may hold values from -0.0625 to 0.0625
- up_proj: bfloat16 [128, 7168, 256], P('dp', None, 'ep'), may hold values from -0.0625 to 0.0625
- down_proj: bfloat16 [128, 1024, 1792], P('dp', None, 'ep'), may hold values from -0.1875 to 0.1875
Outputs:
- served: bfloat16 [2560, 64, 512], P('dp', 'ep')
- expert_mix: bfloat16 [2048, 7168], P('dp', 'ep')
Inputs may be any that keep to these rules, and one draw needn't show every extreme that they name: `movers`: row i lists distinct request slots of rank i, followed by 16 in unused entries; a rank whose partner (i + 64) mod 128 lists any slot lists none itself. `routes`: each row names 8 different experts; among the 16 rows of one dp rank no expert is named more than 8 times.
All inputs are finite; a program needn't handle non-finite values.
Results may differ from a plain program's by a relative error of at most 0.015.
Values may be sent and summed in bfloat16 or wider, within the bound.
No kernel may reach another device: no remote copies, remote signals or barrier semaphores. Data moves between devices by JAX's collectives and lax.ppermute only.
A program may use at most 128 MiB of HBM per device.

v0:
```python
import jax
import jax.numpy as jnp
from jax import lax
from jax.experimental import pallas as pl
from jax.experimental.pallas import tpu as pltpu
from jax.sharding import Mesh, PartitionSpec as P

LAT = 512
EXPERTS = 32
CAP = 8
PLANE = ("z", "y")
SOFTMAX_SCALE = 192 ** (-0.5)
BF = jnp.bfloat16
F32 = jnp.float32


def shifted(x, axis, by):
    devices = lax.axis_size(axis)
    return lax.ppermute(x, axis, [(i, (i + by) % devices) for i in range(devices)])


def attend(queries, latent_cache, lengths, core):
    span = latent_cache.shape[1]
    heads = queries.shape[1] // 2
    scores = jnp.einsum("shc,stc->sht", queries, latent_cache, preferred_element_type=F32)
    scores = scores * SOFTMAX_SCALE
    positions = core * span + jnp.arange(span, dtype=jnp.int32)
    valid = positions[None, None, :] < lengths[:, None, None]
    masked = jnp.where(valid, scores, -1e30)
    peak = jnp.max(masked, axis=2)
    weights = jnp.where(valid, jnp.exp(masked - peak[:, :, None]), 0.0)
    total = jnp.sum(weights, axis=2)
    numerator = jnp.einsum(
        "sht,stc->shc", weights.astype(BF), latent_cache[:, :, :LAT], preferred_element_type=F32
    )

    def mine(a):
        return lax.dynamic_slice_in_dim(a, core * heads, heads, 1)

    def other(a):
        return lax.dynamic_slice_in_dim(a, (1 - core) * heads, heads, 1)

    far_numerator = shifted(other(numerator).astype(BF), "ep", 1).astype(F32)
    far_stats = shifted(jnp.stack([other(peak), other(total)]), "ep", 1)
    near_peak, far_peak = mine(peak), far_stats[0]
    both = jnp.maximum(near_peak, far_peak)
    near_scale, far_scale = jnp.exp(near_peak - both), jnp.exp(far_peak - both)
    denominator = near_scale * mine(total) + far_scale * far_stats[1]
    combined = (
        near_scale[:, :, None] * mine(numerator) + far_scale[:, :, None] * far_numerator
    )
    return (combined / denominator[:, :, None]).astype(BF)


def slot_rows(core, hidden, norm_gain, routes, gate_weights):
    requests, model_width = hidden.shape
    half = model_width // 2
    slots = EXPERTS * CAP

    def kernel(core_ref, all_ref, half_ref, gain_ref, routes_ref, gates_ref, out_ref, mix_ref):
        del core_ref
        ids = routes_ref[...].astype(F32)
        gates = gates_ref[...].astype(F32)
        lane = lax.broadcasted_iota(jnp.int32, (requests, slots), 1)
        expert = (lane >> 3).astype(F32)
        member = jnp.zeros((requests, slots), F32)
        weight = jnp.zeros((requests, slots), F32)
        for k in range(routes.shape[1]):
            hit = ids[:, k : k + 1] == expert
            member = jnp.where(hit, 1.0, member)
            weight = jnp.where(hit, gates[:, k : k + 1], weight)
        left = lax.broadcasted_iota(jnp.int32, (requests, requests), 0)
        right = lax.broadcasted_iota(jnp.int32, (requests, requests), 1)
        lower = jnp.where(right < left, 1.0, 0.0).astype(BF)
        earlier = jnp.dot(lower, member.astype(BF), preferred_element_type=F32)
        fits = (member > 0.5) & (earlier == (lane & 7).astype(F32))
        mix_ref[...] = jnp.where(fits, weight, 0.0).astype(BF)
        chosen = jnp.where(fits, 1.0, 0.0).astype(BF)
        wide = all_ref[...].astype(F32)
        inverse = lax.rsqrt(jnp.mean(wide * wide, axis=1, keepdims=True) + 1e-06)
        for start in range(0, half, 512):
            columns = slice(start, start + 512)
            normed = half_ref[:, columns].astype(F32) * inverse * gain_ref[:, columns]
            out_ref[:, columns] = lax.dot_general(
                chosen, normed.astype(BF), (((0,), (0,)), ((), ())), preferred_element_type=F32
            ).astype(BF)

    return pl.pallas_call(
        kernel,
        out_shape=(
            jax.ShapeDtypeStruct((slots, half), BF),
            jax.ShapeDtypeStruct((requests, slots), BF),
        ),
        grid_spec=pltpu.PrefetchScalarGridSpec(
            num_scalar_prefetch=1,
            grid=(1,),
            in_specs=[
                pl.BlockSpec((requests, model_width), lambda i, c: (0, 0)),
                pl.BlockSpec((requests, half), lambda i, c: (0, c[0])),
                pl.BlockSpec((1, half), lambda i, c: (0, c[0])),
                pl.BlockSpec(routes.shape, lambda i, c: (0, 0)),
                pl.BlockSpec(gate_weights.shape, lambda i, c: (0, 0)),
            ],
            out_specs=(
                pl.BlockSpec((slots, half), lambda i, c: (0, 0)),
                pl.BlockSpec((requests, slots), lambda i, c: (0, 0)),
            ),
        ),
    )(core.reshape(1), hidden, hidden, norm_gain.reshape(1, -1), routes, gate_weights)


def local(
    queries,
    latent_cache,
    cache_lens,
    movers,
    hidden,
    norm_gain,
    routes,
    gate_weights,
    gate_proj,
    up_proj,
    down_proj,
):
    requests, model_width = hidden.shape
    half = model_width // 2
    count = EXPERTS * CAP
    core = lax.axis_index("ep")
    x_index = lax.axis_index("x")

    outbound, combine = slot_rows(core, hidden, norm_gain, routes, gate_weights)
    rows = lax.all_to_all(
        outbound.reshape(EXPERTS, CAP, half), PLANE, split_axis=0, concat_axis=0, tiled=True
    ).reshape(count, half)

    ahead, behind = shifted(rows, "x", 1), shifted(rows, "x", -1)
    rows, gate_proj, up_proj, down_proj, hidden, queries, latent_cache, movers = (
        lax.optimization_barrier(
            (rows, gate_proj, up_proj, down_proj, hidden, queries, latent_cache, movers)
        )
    )

    both = jnp.concatenate([gate_proj[0], up_proj[0]], axis=1)
    far_weights = lax.dynamic_slice_in_dim(both, (1 - core) * half, half, 0)
    near_weights = lax.dynamic_slice_in_dim(both, core * half, half, 0)
    mixed = jnp.concatenate([near_weights, shifted(far_weights, "ep", 1)], axis=1)

    attention = attend(queries, latent_cache, cache_lens, core)
    listed = movers[0]
    slot_ids = jnp.arange(requests, dtype=jnp.int32)
    flagged = jnp.any(slot_ids[:, None] == listed[None, :], axis=1)
    nothing = jnp.zeros((), BF)
    picks = (listed[:, None] == slot_ids[None, :]).astype(BF)
    moved = jnp.einsum("mr,rhd->mhd", picks, attention, preferred_element_type=F32).astype(BF)
    arrived_contexts = shifted(moved, "z", 4)
    served = jnp.concatenate(
        [jnp.where(flagged[:, None, None], nothing, attention), arrived_contexts], axis=0
    )

    def down_rows(which):
        parts = []
        for by in range(4):
            source = (x_index + by) % 4
            parts.append(
                lax.dynamic_slice_in_dim(down_proj[0], source * 256 + which * 128, 128, 0)
            )
        return jnp.concatenate(parts, axis=0)

    near_down, far_down = down_rows(core), down_rows(1 - core)

    def activate(blocks):
        total = [jnp.dot(b, mixed, preferred_element_type=F32) for b in blocks]
        total = jnp.concatenate(total, axis=0)
        value = total[:, :256] + shifted(total[:, 256:], "ep", 1)
        activated = (jax.nn.silu(value[:, :128]) * value[:, 128:]).astype(BF)
        return activated.reshape(-1, count, 128)

    def spread_along_x(activated):
        return [activated] + [shifted(activated, "x", -by) for by in (1, 2, 3)]

    own = spread_along_x(activate([rows]))
    ahead, behind, own, served = lax.optimization_barrier((ahead, behind, own, served))
    middle = count // 2
    across = [shifted(ahead[:middle], "x", 1), shifted(behind[middle:], "x", -1)]
    near = spread_along_x(activate([ahead, behind]))
    across, near = lax.optimization_barrier((across, near))
    far = spread_along_x(activate([jnp.concatenate(across, axis=0)]))

    by_home = [
        [a[0] for a in own],
        [a[1] for a in near],
        [a[0] for a in far],
        [a[0] for a in near],
    ]
    stripes = [
        jnp.concatenate([by_home[(r - s) % 4][s] for s in range(4)], axis=1) for r in range(4)
    ]
    twice = jnp.concatenate(stripes + stripes[:3], axis=0)
    joined = lax.dynamic_slice_in_dim(twice, (4 - x_index) % 4 * count, 4 * count, 0)
    expert_out = (
        jnp.dot(joined, near_down, preferred_element_type=F32)
        + jnp.dot(shifted(joined, "ep", 1), far_down, preferred_element_type=F32)
    ).astype(BF)
    returned = lax.all_to_all(
        expert_out.reshape(4 * EXPERTS, CAP, -1),
        ("x",) + PLANE,
        split_axis=0,
        concat_axis=0,
        tiled=True,
    )
    weighted = jnp.einsum(
        "rk,qkd->rqd",
        combine,
        returned.reshape(4, count, -1),
        preferred_element_type=F32,
    ).reshape(requests, half)
    own_hidden = lax.dynamic_slice_in_dim(hidden, core * half, half, 1).astype(F32)
    expert_mix = (own_hidden + weighted).astype(BF)
    return served, expert_mix


def solution(mesh):
    grid = Mesh(mesh.devices.reshape(8, 4, 4, 2), ("z", "y", "x", "ep"))
    dp = ("z", "y", "x")
    placed = (
        P(dp, None, None),
        P(dp, "ep", None),
        P(dp),
        P(dp, None),
        P(dp, None),
        P(),
        P(dp, None),
        P(dp, None),
        P(dp, None, "ep"),
        P(dp, None, "ep"),
        P(dp, None, "ep"),
    )
    return jax.shard_map(
        local,
        mesh=grid,
        in_specs=placed,
        out_specs=(P(dp, "ep", None), P(dp, "ep")),
        check_vma=False,
    )
```

profile of v0, /device:TPU:32, one launch (start us, length us, event | category | flops | bytes accessed | tf_op | source)
XLA Modules:
  0.0 235.7 jit_solution(4558309714823730495)
XLA Ops:
  0.6 1.5 copy.29.routes_ref
  2.1 1.3 copy.30.gates_ref
  3.5 3.2 %shard_map.122 = (bf16[256,3584]{1,0:T(8,128)(2,1)}, bf16[16,256]{1,0:T(8,128)(2,1)}) custom-call(s32[1]{0:T(128)} %bitcast.core_ref, bf16[16,7168]{1,0:T(8,128)(2,1)} %half_ref.1, bf16[16,7168]{1,0:T(8,128)(2,1)} %half_ref.1, f32[1,7168]{1,0:T(1,128)} %bitcast.111, s32[16,8]{1,0:T(8,128)} %copy.29.routes_ref, bf16[16,8]{1,0:T(8,128)(2,1)} %copy.30.gates_ref), custom_call_target="tpu_custom_call" | custom-call | tf_op jit(solution)/shard_map/pallas_call | solution.py:88
  6.6 11.4 %all-to-all-start = ((bf16[32,8,3584]{2,1,0:T(8,128)(2,1)}), bf16[32,8,3584]{2,1,0:T(8,128)(2,1)S(1)}, u32[]{:S(2)}, u32[]{:S(2)}) async-start(bf16[32,8,3584]{2,1,0:T(8,128)(2,1)} %bitcast.92), calls=%async_computation | async-start | bytes 3670016 | tf_op jit(solution)/shard_map/all_to_all | solution.py:132
  18.0 44.0 %all-to-all-done = bf16[32,8,3584]{2,1,0:T(8,128)(2,1)S(1)} async-done(((bf16[32,8,3584]{2,1,0:T(8,128)(2,1)}), bf16[32,8,3584]{2,1,0:T(8,128)(2,1)S(1)}, u32[]{:S(2)}, u32[]{:S(2)}) %all-to-all-start) | async-done | bytes 1835040 | tf_op jit(solution)/shard_map/all_to_all | solution.py:132
  62.0 4.3 %fusion.4 = (bf16[3584,256]{1,0:T(8,128)(2,1)}, bf16[3584,256]{1,0:T(8,128)(2,1)}) fusion(s32[]{:T(128)S(6)} %select_n.86, bf16[7168,128]{1,0:T(8,128)(2,1)} %bitcast.93, bf16[7168,128]{1,0:T(8,128)(2,1)} %bitcast.94, s32[]{:T(128)S(6)} %select_n.87), kind=kLoop, calls=%fused_computation.11 | loop fusion | flops 7340032 | bytes 7340040 | tf_op jit(solution)/shard_map/concatenate | solution.py:143
  66.4 1.5 collective-permute-start
  68.0 1.7 collective-permute-start.1
  69.7 4.3 %copy.31 = bf16[16,128,576]{2,1,0:T(8,128)(2,1)} copy(bf16[16,128,576]{1,2,0:T(8,128)(2,1)} %param.12) | data formatting | bytes 4718592 | tf_op jit(solution)/shard_map/optimization_barrier | solution.py:138
  74.0 2.5 %fusion.63 = (f32[16,64]{1,0:T(8,128)S(1)}, f32[16,64,128]{2,1,0:T(8,128)S(1)}) fusion(bf16[16,64,576]{2,1,0:T(8,128)(2,1)S(1)} %copy-done, bf16[16,128,576]{1,2,0:T(8,128)(2,1)} %param.12, pred[16,128]{1,0:T(8,128)(4,1)S(1)} %broadcast_compare_fusion), kind=kOutput, calls=%fused_computation.113 | convolution fusion | flops 151387136 | bytes 4069376 | tf_op jit(solution)/shard_map/shc,stc->sht/dot_general | solution.py:25
  78.5 2.6 %fusion.60 = f32[256,512]{1,0:T(8,128)S(1)} fusion(bf16[256,3584]{1,0:T(8,128)(2,1)S(1)} %bitcast.91, bf16[3584,256]{1,0:T(8,128)(2,1)} %collective-permute-done.2, bf16[3584,256]{1,0:T(8,128)(2,1)S(1)} %copy-done.3), kind=kOutput, calls=%fused_computation.112 | convolution fusion | flops 946864128 | bytes 6029312 | tf_op jit(solution)/shard_map/dot_general | solution.py:172
  82.1 1.5 collective-permute-start.9
  83.7 1.6 collective-permute-start.4
  86.2 8.6 %collective-permute-done.9 = bf16[4,32,512]{2,1,0:T(8,128)(2,1)S(1)} collective-permute-done((bf16[4,32,512]{2,1,0:T(8,128)(2,1)S(1)}, bf16[4,32,512]{2,1,0:T(8,128)(2,1)S(1)}, u32[]{:S(2)}, u32[]{:S(2)}) %collective-permute-start.9) | collective-permute-done | bytes 131104 | tf_op jit(solution)/shard_map/ppermute | solution.py:19
  96.0 14.6 %collective-permute-done = bf16[256,3584]{1,0:T(8,128)(2,1)} collective-permute-done((bf16[256,3584]{1,0:T(8,128)(2,1)S(1)}, bf16[256,3584]{1,0:T(8,128)(2,1)}, u32[]{:S(2)}, u32[]{:S(2)}) %collective-permute-start) | collective-permute-done | bytes 1835040 | tf_op jit(solution)/shard_map/ppermute | solution.py:19
  110.9 1.3 collective-permute-done.4
  112.9 3.2 %fusion.59 = f32[256,512]{1,0:T(8,128)S(1)} fusion(bf16[256,3584]{1,0:T(8,128)(2,1)} %collective-permute-done, bf16[3584,256]{1,0:T(8,128)(2,1)} %collective-permute-done.2, bf16[3584,256]{1,0:T(8,128)(2,1)S(1)} %copy-done.3), kind=kOutput, calls=%fused_computation.111 | convolution fusion | flops 946864128 | bytes 6029312 | tf_op jit(solution)/shard_map/dot_general | solution.py:172
  116.1 3.2 %fusion.58 = f32[256,512]{1,0:T(8,128)S(1)} fusion(bf16[256,3584]{1,0:T(8,128)(2,1)} %collective-permute-done.1, bf16[3584,256]{1,0:T(8,128)(2,1)} %collective-permute-done.2, bf16[3584,256]{1,0:T(8,128)(2,1)S(1)} %copy-done.3), kind=kOutput, calls=%fused_computation.110 | convolution fusion | flops 946864128 | bytes 6029312 | tf_op jit(solution)/shard_map/dot_general | solution.py:172
  119.4 2.2 slice.82
  121.5 2.3 slice.83
  123.8 2.1 collective-permute-start.10
  127.2 1.8 collective-permute-start.13
  130.3 21.9 %collective-permute-done.13 = bf16[2,256,128]{2,1,0:T(8,128)(2,1)} collective-permute-done((bf16[2,256,128]{2,1,0:T(8,128)(2,1)S(1)}, bf16[2,256,128]{2,1,0:T(8,128)(2,1)}, u32[]{:S(2)}, u32[]{:S(2)}) %collective-permute-start.13) | collective-permute-done | bytes 131104 | tf_op jit(solution)/shard_map/ppermute | solution.py:19
  153.7 3.2 %fusion.5 = f32[256,512]{1,0:T(8,128)S(1)} fusion(bf16[128,3584]{1,0:T(8,128)(2,1)} %collective-permute-done.11, bf16[128,3584]{1,0:T(8,128)(2,1)} %collective-permute-done.10, bf16[3584,256]{1,0:T(8,128)(2,1)} %collective-permute-done.2, bf16[3584,256]{1,0:T(8,128)(2,1)S(1)} %copy-done.4), kind=kOutput, calls=%fused_computation.12 | convolution fusion | flops 950534144 | bytes 6029312 | tf_op jit(solution)/shard_map/dot_general | solution.py:172
  159.8 1.3 collective-permute-start.17
  161.1 2.9 %collective-permute-start.18 = (bf16[1,256,128]{2,1,0:T(8,128)(2,1)S(1)}, bf16[1,256,128]{2,1,0:T(8,128)(2,1)S(1)}, u32[]{:S(2)}, u32[]{:S(2)}) collective-permute-start(bf16[1,256,128]{2,1,0:T(8,128)(2,1)S(1)} %fusion.73), channel_id=1, source_target_pairs={{0,2},{2,4},{4,6},{6,0},{1,3},{3,5},{5,7},{7,1},{8,10},{10,12},{12... | collective-permute-start | bytes 196616 | tf_op jit(solution)/shard_map/ppermute | solution.py:19
  165.9 1.4 collective-permute-done.18
  170.5 2.5 %fusion.11 = f32[1024,896]{1,0:T(8,128)S(1)} fusion(bf16[1024,512]{1,0:T(8,128)(2,1)} %constant_dynamic-slice_fusion, bf16[128,896]{1,0:T(8,128)(2,1)S(1)} %get-tuple-element.59, bf16[128,896]{1,0:T(8,128)(2,1)S(1)} %get-tuple-element.60, bf16[128,896]{1,0:T(8,128)(2,1)S(1)} %get-tuple-element.61, bf16[128,896]{1,0:T(8,128)(2,1)S(1)} %get-tuple-element.62), kind=kOutput, calls=%fused_computation.23 | convolution fusion | flops 943194112 | bytes 5636096 | tf_op jit(solution)/shard_map/dot_general | solution.py:201
  173.0 2.5 %fusion.9 = bf16[128,8,896]{2,1,0:T(8,128)(2,1)S(1)} fusion(f32[1024,896]{1,0:T(8,128)S(1)} %fusion.11, bf16[1024,512]{1,0:T(8,128)(2,1)} %collective-permute-done.20, bf16[128,896]{1,0:T(8,128)(2,1)S(1)} %get-tuple-element.56, bf16[128,896]{1,0:T(8,128)(2,1)S(1)} %get-tuple-element.57, bf16[128,896]{1,0:T(8,128)(2,1)S(1)} %get-tuple-element.58, ...), kind=kOutput, calls=%fused_computation.16 | convolution fusion | flops 945029120 | bytes 7471104 | tf_op jit(solution)/shard_map/dot_general | solution.py:202
  175.5 56.1 %all_to_all.10 = bf16[128,8,896]{2,1,0:T(8,128)(2,1)} all-to-all(bf16[128,8,896]{2,1,0:T(8,128)(2,1)S(1)} %fusion.9), channel_id=1, replica_groups=mesh['z'=8,'y'=4,'x'=4,'ep'=2] {'x','z','y'}, dimensions={0} | all-to-all | bytes 3670016 | tf_op jit(solution)/shard_map/all_to_all | solution.py:204
  231.6 2.8 %copy.34 = bf16[4,896,256]{2,1,0:T(8,128)(2,1)S(1)} copy(bf16[4,896,256]{1,2,0:T(8,128)(2,1)} %bitcast.88) | data formatting | bytes 3670016 | tf_op jit(solution)/shard_map/rk,qkd->rqd/dot_general | solution.py:211
  234.4 1.2 fusion
  (83 shorter events, 18.0 us)
Async XLA Ops:
  0.6 73.4 %copy-start = (bf16[16,64,576]{2,1,0:T(8,128)(2,1)S(1)}, bf16[16,64,576]{2,1,0:T(8,128)(2,1)}, u32[]{:S(2)}) copy-start(bf16[16,64,576]{2,1,0:T(8,128)(2,1)} %param.11) | copy-start | bytes 3538948
  6.6 55.4 %all-to-all-start = ((bf16[32,8,3584]{2,1,0:T(8,128)(2,1)}), bf16[32,8,3584]{2,1,0:T(8,128)(2,1)S(1)}, u32[]{:S(2)}, u32[]{:S(2)}) async-start(bf16[32,8,3584]{2,1,0:T(8,128)(2,1)} %bitcast.92), calls=%async_computation | async-start | bytes 3670016 | tf_op jit(solution)/shard_map/all_to_all | solution.py:132
  62.0 4.4 %copy-start.7 = (s32[16]{0:T(128)S(1)}, s32[16]{0:T(128)}, u32[]{:S(2)}) copy-start(s32[16]{0:T(128)} %param.13) | copy-start | bytes 196
  66.3 12.1 %collective-permute-start.2 = (bf16[3584,256]{1,0:T(8,128)(2,1)}, bf16[3584,256]{1,0:T(8,128)(2,1)}, u32[]{:S(2)}, u32[]{:S(2)}) collective-permute-start(bf16[3584,256]{1,0:T(8,128)(2,1)} %get-tuple-element.54), channel_id=1, source_target_pairs={{0,1},{1,0},{2,3},{3,2},{4,5},{5,4},{6,7},{7,6},{8,9},{9,8},{10,11... | collective-permute-start | bytes 5505032 | tf_op jit(solution)/shard_map/ppermute | solution.py:19
  66.4 44.1 %collective-permute-start = (bf16[256,3584]{1,0:T(8,128)(2,1)S(1)}, bf16[256,3584]{1,0:T(8,128)(2,1)}, u32[]{:S(2)}, u32[]{:S(2)}) collective-permute-start(bf16[256,3584]{1,0:T(8,128)(2,1)S(1)} %bitcast.89), channel_id=1, source_target_pairs={{0,2},{2,4},{4,6},{6,0},{1,3},{3,5},{5,7},{7,1},{8,10},{10,12},{12... | collective-permute-start | bytes 5505032 | tf_op jit(solution)/shard_map/ppermute | solution.py:19
  68.0 43.0 %collective-permute-start.1 = (bf16[256,3584]{1,0:T(8,128)(2,1)S(1)}, bf16[256,3584]{1,0:T(8,128)(2,1)}, u32[]{:S(2)}, u32[]{:S(2)}) collective-permute-start(bf16[256,3584]{1,0:T(8,128)(2,1)S(1)} %bitcast.90), channel_id=1, source_target_pairs={{0,6},{2,0},{4,2},{6,4},{1,7},{3,1},{5,3},{7,5},{8,14},{10,8},{12,... | collective-permute-start | bytes 5505032 | tf_op jit(solution)/shard_map/ppermute | solution.py:19
  74.0 3.1 %copy-start.1 = (bf16[16,128,576]{2,1,0:T(8,128)(2,1)S(1)}, bf16[16,128,576]{2,1,0:T(8,128)(2,1)}, u32[]{:S(2)}) copy-start(bf16[16,128,576]{2,1,0:T(8,128)(2,1)} %copy.31) | copy-start | bytes 7077892
  77.0 1.3 copy-start.8
  77.0 1.5 copy-start.3
  77.0 1.4 collective-permute-start.7
  77.7 3.6 %collective-permute-start.8 = (bf16[16,32,512]{2,1,0:T(8,128)(2,1)S(1)}, bf16[16,32,512]{2,1,0:T(8,128)(2,1)S(1)}, u32[]{:S(2)}, u32[]{:S(2)}) collective-permute-start(bf16[16,32,512]{2,1,0:T(8,128)(2,1)S(1)} %dynamic-slice_convert_fusion), channel_id=1, source_target_pairs={{0,1},{1,0},{2,3},{3,2},{4,5},{5,4},{6,7},{7,6},{8,9},{9,8},{10,11... | collective-permute-start | bytes 1572872 | tf_op jit(solution)/shard_map/ppermute | solution.py:19
  81.2 2.5 %collective-permute-start.3 = (f32[256,256]{1,0:T(8,128)S(1)}, f32[256,256]{1,0:T(8,128)S(1)}, u32[]{:S(2)}, u32[]{:S(2)}) collective-permute-start(f32[256,256]{1,0:T(8,128)S(1)} %slice.101), channel_id=1, source_target_pairs={{0,1},{1,0},{2,3},{3,2},{4,5},{5,4},{6,7},{7,6},{8,9},{9,8},{10,11... | collective-permute-start | bytes 786440 | tf_op jit(solution)/shard_map/ppermute | solution.py:19
  82.1 12.7 %collective-permute-start.9 = (bf16[4,32,512]{2,1,0:T(8,128)(2,1)S(1)}, bf16[4,32,512]{2,1,0:T(8,128)(2,1)S(1)}, u32[]{:S(2)}, u32[]{:S(2)}) collective-permute-start(bf16[4,32,512]{2,1,0:T(8,128)(2,1)S(1)} %copy.38), channel_id=1, source_target_pairs={{0,128},{32,160},{64,192},{96,224},{128,0},{160,32},{192,64},{224,... | collective-permute-start | bytes 393224 | tf_op jit(solution)/shard_map/ppermute | solution.py:19
  83.7 28.4 %collective-permute-start.4 = (bf16[1,256,128]{2,1,0:T(8,128)(2,1)S(1)}, bf16[1,256,128]{2,1,0:T(8,128)(2,1)S(1)}, u32[]{:S(2)}, u32[]{:S(2)}) collective-permute-start(bf16[1,256,128]{2,1,0:T(8,128)(2,1)S(1)} %fusion.39), channel_id=1, source_target_pairs={{0,6},{2,0},{4,2},{6,4},{1,7},{3,1},{5,3},{7,5},{8,14},{10,8},{12,... | collective-permute-start | bytes 196616 | tf_op jit(solution)/shard_map/ppermute | solution.py:19
  85.4 27.5 %collective-permute-start.5 = (bf16[1,256,128]{2,1,0:T(8,128)(2,1)S(1)}, bf16[1,256,128]{2,1,0:T(8,128)(2,1)S(1)}, u32[]{:S(2)}, u32[]{:S(2)}) collective-permute-start(bf16[1,256,128]{2,1,0:T(8,128)(2,1)S(1)} %fusion.39), channel_id=1, source_target_pairs={{0,4},{2,6},{4,0},{6,2},{1,5},{3,7},{5,1},{7,3},{8,12},{10,14},{12... | collective-permute-start | bytes 196616 | tf_op jit(solution)/shard_map/ppermute | solution.py:19
  94.8 18.1 %collective-permute-start.6 = (bf16[1,256,128]{2,1,0:T(8,128)(2,1)S(1)}, bf16[1,256,128]{2,1,0:T(8,128)(2,1)S(1)}, u32[]{:S(2)}, u32[]{:S(2)}) collective-permute-start(bf16[1,256,128]{2,1,0:T(8,128)(2,1)S(1)} %fusion.39), channel_id=1, source_target_pairs={{0,2},{2,4},{4,6},{6,0},{1,3},{3,5},{5,7},{7,1},{8,10},{10,12},{12... | collective-permute-start | bytes 196616 | tf_op jit(solution)/shard_map/ppermute | solution.py:19
  119.3 7.8 %collective-permute-start.12 = (f32[512,256]{1,0:T(8,128)S(1)}, f32[512,256]{1,0:T(8,128)S(1)}, u32[]{:S(2)}, u32[]{:S(2)}) collective-permute-start(f32[512,256]{1,0:T(8,128)S(1)} %pad_maximum_fusion.2), channel_id=1, source_target_pairs={{0,1},{1,0},{2,3},{3,2},{4,5},{5,4},{6,7},{7,6},{8,9},{9,8},{10,11... | collective-permute-start | bytes 1572872 | tf_op jit(solution)/shard_map/ppermute | solution.py:19
  123.8 29.9 %copy-start.4 = (bf16[3584,256]{1,0:T(8,128)(2,1)S(1)}, bf16[3584,256]{1,0:T(8,128)(2,1)}, u32[]{:S(2)}) copy-start(bf16[3584,256]{1,0:T(8,128)(2,1)} %get-tuple-element.53) | copy-start | bytes 5505028
  123.8 29.9 %collective-permute-start.10 = (bf16[128,3584]{1,0:T(8,128)(2,1)}, bf16[128,3584]{1,0:T(8,128)(2,1)}, u32[]{:S(2)}, u32[]{:S(2)}) collective-permute-start(bf16[128,3584]{1,0:T(8,128)(2,1)} %slice.82), channel_id=1, source_target_pairs={{0,2},{2,4},{4,6},{6,0},{1,3},{3,5},{5,7},{7,1},{8,10},{10,12},{12... | collective-permute-start | bytes 2752520 | tf_op jit(solution)/shard_map/ppermute | solution.py:19
  125.9 27.8 %collective-permute-start.11 = (bf16[128,3584]{1,0:T(8,128)(2,1)}, bf16[128,3584]{1,0:T(8,128)(2,1)}, u32[]{:S(2)}, u32[]{:S(2)}) collective-permute-start(bf16[128,3584]{1,0:T(8,128)(2,1)} %slice.83), channel_id=1, source_target_pairs={{0,6},{2,0},{4,2},{6,4},{1,7},{3,1},{5,3},{7,5},{8,14},{10,8},{12,... | collective-permute-start | bytes 2752520 | tf_op jit(solution)/shard_map/ppermute | solution.py:19
  127.2 25.0 %collective-permute-start.13 = (bf16[2,256,128]{2,1,0:T(8,128)(2,1)S(1)}, bf16[2,256,128]{2,1,0:T(8,128)(2,1)}, u32[]{:S(2)}, u32[]{:S(2)}) collective-permute-start(bf16[2,256,128]{2,1,0:T(8,128)(2,1)S(1)} %bitcast.97), channel_id=1, source_target_pairs={{0,6},{2,0},{4,2},{6,4},{1,7},{3,1},{5,3},{7,5},{8,14},{10,8},{12,... | collective-permute-start | bytes 393224 | tf_op jit(solution)/shard_map/ppermute | solution.py:19
  129.1 23.4 %collective-permute-start.14 = (bf16[2,256,128]{2,1,0:T(8,128)(2,1)S(1)}, bf16[2,256,128]{2,1,0:T(8,128)(2,1)}, u32[]{:S(2)}, u32[]{:S(2)}) collective-permute-start(bf16[2,256,128]{2,1,0:T(8,128)(2,1)S(1)} %bitcast.98), channel_id=1, source_target_pairs={{0,4},{2,6},{4,0},{6,2},{1,5},{3,7},{5,1},{7,3},{8,12},{10,14},{12... | collective-permute-start | bytes 393224 | tf_op jit(solution)/shard_map/ppermute | solution.py:19
  130.3 23.4 %collective-permute-start.15 = (bf16[2,256,128]{2,1,0:T(8,128)(2,1)S(1)}, bf16[2,256,128]{2,1,0:T(8,128)(2,1)}, u32[]{:S(2)}, u32[]{:S(2)}) collective-permute-start(bf16[2,256,128]{2,1,0:T(8,128)(2,1)S(1)} %bitcast.99), channel_id=1, source_target_pairs={{0,2},{2,4},{4,6},{6,0},{1,3},{3,5},{5,7},{7,1},{8,10},{10,12},{12... | collective-permute-start | bytes 393224 | tf_op jit(solution)/shard_map/ppermute | solution.py:19
  156.9 2.8 %collective-permute-start.16 = (f32[256,256]{1,0:T(8,128)S(1)}, f32[256,256]{1,0:T(8,128)S(1)}, u32[]{:S(2)}, u32[]{:S(2)}) collective-permute-start(f32[256,256]{1,0:T(8,128)S(1)} %slice.112), channel_id=1, source_target_pairs={{0,1},{1,0},{2,3},{3,2},{4,5},{5,4},{6,7},{7,6},{8,9},{9,8},{10,11... | collective-permute-start | bytes 786440 | tf_op jit(solution)/shard_map/ppermute | solution.py:19
  159.8 6.1 %collective-permute-start.17 = (bf16[1,256,128]{2,1,0:T(8,128)(2,1)S(1)}, bf16[1,256,128]{2,1,0:T(8,128)(2,1)S(1)}, u32[]{:S(2)}, u32[]{:S(2)}) collective-permute-start(bf16[1,256,128]{2,1,0:T(8,128)(2,1)S(1)} %fusion.73), channel_id=1, source_target_pairs={{0,4},{2,6},{4,0},{6,2},{1,5},{3,7},{5,1},{7,3},{8,12},{10,14},{12... | collective-permute-start | bytes 196616 | tf_op jit(solution)/shard_map/ppermute | solution.py:19
  161.1 6.2 %collective-permute-start.18 = (bf16[1,256,128]{2,1,0:T(8,128)(2,1)S(1)}, bf16[1,256,128]{2,1,0:T(8,128)(2,1)S(1)}, u32[]{:S(2)}, u32[]{:S(2)}) collective-permute-start(bf16[1,256,128]{2,1,0:T(8,128)(2,1)S(1)} %fusion.73), channel_id=1, source_target_pairs={{0,2},{2,4},{4,6},{6,0},{1,3},{3,5},{5,7},{7,1},{8,10},{10,12},{12... | collective-permute-start | bytes 196616 | tf_op jit(solution)/shard_map/ppermute | solution.py:19
  164.1 4.3 %collective-permute-start.19 = (bf16[1,256,128]{2,1,0:T(8,128)(2,1)S(1)}, bf16[1,256,128]{2,1,0:T(8,128)(2,1)S(1)}, u32[]{:S(2)}, u32[]{:S(2)}) collective-permute-start(bf16[1,256,128]{2,1,0:T(8,128)(2,1)S(1)} %fusion.73), channel_id=1, source_target_pairs={{0,6},{2,0},{4,2},{6,4},{1,7},{3,1},{5,3},{7,5},{8,14},{10,8},{12,... | collective-permute-start | bytes 196616 | tf_op jit(solution)/shard_map/ppermute | solution.py:19
  168.5 1.9 copy-start.2
  169.7 3.3 %collective-permute-start.20 = (bf16[1024,512]{1,0:T(8,128)(2,1)}, bf16[1024,512]{1,0:T(8,128)(2,1)}, u32[]{:S(2)}, u32[]{:S(2)}) collective-permute-start(bf16[1024,512]{1,0:T(8,128)(2,1)} %constant_dynamic-slice_fusion), channel_id=1, source_target_pairs={{0,1},{1,0},{2,3},{3,2},{4,5},{5,4},{6,7},{7,6},{8,9},{9,8},{10,11... | collective-permute-start | bytes 3145736 | tf_op jit(solution)/shard_map/ppermute | solution.py:19
  231.6 2.8 %copy-start.5 = (bf16[16,7168]{1,0:T(8,128)(2,1)S(1)}, bf16[16,7168]{1,0:T(8,128)(2,1)}, u32[]{:S(2)}) copy-start(bf16[16,7168]{1,0:T(8,128)(2,1)} %half_ref.1) | copy-start | bytes 688132
  231.6 2.8 %copy-start.6 = (bf16[16,256]{1,0:T(8,128)(2,1)S(1)}, bf16[16,256]{1,0:T(8,128)(2,1)}, u32[]{:S(2)}) copy-start(bf16[16,256]{1,0:T(8,128)(2,1)} %get-tuple-element.34) | copy-start | bytes 24580
where the time goes:
time: 237 us; the launch traced here: 236 us
  waiting for transfers between devices  96.3 us (41%)
  blocking collectives  56.1 us (24%)
  starting transfers between devices  31.3 us (13%)
  matrix products  21.7 us (9%)
  local copies, waits for them, and re-layouts  19.2 us (8%)
  other arithmetic  6.92 us (3%)
  Pallas kernels  3.15 us (1%)
    all_to_all x1, blocking collectives, local(): lax.all_to_all(expert_out.reshape(4 * EXPERTS, CAP, -1), ('x',) + PLANE,...  56.1 us
    ppermute x21, waiting for transfers between devices, shifted(): lax.ppermute(x, axis, [(i, (i + by) % devices) for i in range(devices)])  52.3 us
    all_to_all x1, waiting for transfers between devices, local(): lax.all_to_all(outbound.reshape(EXPERTS, CAP, half), PLANE, split_axis=0,...  44 us
    ppermute x21, starting transfers between devices, shifted(): lax.ppermute(x, axis, [(i, (i + by) % devices) for i in range(devices)])  20 us
    dot_general x4, matrix products, activate(): total = [jnp.dot(b, mixed, preferred_element_type=F32) for b in blocks]  12.1 us
    all_to_all x1, starting transfers between devices, local(): lax.all_to_all(outbound.reshape(EXPERTS, CAP, half), PLANE, split_axis=0,...  11.4 us
  transfers between devices with their start and end apart: 22, of which 12 were waited for; matrix products, arithmetic and copies ran while one was open for 10% of the time, Pallas kernels for 0%

commit v1 on v0

v1 whole, which is shorter than its diff:
```python
import jax
import jax.numpy as jnp
from jax import lax
from jax.experimental import pallas as pl
from jax.experimental.pallas import tpu as pltpu
from jax.sharding import Mesh, PartitionSpec as P

LAT = 512
EXPERTS = 32
CAP = 8
AWAY = (0, 1, 7, 4, 2, 3, 6, 5)
SOFTMAX_SCALE = 192 ** (-0.5)
BF = jnp.bfloat16
F32 = jnp.float32


def shifted(x, axis, by):
    devices = lax.axis_size(axis)
    return lax.ppermute(x, axis, [(i, (i + by) % devices) for i in range(devices)])


def attend(queries, latent_cache, lengths, core):
    span = latent_cache.shape[1]
    heads = queries.shape[1] // 2
    scores = jnp.einsum("shc,stc->sht", queries, latent_cache, preferred_element_type=F32)
    scores = scores * SOFTMAX_SCALE
    positions = core * span + jnp.arange(span, dtype=jnp.int32)
    valid = positions[None, None, :] < lengths[:, None, None]
    masked = jnp.where(valid, scores, -1e30)
    peak = jnp.max(masked, axis=2)
    weights = jnp.where(valid, jnp.exp(masked - peak[:, :, None]), 0.0)
    total = jnp.sum(weights, axis=2)
    numerator = jnp.einsum(
        "sht,stc->shc", weights.astype(BF), latent_cache[:, :, :LAT], preferred_element_type=F32
    )

    def mine(a):
        return lax.dynamic_slice_in_dim(a, core * heads, heads, 1)

    def other(a):
        return lax.dynamic_slice_in_dim(a, (1 - core) * heads, heads, 1)

    far_numerator = shifted(other(numerator).astype(BF), "ep", 1).astype(F32)
    far_stats = shifted(jnp.stack([other(peak), other(total)]), "ep", 1)
    near_peak, far_peak = mine(peak), far_stats[0]
    both = jnp.maximum(near_peak, far_peak)
    near_scale, far_scale = jnp.exp(near_peak - both), jnp.exp(far_peak - both)
    denominator = near_scale * mine(total) + far_scale * far_stats[1]
    combined = (
        near_scale[:, :, None] * mine(numerator) + far_scale[:, :, None] * far_numerator
    )
    return (combined / denominator[:, :, None]).astype(BF)


def pack_rows(core, hidden, norm_gain, routes, gate_weights):
    requests, model_width = hidden.shape
    half = model_width // 2
    slots = EXPERTS * CAP
    top = routes.shape[1]

    def kernel(
        core_ref, all_ref, half_ref, gain_ref, routes_ref, ids_ref, gates_ref, out_ref, mix_ref
    ):
        del core_ref
        wide = all_ref[...].astype(F32)
        inverse = lax.rsqrt(jnp.mean(wide * wide, axis=1, keepdims=True) + 1e-06)
        normed = half_ref[...].astype(F32) * inverse * gain_ref[...]
        out_ref[:, :half] = normed.astype(BF)
        named = routes_ref[...].astype(F32)
        fill = jnp.full((requests, 128 - top), -1.0, F32)
        out_ref[:, half:] = jnp.concatenate([named, fill], axis=1).astype(BF)
        ids = ids_ref[...].astype(F32)
        gates = gates_ref[...].astype(F32)
        place = lax.broadcasted_iota(jnp.int32, (slots, requests), 0)
        expert = (((place >> 3) & 7) * 4 + (place >> 6)).astype(F32)
        member = jnp.zeros((slots, requests), F32)
        weight = jnp.zeros((slots, requests), F32)
        for k in range(top):
            hit = ids[k : k + 1, :] == expert
            member = jnp.where(hit, 1.0, member)
            weight = jnp.where(hit, gates[k : k + 1, :], weight)
        left = lax.broadcasted_iota(jnp.int32, (requests, requests), 0)
        right = lax.broadcasted_iota(jnp.int32, (requests, requests), 1)
        before = jnp.where(left < right, 1.0, 0.0).astype(BF)
        earlier = jnp.dot(member.astype(BF), before, preferred_element_type=F32)
        fits = (member > 0.5) & (earlier == (place & 7).astype(F32))
        mix_ref[...] = jnp.where(fits, weight, 0.0).astype(BF)

    return pl.pallas_call(
        kernel,
        out_shape=(
            jax.ShapeDtypeStruct((requests, half + 128), BF),
            jax.ShapeDtypeStruct((slots, requests), BF),
        ),
        grid_spec=pltpu.PrefetchScalarGridSpec(
            num_scalar_prefetch=1,
            grid=(1,),
            in_specs=[
                pl.BlockSpec((requests, model_width), lambda i, c: (0, 0)),
                pl.BlockSpec((requests, half), lambda i, c: (0, c[0])),
                pl.BlockSpec((1, half), lambda i, c: (0, c[0])),
                pl.BlockSpec((requests, top), lambda i, c: (0, 0)),
                pl.BlockSpec((top, requests), lambda i, c: (0, 0)),
                pl.BlockSpec((top, requests), lambda i, c: (0, 0)),
            ],
            out_specs=(
                pl.BlockSpec((requests, half + 128), lambda i, c: (0, 0)),
                pl.BlockSpec((slots, requests), lambda i, c: (0, 0)),
            ),
        ),
    )(
        core.reshape(1),
        hidden,
        hidden,
        norm_gain.reshape(1, -1),
        routes,
        routes.T,
        gate_weights.T,
    )


def choose_rows(z_index, blocks):
    count = len(blocks)
    half = blocks[0].shape[1] - 128
    rows = 8 * 16
    span = 4 * CAP
    lanes = 8 * span

    def kernel(z_ref, *refs):
        sources, outs = refs[:count], refs[count:]
        z = z_ref[0]
        ids = jnp.concatenate([ref[:, half:] for ref in sources], axis=0).astype(F32)
        lane = lax.broadcasted_iota(jnp.int32, (rows, lanes), 1)
        block = lax.broadcasted_iota(jnp.int32, (rows, lanes), 0) >> 4
        away = sum(jnp.where(block == n, by, 0) for n, by in enumerate(AWAY))
        rank = (lane >> 7) * 4 + ((lane >> 3) & 3)
        expert = (z * 4 + ((lane >> 5) & 3)).astype(F32)
        member = jnp.zeros((rows, lanes), F32)
        for k in range(8):
            member = jnp.where(ids[:, k : k + 1] == expert, 1.0, member)
        left = lax.broadcasted_iota(jnp.int32, (rows, rows), 0)
        right = lax.broadcasted_iota(jnp.int32, (rows, rows), 1)
        lower = jnp.where((right < left) & (right >> 4 == left >> 4), 1.0, 0.0)
        slot = jnp.dot(lower.astype(BF), member.astype(BF), preferred_element_type=F32)
        fits = (member > 0.5) & (slot == (lane & 7).astype(F32))
        fits = fits & (rank == ((z + 8 - away) & 7))
        chosen = jnp.where(fits, 1.0, 0.0).astype(BF)
        for start in range(0, half, 512):
            columns = slice(start, start + 512)
            data = jnp.concatenate([ref[:, columns] for ref in sources], axis=0)
            picked = lax.dot_general(
                chosen, data, (((0,), (0,)), ((), ())), preferred_element_type=F32
            ).astype(BF)
            for n in range(8):
                outs[n // 4][n % 4, :, columns] = picked[n * span : (n + 1) * span]

    shape = jax.ShapeDtypeStruct((4, span, half), BF)
    vmem = pl.BlockSpec(memory_space=pltpu.VMEM)
    return pl.pallas_call(
        kernel,
        out_shape=(shape,) * 2,
        in_specs=[pl.BlockSpec(memory_space=pltpu.SMEM)] + [vmem] * count,
        out_specs=(vmem,) * 2,
    )(z_index.reshape(1), *blocks)


def add_experts(core, hidden, mix, returned):
    requests = hidden.shape[0]
    blocks, slots, width = returned.shape

    def kernel(core_ref, hidden_ref, mix_ref, returned_ref, out_ref):
        del core_ref
        weighted = lax.dot_general(
            mix_ref[...],
            returned_ref[0],
            (((0,), (0,)), ((), ())),
            preferred_element_type=F32,
        )
        out_ref[...] = (hidden_ref[...].astype(F32) + weighted).astype(BF)

    return pl.pallas_call(
        kernel,
        out_shape=jax.ShapeDtypeStruct((requests, blocks * width), BF),
        grid_spec=pltpu.PrefetchScalarGridSpec(
            num_scalar_prefetch=1,
            grid=(blocks,),
            in_specs=[
                pl.BlockSpec((requests, width), lambda i, c: (0, c[0] * blocks + i)),
                pl.BlockSpec((slots, requests), lambda i, c: (0, 0)),
                pl.BlockSpec((1, slots, width), lambda i, c: (i, 0, 0)),
            ],
            out_specs=pl.BlockSpec((requests, width), lambda i, c: (0, i)),
        ),
    )(core.reshape(1), hidden, mix, returned)


def local(
    queries,
    latent_cache,
    cache_lens,
    movers,
    hidden,
    norm_gain,
    routes,
    gate_weights,
    gate_proj,
    up_proj,
    down_proj,
):
    requests, model_width = hidden.shape
    half = model_width // 2
    count = EXPERTS * CAP
    core = lax.axis_index("ep").astype(jnp.int32)
    x_index = lax.axis_index("x").astype(jnp.int32)

    z_index = lax.axis_index("z").astype(jnp.int32)
    packed, mix = pack_rows(core, hidden, norm_gain, routes, gate_weights)
    packed, gate_proj, up_proj, down_proj = lax.optimization_barrier(
        (packed, gate_proj, up_proj, down_proj)
    )
    after, before = shifted(packed, "z", 1), shifted(packed, "z", -1)
    opposite = shifted(packed, "z", 4)
    upward = shifted(jnp.concatenate([packed, after], axis=0), "z", 2)
    downward = shifted(jnp.concatenate([packed, before], axis=0), "z", -2)
    picked = choose_rows(z_index, [packed, after, before, opposite, upward, downward])
    low, high = [
        lax.all_to_all(part, "y", split_axis=0, concat_axis=0, tiled=True).reshape(-1, half)
        for part in picked
    ]

    both = jnp.concatenate([gate_proj[0], up_proj[0]], axis=1)
    far_weights = lax.dynamic_slice_in_dim(both, (1 - core) * half, half, 0)
    near_weights = lax.dynamic_slice_in_dim(both, core * half, half, 0)
    mixed = jnp.concatenate([near_weights, shifted(far_weights, "ep", 1)], axis=1)

    def down_rows(which):
        parts = []
        for by in range(4):
            source = (x_index + by) % 4
            parts.append(
                lax.dynamic_slice_in_dim(down_proj[0], source * 256 + which * 128, 128, 0)
            )
        return jnp.concatenate(parts, axis=0)

    near_down, far_down = down_rows(core), down_rows(1 - core)
    low, high, mixed, near_down, far_down, queries, latent_cache, movers = (
        lax.optimization_barrier(
            (low, high, mixed, near_down, far_down, queries, latent_cache, movers)
        )
    )

    ahead_low, behind_low = shifted(low, "x", 1), shifted(low, "x", -1)
    ahead_high, behind_high = shifted(high, "x", 1), shifted(high, "x", -1)
    across_low, across_high = shifted(ahead_low, "x", 1), shifted(behind_high, "x", -1)

    attention = attend(queries, latent_cache, cache_lens, core)
    listed = movers[0]
    slot_ids = jnp.arange(requests, dtype=jnp.int32)
    flagged = jnp.any(slot_ids[:, None] == listed[None, :], axis=1)
    nothing = jnp.zeros((), BF)
    picks = (listed[:, None] == slot_ids[None, :]).astype(BF)
    moved = jnp.einsum("mr,rhd->mhd", picks, attention, preferred_element_type=F32).astype(BF)
    arrived_contexts = shifted(moved, "z", 4)
    served = jnp.concatenate(
        [jnp.where(flagged[:, None, None], nothing, attention), arrived_contexts], axis=0
    )

    def products(blocks):
        return [jnp.dot(b, mixed, preferred_element_type=F32) for b in blocks]

    def activate(totals):
        total = jnp.concatenate(totals, axis=0)
        value = total[:, :256] + shifted(total[:, 256:], "ep", 1)
        activated = (jax.nn.silu(value[:, :128]) * value[:, 128:]).astype(BF)
        activated = jnp.swapaxes(activated.reshape(-1, 2, 4, 4 * CAP, 128), 1, 2)
        return activated.reshape(-1, count, 128)

    own = activate(products([low, high]))
    ahead_low, ahead_high, behind_low, behind_high, own, served = lax.optimization_barrier(
        (ahead_low, ahead_high, behind_low, behind_high, own, served)
    )
    after_x = products([behind_low, behind_high])
    before_x = products([ahead_low, ahead_high])
    across_low, across_high, after_x, before_x = lax.optimization_barrier(
        (across_low, across_high, after_x, before_x)
    )
    others = activate(after_x + products([across_low, across_high]) + before_x)
    acts = jnp.concatenate([own, others], axis=0)
    held = [acts] + [shifted(acts, "x", -by) for by in (1, 2, 3)]
    stripes = [jnp.concatenate([held[s][(r - s) % 4] for s in range(4)], axis=1) for r in range(4)]
    twice = jnp.concatenate(stripes + stripes[:3], axis=0)
    joined = lax.dynamic_slice_in_dim(twice, (4 - x_index) % 4 * count, 4 * count, 0)
    expert_out = (
        jnp.dot(joined, near_down, preferred_element_type=F32)
        + jnp.dot(shifted(joined, "ep", 1), far_down, preferred_element_type=F32)
    ).astype(BF)
    returned = lax.all_to_all(
        expert_out.reshape(4 * EXPERTS, CAP, -1),
        ("x", "y", "z"),
        split_axis=0,
        concat_axis=0,
        tiled=True,
    )
    expert_mix = add_experts(core, hidden, mix, returned.reshape(4, count, -1))
    return served, expert_mix


def solution(mesh):
    grid = Mesh(mesh.devices.reshape(8, 4, 4, 2), ("z", "y", "x", "ep"))
    dp = ("z", "y", "x")
    placed = (
        P(dp, None, None),
        P(dp, "ep", None),
        P(dp),
        P(dp, None),
        P(dp, None),
        P(),
        P(dp, None),
        P(dp, None),
        P(dp, None, "ep"),
        P(dp, None, "ep"),
        P(dp, None, "ep"),
    )
    return jax.shard_map(
        local,
        mesh=grid,
        in_specs=placed,
        out_specs=(P(dp, "ep", None), P(dp, "ep")),
        check_vma=False,
    )
```

time: 237 us -> 252 us (1.063)
  starting transfers between devices: 31.3 us -> 41.5 us
  local copies, waits for them, and re-layouts: 19.2 us -> 9.17 us
  other arithmetic: 6.92 us -> 13.5 us
  Pallas kernels: 3.15 us -> 9.19 us
  matrix products: 21.7 us -> 15.7 us
  waiting for transfers between devices: 96.3 us -> 102 us
  blocking collectives: 56.1 us -> 59.2 us
    ppermute x21, waiting for transfers between devices: 52.3 us -> 88.2 us  [shifted(): lax.ppermute(x, axis, [(i, (i + by) % devices) for i in range(devices)])]
    all_to_all x1 -> x2, waiting for transfers between devices: 44 us -> 13.6 us  [local(): lax.all_to_all(part, 'y', split_axis=0, concat_axis=0, tiled=True)]
    ppermute x21, starting transfers between devices: 20 us -> 32.8 us  [shifted(): lax.ppermute(x, axis, [(i, (i + by) % devices) for i in range(devices)])]
    concatenate x1 -> x5, other arithmetic: 0.04 us -> 7.37 us  [the longest x1 3.54 us: local(): jnp.concatenate([near_weights, shifted(far_weights, 'ep', 1)], axis=1)]
    pallas_call x1 -> x3, Pallas kernels: 3.15 us -> 9.19 us  [the longest x1 3.74 us: add_experts(): pl.pallas_call(kernel, out_shape=jax.ShapeDtypeStruct((requests, blocks *...]
    slice x2 -> x1, local copies, waits for them, and re-layouts: 4.44 us -> 0.01 us  [local(): held[s][(r - s) % 4]]
    dot_general x5 -> x8, matrix products: 13.3 us -> 9.77 us  [products(): return [jnp.dot(b, mixed, preferred_element_type=F32) for b in blocks]]
    all_to_all x1, blocking collectives: 56.1 us -> 59.2 us  [local(): lax.all_to_all(expert_out.reshape(4 * EXPERTS, CAP, -1), ('x', 'y', 'z'),...]
  transfers between devices with their start and end apart: 22 -> 23, of which waited for: 12 -> 15; matrix products, arithmetic and copies ran while one was open for 10% -> 11% of each run, Pallas kernels for 0% -> 1%
where the time goes in v1:
time: 252 us; the launch traced here: 251 us
  waiting for transfers between devices  102 us (40%)
  blocking collectives  59.2 us (23%)
  starting transfers between devices  41.5 us (16%)
  matrix products  15.7 us (6%)
  other arithmetic  13.5 us (5%)
  Pallas kernels  9.19 us (4%)
  local copies, waits for them, and re-layouts  9.17 us (4%)
    ppermute x21, waiting for transfers between devices, shifted(): lax.ppermute(x, axis, [(i, (i + by) % devices) for i in range(devices)])  88.2 us
    all_to_all x1, blocking collectives, local(): lax.all_to_all(expert_out.reshape(4 * EXPERTS, CAP, -1), ('x', 'y', 'z'),...  59.2 us
    ppermute x21, starting transfers between devices, shifted(): lax.ppermute(x, axis, [(i, (i + by) % devices) for i in range(devices)])  32.8 us
    all_to_all x2, waiting for transfers between devices, local(): lax.all_to_all(part, 'y', split_axis=0, concat_axis=0, tiled=True)  13.6 us
    dot_general x8, matrix products, products(): return [jnp.dot(b, mixed, preferred_element_type=F32) for b in blocks]  9.77 us
    all_to_all x2, starting transfers between devices, local(): lax.all_to_all(part, 'y', split_axis=0, concat_axis=0, tiled=True)  8.67 us
  transfers between devices with their start and end apart: 23, of which 15 were waited for; matrix products, arithmetic and copies ran while one was open for 11% of the time, Pallas kernels for 1%

profile of v1, /device:TPU:32, one launch (start us, length us, event | category | flops | bytes accessed | tf_op | source)
XLA Modules:
  0.0 251.0 jit_solution(5509266726995351649)
XLA Ops:
  2.1 2.0 shard_map.122
  4.1 3.7 %fusion.4 = (bf16[3584,256]{1,0:T(8,128)(2,1)S(1)}, bf16[3584,256]{1,0:T(8,128)(2,1)}) fusion(s32[]{:T(128)S(6)} %select_n.85, bf16[7168,128]{1,0:T(8,128)(2,1)} %bitcast.111, bf16[7168,128]{1,0:T(8,128)(2,1)} %bitcast.112, s32[]{:T(128)S(6)} %select_n.86), kind=kLoop, calls=%fused_computation.10 | loop fusion | flops 7340032 | bytes 7340040 | tf_op jit(solution)/shard_map/concatenate | solution.py:231
  7.8 1.9 collective-permute-start
  9.8 3.7 %collective-permute-done.refs_1_ = bf16[16,3712]{1,0:T(8,128)(2,1)S(1)} collective-permute-done((bf16[16,3712]{1,0:T(8,128)(2,1)S(1)}, bf16[16,3712]{1,0:T(8,128)(2,1)S(1)}, u32[]{:S(2)}, u32[]{:S(2)}) %collective-permute-start) | collective-permute-done | bytes 118816 | tf_op jit(solution)/shard_map/ppermute | solution.py:19
  16.1 5.5 %collective-permute-start.3 = (bf16[32,3712]{1,0:T(8,128)(2,1)}, bf16[32,3712]{1,0:T(8,128)(2,1)}, u32[]{:S(2)}, u32[]{:S(2)}) collective-permute-start(bf16[32,3712]{1,0:T(8,128)(2,1)} %get-tuple-element.91), channel_id=1, source_target_pairs={{0,64},{32,96},{64,128},{96,160},{128,192},{160,224},{192,0},{224,... | collective-permute-start | bytes 712712 | tf_op jit(solution)/shard_map/ppermute | solution.py:19
  21.6 3.8 %collective-permute-start.2 = (bf16[16,3712]{1,0:T(8,128)(2,1)S(1)}, bf16[16,3712]{1,0:T(8,128)(2,1)}, u32[]{:S(2)}, u32[]{:S(2)}) collective-permute-start(bf16[16,3712]{1,0:T(8,128)(2,1)S(1)} %copy-done.6), channel_id=1, source_target_pairs={{0,128},{32,160},{64,192},{96,224},{128,0},{160,32},{192,64},{224,... | collective-permute-start | bytes 356360 | tf_op jit(solution)/shard_map/ppermute | solution.py:19
  25.4 14.7 %collective-permute-done.2.refs_3_ = bf16[16,3712]{1,0:T(8,128)(2,1)} collective-permute-done((bf16[16,3712]{1,0:T(8,128)(2,1)S(1)}, bf16[16,3712]{1,0:T(8,128)(2,1)}, u32[]{:S(2)}, u32[]{:S(2)}) %collective-permute-start.2) | collective-permute-done | bytes 118816 | tf_op jit(solution)/shard_map/ppermute | solution.py:19
  40.2 3.5 %shard_map.123 = (bf16[4,32,3584]{2,1,0:T(8,128)(2,1)}, bf16[4,32,3584]{2,1,0:T(8,128)(2,1)}) custom-call(s32[1]{0:T(128)} %bitcast.z_ref, bf16[16,3712]{1,0:T(8,128)(2,1)} %get-tuple-element.31.refs_0_, bf16[16,3712]{1,0:T(8,128)(2,1)} %copy-done.7, bf16[16,3712]{1,0:T(8,128)(2,1)} %copy-done.8, bf16[16,3712]{1,0:T(8,128)(2,1)} %collective-permute-done.2.refs_3_, ...), custom_call_target="tpu_custom_call" | custom-call | tf_op jit(solution)/shard_map/pallas_call | solution.py:159
  43.7 4.5 %all-to-all-start = ((bf16[4,32,3584]{2,1,0:T(8,128)(2,1)}), bf16[4,32,3584]{2,1,0:T(8,128)(2,1)}, u32[]{:S(2)}, u32[]{:S(2)}) async-start(bf16[4,32,3584]{2,1,0:T(8,128)(2,1)} %get-tuple-element.32), calls=%async_computation | async-start | bytes 1835008 | tf_op jit(solution)/shard_map/all_to_all | solution.py:227
  48.1 2.7 %dynamic-slice_bitcast_fusion.3 = (bf16[128,896]{1,0:T(8,128)(2,1)S(1)}, bf16[128,896]{1,0:T(8,128)(2,1)}, bf16[128,896]{1,0:T(8,128)(2,1)}, bf16[128,896]{1,0:T...) fusion(bf16[1,1024,896]{2,1,0:T(8,128)(2,1)} %param.21, ...), kind=kLoop, calls=%fused_computation.48 | loop fusion | bytes 3670048 | tf_op jit(solution)/shard_map/dynamic_slice | solution.py:241
  51.0 9.2 %all-to-all-done = bf16[4,32,3584]{2,1,0:T(8,128)(2,1)} async-done(((bf16[4,32,3584]{2,1,0:T(8,128)(2,1)}), bf16[4,32,3584]{2,1,0:T(8,128)(2,1)}, u32[]{:S(2)}, u32[]{:S(2)}) %all-to-all-start) | async-done | bytes 917536 | tf_op jit(solution)/shard_map/all_to_all | solution.py:227
  60.2 4.2 %all-to-all-start.1 = ((bf16[4,32,3584]{2,1,0:T(8,128)(2,1)}), bf16[4,32,3584]{2,1,0:T(8,128)(2,1)}, u32[]{:S(2)}, u32[]{:S(2)}) async-start(bf16[4,32,3584]{2,1,0:T(8,128)(2,1)} %get-tuple-element.33), calls=%async_computation.1 | async-start | bytes 1835008 | tf_op jit(solution)/shard_map/all_to_all | solution.py:227
  64.4 3.0 %pad_maximum_fusion.1 = (bf16[512,896]{1,0:T(8,128)(2,1)}, bf16[512,896]{1,0:T(8,128)(2,1)}) fusion(bf16[128,896]{1,0:T(8,128)(2,1)} %get-tuple-element.69, bf16[128,896]{1,0:T(8,128)(2,1)} %get-tuple-element.70, bf16[128,896]{1,0:T(8,128)(2,1)} %get-tuple-element.71, bf16[128,896]{1,0:T(8,128)(2,1)} %get-tuple-element.72, ...), kind=kLoop, calls=%fused_computation.17 | loop fusion | flops 7340032 | bytes 3670016 | tf_op jit(solution)/shard_map/concatenate | solution.py:243
  67.4 3.5 %pad_maximum_fusion = bf16[3584,512]{1,0:T(8,128)(2,1)} fusion(bf16[3584,256]{1,0:T(8,128)(2,1)} %collective-permute-done.5, bf16[3584,256]{1,0:T(8,128)(2,1)S(1)} %get-tuple-element.63), kind=kLoop, calls=%fused_computation.4 | loop fusion | flops 7340032 | bytes 7340032 | tf_op jit(solution)/shard_map/concatenate | solution.py:234
  70.9 4.3 %all-to-all-done.1 = bf16[4,32,3584]{2,1,0:T(8,128)(2,1)} async-done(((bf16[4,32,3584]{2,1,0:T(8,128)(2,1)}), bf16[4,32,3584]{2,1,0:T(8,128)(2,1)}, u32[]{:S(2)}, u32[]{:S(2)}) %all-to-all-start.1) | async-done | bytes 917536 | tf_op jit(solution)/shard_map/all_to_all | solution.py:227
  76.7 2.9 %fusion.37 = f32[128,512]{1,0:T(8,128)S(1)} fusion(bf16[128,3584]{1,0:T(8,128)(2,1)} %bitcast.5, bf16[3584,512]{1,0:T(8,128)(2,1)} %pad_maximum_fusion), kind=kOutput, calls=%fused_computation.100 | convolution fusion | flops 469762048 | bytes 4849664 | tf_op jit(solution)/shard_map/dot_general | solution.py:269
  83.1 4.3 %copy.25 = bf16[16,128,576]{2,1,0:T(8,128)(2,1)} copy(bf16[16,128,576]{1,2,0:T(8,128)(2,1)} %param.12) | data formatting | bytes 4718592 | tf_op jit(solution)/shard_map/optimization_barrier | solution.py:247
  87.4 2.5 fusion.36
  96.6 6.7 %collective-permute-start.13 = (bf16[4,32,512]{2,1,0:T(8,128)(2,1)S(1)}, bf16[4,32,512]{2,1,0:T(8,128)(2,1)S(1)}, u32[]{:S(2)}, u32[]{:S(2)}) collective-permute-start(bf16[4,32,512]{2,1,0:T(8,128)(2,1)S(1)} %copy.33), channel_id=1, source_target_pairs={{0,128},{32,160},{64,192},{96,224},{128,0},{160,32},{192,64},{224,... | collective-permute-start | bytes 393224 | tf_op jit(solution)/shard_map/ppermute | solution.py:19
  103.4 3.2 %collective-permute-done.13 = bf16[4,32,512]{2,1,0:T(8,128)(2,1)S(1)} collective-permute-done((bf16[4,32,512]{2,1,0:T(8,128)(2,1)S(1)}, bf16[4,32,512]{2,1,0:T(8,128)(2,1)S(1)}, u32[]{:S(2)}, u32[]{:S(2)}) %collective-permute-start.13) | collective-permute-done | bytes 131104 | tf_op jit(solution)/shard_map/ppermute | solution.py:19
  107.5 6.6 %collective-permute-done.7 = bf16[128,3584]{1,0:T(8,128)(2,1)} collective-permute-done((bf16[128,3584]{1,0:T(8,128)(2,1)}, bf16[128,3584]{1,0:T(8,128)(2,1)}, u32[]{:S(2)}, u32[]{:S(2)}) %collective-permute-start.7) | collective-permute-done | bytes 917536 | tf_op jit(solution)/shard_map/ppermute | solution.py:19
  114.1 2.4 collective-permute-done.8
  116.5 18.9 %collective-permute-done.9 = bf16[128,3584]{1,0:T(8,128)(2,1)S(1)} collective-permute-done((bf16[128,3584]{1,0:T(8,128)(2,1)}, bf16[128,3584]{1,0:T(8,128)(2,1)S(1)}, u32[]{:S(2)}, u32[]{:S(2)}) %collective-permute-start.9) | collective-permute-done | bytes 917536 | tf_op jit(solution)/shard_map/ppermute | solution.py:19
  138.4 2.0 collective-permute-start.15
  142.4 17.6 %collective-permute-done.14 = bf16[128,3584]{1,0:T(8,128)(2,1)S(1)} collective-permute-done((bf16[128,3584]{1,0:T(8,128)(2,1)S(1)}, bf16[128,3584]{1,0:T(8,128)(2,1)S(1)}, u32[]{:S(2)}, u32[]{:S(2)}) %collective-permute-start.14) | collective-permute-done | bytes 917536 | tf_op jit(solution)/shard_map/ppermute | solution.py:19
  161.6 2.3 collective-permute-done.16
  164.2 3.1 %collective-permute-start.17 = (bf16[4,256,128]{2,1,0:T(8,128)(2,1)S(1)}, bf16[4,256,128]{2,1,0:T(8,128)(2,1)S(1)}, u32[]{:S(2)}, u32[]{:S(2)}) collective-permute-start(bf16[4,256,128]{2,1,0:T(8,128)(2,1)S(1)} %pad_maximum_fusion.7), channel_id=1, source_target_pairs={{0,6},{2,0},{4,2},{6,4},{1,7},{3,1},{5,3},{7,5},{8,14},{10,8},{12,... | collective-permute-start | bytes 786440 | tf_op jit(solution)/shard_map/ppermute | solution.py:19
  168.6 10.2 %collective-permute-done.17 = bf16[4,256,128]{2,1,0:T(8,128)(2,1)S(1)} collective-permute-done((bf16[4,256,128]{2,1,0:T(8,128)(2,1)S(1)}, bf16[4,256,128]{2,1,0:T(8,128)(2,1)S(1)}, u32[]{:S(2)}, u32[]{:S(2)}) %collective-permute-start.17) | collective-permute-done | bytes 262176 | tf_op jit(solution)/shard_map/ppermute | solution.py:19
  178.8 3.4 %collective-permute-done.19 = bf16[4,256,128]{2,1,0:T(8,128)(2,1)S(1)} collective-permute-done((bf16[4,256,128]{2,1,0:T(8,128)(2,1)S(1)}, bf16[4,256,128]{2,1,0:T(8,128)(2,1)S(1)}, u32[]{:S(2)}, u32[]{:S(2)}) %collective-permute-start.19) | collective-permute-done | bytes 262176 | tf_op jit(solution)/shard_map/ppermute | solution.py:19
  182.9 2.6 %collective-permute-done.20 = bf16[1024,512]{1,0:T(8,128)(2,1)S(1)} collective-permute-done((bf16[1024,512]{1,0:T(8,128)(2,1)S(1)}, bf16[1024,512]{1,0:T(8,128)(2,1)S(1)}, u32[]{:S(2)}, u32[]{:S(2)}) %collective-permute-start.20) | collective-permute-done | bytes 1048608 | tf_op jit(solution)/shard_map/ppermute | solution.py:19
  188.1 59.2 %all_to_all.15 = bf16[128,8,896]{2,1,0:T(8,128)(2,1)} all-to-all(bf16[128,8,896]{2,1,0:T(8,128)(2,1)S(1)} %fusion.2), channel_id=1, replica_groups=mesh['z'=8,'y'=4,'x'=4,'ep'=2] {'x','y','z'}, dimensions={0} | all-to-all | bytes 3670016 | tf_op jit(solution)/shard_map/all_to_all | solution.py:297
  247.3 3.7 %shard_map.124 = bf16[16,3584]{1,0:T(8,128)(2,1)} custom-call(s32[1]{0:T(128)} %bitcast.1.core_ref, bf16[16,7168]{1,0:T(8,128)(2,1)} %hidden_ref.1, bf16[256,16]{1,0:T(8,128)(2,1)} %get-tuple-element.44.mix_ref, bf16[4,256,896]{2,1,0:T(8,128)(2,1)} %bitcast.110), custom_call_target="tpu_custom_call" | custom-call | tf_op jit(solution)/shard_map/pallas_call | solution.py:181
  (97 shorter events, 27.9 us)
Async XLA Ops:
  0.6 86.8 %copy-start = (bf16[16,64,576]{2,1,0:T(8,128)(2,1)S(1)}, bf16[16,64,576]{2,1,0:T(8,128)(2,1)}, u32[]{:S(2)}) copy-start(bf16[16,64,576]{2,1,0:T(8,128)(2,1)} %param.11) | copy-start | bytes 3538948
  4.1 3.7 %copy-start.6 = (bf16[16,3712]{1,0:T(8,128)(2,1)S(1)}, bf16[16,3712]{1,0:T(8,128)(2,1)}, u32[]{:S(2)}) copy-start(bf16[16,3712]{1,0:T(8,128)(2,1)} %get-tuple-element.31.refs_0_) | copy-start | bytes 356356
  7.8 59.6 %collective-permute-start.5 = (bf16[3584,256]{1,0:T(8,128)(2,1)}, bf16[3584,256]{1,0:T(8,128)(2,1)}, u32[]{:S(2)}, u32[]{:S(2)}) collective-permute-start(bf16[3584,256]{1,0:T(8,128)(2,1)} %get-tuple-element.64), channel_id=1, source_target_pairs={{0,1},{1,0},{2,3},{3,2},{4,5},{5,4},{6,7},{7,6},{8,9},{9,8},{10,11... | collective-permute-start | bytes 5505032 | tf_op jit(solution)/shard_map/ppermute | solution.py:19
  7.8 5.7 %collective-permute-start = (bf16[16,3712]{1,0:T(8,128)(2,1)S(1)}, bf16[16,3712]{1,0:T(8,128)(2,1)S(1)}, u32[]{:S(2)}, u32[]{:S(2)}) collective-permute-start(bf16[16,3712]{1,0:T(8,128)(2,1)S(1)} %copy-done.6), channel_id=1, source_target_pairs={{0,32},{32,64},{64,96},{96,128},{128,160},{160,192},{192,224},{224... | collective-permute-start | bytes 356360 | tf_op jit(solution)/shard_map/ppermute | solution.py:19
  9.7 5.5 %collective-permute-start.1 = (bf16[16,3712]{1,0:T(8,128)(2,1)S(1)}, bf16[16,3712]{1,0:T(8,128)(2,1)S(1)}, u32[]{:S(2)}, u32[]{:S(2)}) collective-permute-start(bf16[16,3712]{1,0:T(8,128)(2,1)S(1)} %copy-done.6), channel_id=1, source_target_pairs={{0,224},{32,0},{64,32},{96,64},{128,96},{160,128},{192,160},{224,1... | collective-permute-start | bytes 356360 | tf_op jit(solution)/shard_map/ppermute | solution.py:19
  13.5 26.6 %copy-start.7 = (bf16[16,3712]{1,0:T(8,128)(2,1)}, bf16[16,3712]{1,0:T(8,128)(2,1)S(1)}, u32[]{:S(2)}) copy-start(bf16[16,3712]{1,0:T(8,128)(2,1)S(1)} %collective-permute-done.refs_1_) | copy-start | bytes 356356
  15.2 24.9 %copy-start.8 = (bf16[16,3712]{1,0:T(8,128)(2,1)}, bf16[16,3712]{1,0:T(8,128)(2,1)S(1)}, u32[]{:S(2)}) copy-start(bf16[16,3712]{1,0:T(8,128)(2,1)S(1)} %collective-permute-done.1.refs_2_) | copy-start | bytes 356356
  16.1 24.1 %collective-permute-start.3 = (bf16[32,3712]{1,0:T(8,128)(2,1)}, bf16[32,3712]{1,0:T(8,128)(2,1)}, u32[]{:S(2)}, u32[]{:S(2)}) collective-permute-start(bf16[32,3712]{1,0:T(8,128)(2,1)} %get-tuple-element.91), channel_id=1, source_target_pairs={{0,64},{32,96},{64,128},{96,160},{128,192},{160,224},{192,0},{224,... | collective-permute-start | bytes 712712 | tf_op jit(solution)/shard_map/ppermute | solution.py:19
  21.6 18.6 %collective-permute-start.4 = (bf16[32,3712]{1,0:T(8,128)(2,1)}, bf16[32,3712]{1,0:T(8,128)(2,1)}, u32[]{:S(2)}, u32[]{:S(2)}) collective-permute-start(bf16[32,3712]{1,0:T(8,128)(2,1)} %get-tuple-element.90), channel_id=1, source_target_pairs={{0,192},{32,224},{64,0},{96,32},{128,64},{160,96},{192,128},{224,1... | collective-permute-start | bytes 712712 | tf_op jit(solution)/shard_map/ppermute | solution.py:19
  21.6 18.6 %collective-permute-start.2 = (bf16[16,3712]{1,0:T(8,128)(2,1)S(1)}, bf16[16,3712]{1,0:T(8,128)(2,1)}, u32[]{:S(2)}, u32[]{:S(2)}) collective-permute-start(bf16[16,3712]{1,0:T(8,128)(2,1)S(1)} %copy-done.6), channel_id=1, source_target_pairs={{0,128},{32,160},{64,192},{96,224},{128,0},{160,32},{192,64},{224,... | collective-permute-start | bytes 356360 | tf_op jit(solution)/shard_map/ppermute | solution.py:19
  43.7 16.5 %all-to-all-start = ((bf16[4,32,3584]{2,1,0:T(8,128)(2,1)}), bf16[4,32,3584]{2,1,0:T(8,128)(2,1)}, u32[]{:S(2)}, u32[]{:S(2)}) async-start(bf16[4,32,3584]{2,1,0:T(8,128)(2,1)} %get-tuple-element.32), calls=%async_computation | async-start | bytes 1835008 | tf_op jit(solution)/shard_map/all_to_all | solution.py:227
  60.2 15.0 %all-to-all-start.1 = ((bf16[4,32,3584]{2,1,0:T(8,128)(2,1)}), bf16[4,32,3584]{2,1,0:T(8,128)(2,1)}, u32[]{:S(2)}, u32[]{:S(2)}) async-start(bf16[4,32,3584]{2,1,0:T(8,128)(2,1)} %get-tuple-element.33), calls=%async_computation.1 | async-start | bytes 1835008 | tf_op jit(solution)/shard_map/all_to_all | solution.py:227
  75.2 4.5 %copy-start.1 = (bf16[3584,512]{1,0:T(8,128)(2,1)S(1)}, bf16[3584,512]{1,0:T(8,128)(2,1)}, u32[]{:S(2)}) copy-start(bf16[3584,512]{1,0:T(8,128)(2,1)} %pad_maximum_fusion) | copy-start | bytes 11010052
  75.2 32.3 %collective-permute-start.6 = (bf16[128,3584]{1,0:T(8,128)(2,1)}, bf16[128,3584]{1,0:T(8,128)(2,1)S(1)}, u32[]{:S(2)}, u32[]{:S(2)}) collective-permute-start(bf16[128,3584]{1,0:T(8,128)(2,1)} %bitcast.5), channel_id=1, source_target_pairs={{0,2},{2,4},{4,6},{6,0},{1,3},{3,5},{5,7},{7,1},{8,10},{10,12},{12... | collective-permute-start | bytes 2752520 | tf_op jit(solution)/shard_map/ppermute | solution.py:19
  81.5 32.6 %collective-permute-start.7 = (bf16[128,3584]{1,0:T(8,128)(2,1)}, bf16[128,3584]{1,0:T(8,128)(2,1)}, u32[]{:S(2)}, u32[]{:S(2)}) collective-permute-start(bf16[128,3584]{1,0:T(8,128)(2,1)} %bitcast.6), channel_id=1, source_target_pairs={{0,2},{2,4},{4,6},{6,0},{1,3},{3,5},{5,7},{7,1},{8,10},{10,12},{12... | collective-permute-start | bytes 2752520 | tf_op jit(solution)/shard_map/ppermute | solution.py:19
  87.4 2.9 %copy-start.3 = (bf16[16,128,576]{2,1,0:T(8,128)(2,1)S(1)}, bf16[16,128,576]{2,1,0:T(8,128)(2,1)}, u32[]{:S(2)}) copy-start(bf16[16,128,576]{2,1,0:T(8,128)(2,1)} %copy.25) | copy-start | bytes 7077892
  91.0 4.7 %collective-permute-start.12 = (bf16[16,32,512]{2,1,0:T(8,128)(2,1)S(1)}, bf16[16,32,512]{2,1,0:T(8,128)(2,1)S(1)}, u32[]{:S(2)}, u32[]{:S(2)}) collective-permute-start(bf16[16,32,512]{2,1,0:T(8,128)(2,1)S(1)} %dynamic-slice_convert_fusion), channel_id=1, source_target_pairs={{0,1},{1,0},{2,3},{3,2},{4,5},{5,4},{6,7},{7,6},{8,9},{9,8},{10,11... | collective-permute-start | bytes 1572872 | tf_op jit(solution)/shard_map/ppermute | solution.py:19
  91.2 1.8 collective-permute-start.11
  91.9 2.9 %collective-permute-start.10 = (f32[256,256]{1,0:T(8,128)S(1)}, f32[256,256]{1,0:T(8,128)S(1)}, u32[]{:S(2)}, u32[]{:S(2)}) collective-permute-start(f32[256,256]{1,0:T(8,128)S(1)} %pad_maximum_fusion.6), channel_id=1, source_target_pairs={{0,1},{1,0},{2,3},{3,2},{4,5},{5,4},{6,7},{7,6},{8,9},{9,8},{10,11... | collective-permute-start | bytes 786440 | tf_op jit(solution)/shard_map/ppermute | solution.py:19
  93.0 23.4 %collective-permute-start.8 = (bf16[128,3584]{1,0:T(8,128)(2,1)}, bf16[128,3584]{1,0:T(8,128)(2,1)S(1)}, u32[]{:S(2)}, u32[]{:S(2)}) collective-permute-start(bf16[128,3584]{1,0:T(8,128)(2,1)} %bitcast.5), channel_id=1, source_target_pairs={{0,6},{2,0},{4,2},{6,4},{1,7},{3,1},{5,3},{7,5},{8,14},{10,8},{12,... | collective-permute-start | bytes 2752520 | tf_op jit(solution)/shard_map/ppermute | solution.py:19
  94.9 40.4 %collective-permute-start.9 = (bf16[128,3584]{1,0:T(8,128)(2,1)}, bf16[128,3584]{1,0:T(8,128)(2,1)S(1)}, u32[]{:S(2)}, u32[]{:S(2)}) collective-permute-start(bf16[128,3584]{1,0:T(8,128)(2,1)} %bitcast.6), channel_id=1, source_target_pairs={{0,6},{2,0},{4,2},{6,4},{1,7},{3,1},{5,3},{7,5},{8,14},{10,8},{12,... | collective-permute-start | bytes 2752520 | tf_op jit(solution)/shard_map/ppermute | solution.py:19
  95.8 39.5 %copy-start.2 = (bf16[3584,512]{1,0:T(8,128)(2,1)S(1)}, bf16[3584,512]{1,0:T(8,128)(2,1)}, u32[]{:S(2)}) copy-start(bf16[3584,512]{1,0:T(8,128)(2,1)} %pad_maximum_fusion) | copy-start | bytes 11010052
  96.6 10.0 %collective-permute-start.13 = (bf16[4,32,512]{2,1,0:T(8,128)(2,1)S(1)}, bf16[4,32,512]{2,1,0:T(8,128)(2,1)S(1)}, u32[]{:S(2)}, u32[]{:S(2)}) collective-permute-start(bf16[4,32,512]{2,1,0:T(8,128)(2,1)S(1)} %copy.33), channel_id=1, source_target_pairs={{0,128},{32,160},{64,192},{96,224},{128,0},{160,32},{192,64},{224,... | collective-permute-start | bytes 393224 | tf_op jit(solution)/shard_map/ppermute | solution.py:19
  137.1 22.9 %collective-permute-start.14 = (bf16[128,3584]{1,0:T(8,128)(2,1)S(1)}, bf16[128,3584]{1,0:T(8,128)(2,1)S(1)}, u32[]{:S(2)}, u32[]{:S(2)}) collective-permute-start(bf16[128,3584]{1,0:T(8,128)(2,1)S(1)} %collective-permute-done.6), channel_id=1, source_target_pairs={{0,2},{2,4},{4,6},{6,0},{1,3},{3,5},{5,7},{7,1},{8,10},{10,12},{12... | collective-permute-start | bytes 2752520 | tf_op jit(solution)/shard_map/ppermute | solution.py:19
  138.4 21.6 %collective-permute-start.15 = (bf16[128,3584]{1,0:T(8,128)(2,1)S(1)}, bf16[128,3584]{1,0:T(8,128)(2,1)S(1)}, u32[]{:S(2)}, u32[]{:S(2)}) collective-permute-start(bf16[128,3584]{1,0:T(8,128)(2,1)S(1)} %collective-permute-done.9), channel_id=1, source_target_pairs={{0,6},{2,0},{4,2},{6,4},{1,7},{3,1},{5,3},{7,5},{8,14},{10,8},{12,... | collective-permute-start | bytes 2752520 | tf_op jit(solution)/shard_map/ppermute | solution.py:19
  161.5 2.4 collective-permute-start.16
  164.2 14.6 %collective-permute-start.17 = (bf16[4,256,128]{2,1,0:T(8,128)(2,1)S(1)}, bf16[4,256,128]{2,1,0:T(8,128)(2,1)S(1)}, u32[]{:S(2)}, u32[]{:S(2)}) collective-permute-start(bf16[4,256,128]{2,1,0:T(8,128)(2,1)S(1)} %pad_maximum_fusion.7), channel_id=1, source_target_pairs={{0,6},{2,0},{4,2},{6,4},{1,7},{3,1},{5,3},{7,5},{8,14},{10,8},{12,... | collective-permute-start | bytes 786440 | tf_op jit(solution)/shard_map/ppermute | solution.py:19
  167.3 11.5 %collective-permute-start.18 = (bf16[4,256,128]{2,1,0:T(8,128)(2,1)S(1)}, bf16[4,256,128]{2,1,0:T(8,128)(2,1)S(1)}, u32[]{:S(2)}, u32[]{:S(2)}) collective-permute-start(bf16[4,256,128]{2,1,0:T(8,128)(2,1)S(1)} %pad_maximum_fusion.7), channel_id=1, source_target_pairs={{0,4},{2,6},{4,0},{6,2},{1,5},{3,7},{5,1},{7,3},{8,12},{10,14},{12... | collective-permute-start | bytes 786440 | tf_op jit(solution)/shard_map/ppermute | solution.py:19
  167.4 14.7 %collective-permute-start.19 = (bf16[4,256,128]{2,1,0:T(8,128)(2,1)S(1)}, bf16[4,256,128]{2,1,0:T(8,128)(2,1)S(1)}, u32[]{:S(2)}, u32[]{:S(2)}) collective-permute-start(bf16[4,256,128]{2,1,0:T(8,128)(2,1)S(1)} %pad_maximum_fusion.7), channel_id=1, source_target_pairs={{0,2},{2,4},{4,6},{6,0},{1,3},{3,5},{5,7},{7,1},{8,10},{10,12},{12... | collective-permute-start | bytes 786440 | tf_op jit(solution)/shard_map/ppermute | solution.py:19
  182.4 3.2 %copy-start.5 = (bf16[512,896]{1,0:T(8,128)(2,1)S(1)}, bf16[512,896]{1,0:T(8,128)(2,1)}, u32[]{:S(2)}) copy-start(bf16[512,896]{1,0:T(8,128)(2,1)} %get-tuple-element.57) | copy-start | bytes 2752516
  182.6 4.2 %copy-start.4 = (bf16[512,896]{1,0:T(8,128)(2,1)S(1)}, bf16[512,896]{1,0:T(8,128)(2,1)}, u32[]{:S(2)}) copy-start(bf16[512,896]{1,0:T(8,128)(2,1)} %get-tuple-element.56) | copy-start | bytes 2752516
  182.6 3.0 %collective-permute-start.20 = (bf16[1024,512]{1,0:T(8,128)(2,1)S(1)}, bf16[1024,512]{1,0:T(8,128)(2,1)S(1)}, u32[]{:S(2)}, u32[]{:S(2)}) collective-permute-start(bf16[1024,512]{1,0:T(8,128)(2,1)S(1)} %constant_dynamic-slice_fusion), channel_id=1, source_target_pairs={{0,1},{1,0},{2,3},{3,2},{4,5},{5,4},{6,7},{7,6},{8,9},{9,8},{10,11... | collective-permute-start | bytes 3145736 | tf_op jit(solution)/shard_map/ppermute | solution.py:19
  (2 other events, 3.9 us)

commit v2 on v1

--- a/solution.py
+++ b/solution.py
@@ -8,7 +8,7 @@
 LAT = 512
 EXPERTS = 32
 CAP = 8
-AWAY = (0, 1, 7, 4, 2, 3, 6, 5)
+PLANE = ("z", "y")
 SOFTMAX_SCALE = 192 ** (-0.5)
 BF = jnp.bfloat16
 F32 = jnp.float32
@@ -52,27 +52,18 @@
     return (combined / denominator[:, :, None]).astype(BF)
 
 
-def pack_rows(core, hidden, norm_gain, routes, gate_weights):
+def slot_rows(core, hidden, norm_gain, routes, gate_weights):
     requests, model_width = hidden.shape
     half = model_width // 2
     slots = EXPERTS * CAP
     top = routes.shape[1]
 
-    def kernel(
-        core_ref, all_ref, half_ref, gain_ref, routes_ref, ids_ref, gates_ref, out_ref, mix_ref
-    ):
+    def kernel(core_ref, all_ref, half_ref, gain_ref, routes_ref, gates_ref, out_ref, mix_ref):
         del core_ref
-        wide = all_ref[...].astype(F32)
-        inverse = lax.rsqrt(jnp.mean(wide * wide, axis=1, keepdims=True) + 1e-06)
-        normed = half_ref[...].astype(F32) * inverse * gain_ref[...]
-        out_ref[:, :half] = normed.astype(BF)
-        named = routes_ref[...].astype(F32)
-        fill = jnp.full((requests, 128 - top), -1.0, F32)
-        out_ref[:, half:] = jnp.concatenate([named, fill], axis=1).astype(BF)
-        ids = ids_ref[...].astype(F32)
+        ids = routes_ref[...].astype(F32)
         gates = gates_ref[...].astype(F32)
         place = lax.broadcasted_iota(jnp.int32, (slots, requests), 0)
-        expert = (((place >> 3) & 7) * 4 + (place >> 6)).astype(F32)
+        expert = (place >> 3).astype(F32)
         member = jnp.zeros((slots, requests), F32)
         weight = jnp.zeros((slots, requests), F32)
         for k in range(top):
@@ -85,11 +76,20 @@
         earlier = jnp.dot(member.astype(BF), before, preferred_element_type=F32)
         fits = (member > 0.5) & (earlier == (place & 7).astype(F32))
         mix_ref[...] = jnp.where(fits, weight, 0.0).astype(BF)
+        chosen = jnp.where(fits, 1.0, 0.0).astype(BF)
+        wide = all_ref[...].astype(F32)
+        inverse = lax.rsqrt(jnp.mean(wide * wide, axis=1, keepdims=True) + 1e-06)
+        for start in range(0, half, 512):
+            columns = slice(start, start + 512)
+            normed = half_ref[:, columns].astype(F32) * inverse * gain_ref[:, columns]
+            out_ref[:, columns] = jnp.dot(
+                chosen, normed.astype(BF), preferred_element_type=F32
+            ).astype(BF)
 
     return pl.pallas_call(
         kernel,
         out_shape=(
-            jax.ShapeDtypeStruct((requests, half + 128), BF),
+            jax.ShapeDtypeStruct((slots, half), BF),
             jax.ShapeDtypeStruct((slots, requests), BF),
         ),
         grid_spec=pltpu.PrefetchScalarGridSpec(
@@ -99,69 +99,15 @@
                 pl.BlockSpec((requests, model_width), lambda i, c: (0, 0)),
                 pl.BlockSpec((requests, half), lambda i, c: (0, c[0])),
                 pl.BlockSpec((1, half), lambda i, c: (0, c[0])),
-                pl.BlockSpec((requests, top), lambda i, c: (0, 0)),
                 pl.BlockSpec((top, requests), lambda i, c: (0, 0)),
                 pl.BlockSpec((top, requests), lambda i, c: (0, 0)),
             ],
             out_specs=(
-                pl.BlockSpec((requests, half + 128), lambda i, c: (0, 0)),
+                pl.BlockSpec((slots, half), lambda i, c: (0, 0)),
                 pl.BlockSpec((slots, requests), lambda i, c: (0, 0)),
             ),
         ),
-    )(
-        core.reshape(1),
-        hidden,
-        hidden,
-        norm_gain.reshape(1, -1),
-        routes,
-        routes.T,
-        gate_weights.T,
-    )
-
-
-def choose_rows(z_index, blocks):
-    count = len(blocks)
-    half = blocks[0].shape[1] - 128
-    rows = 8 * 16
-    span = 4 * CAP
-    lanes = 8 * span
-
-    def kernel(z_ref, *refs):
-        sources, outs = refs[:count], refs[count:]
-        z = z_ref[0]
-        ids = jnp.concatenate([ref[:, half:] for ref in sources], axis=0).astype(F32)
-        lane = lax.broadcasted_iota(jnp.int32, (rows, lanes), 1)
-        block = lax.broadcasted_iota(jnp.int32, (rows, lanes), 0) >> 4
-        away = sum(jnp.where(block == n, by, 0) for n, by in enumerate(AWAY))
-        rank = (lane >> 7) * 4 + ((lane >> 3) & 3)
-        expert = (z * 4 + ((lane >> 5) & 3)).astype(F32)
-        member = jnp.zeros((rows, lanes), F32)
-        for k in range(8):
-            member = jnp.where(ids[:, k : k + 1] == expert, 1.0, member)
-        left = lax.broadcasted_iota(jnp.int32, (rows, rows), 0)
-        right = lax.broadcasted_iota(jnp.int32, (rows, rows), 1)
-        lower = jnp.where((right < left) & (right >> 4 == left >> 4), 1.0, 0.0)
-        slot = jnp.dot(lower.astype(BF), member.astype(BF), preferred_element_type=F32)
-        fits = (member > 0.5) & (slot == (lane & 7).astype(F32))
-        fits = fits & (rank == ((z + 8 - away) & 7))
-        chosen = jnp.where(fits, 1.0, 0.0).astype(BF)
-        for start in range(0, half, 512):
-            columns = slice(start, start + 512)
-            data = jnp.concatenate([ref[:, columns] for ref in sources], axis=0)
-            picked = lax.dot_general(
-                chosen, data, (((0,), (0,)), ((), ())), preferred_element_type=F32
-            ).astype(BF)
-            for n in range(8):
-                outs[n // 4][n % 4, :, columns] = picked[n * span : (n + 1) * span]
-
-    shape = jax.ShapeDtypeStruct((4, span, half), BF)
-    vmem = pl.BlockSpec(memory_space=pltpu.VMEM)
-    return pl.pallas_call(
-        kernel,
-        out_shape=(shape,) * 2,
-        in_specs=[pl.BlockSpec(memory_space=pltpu.SMEM)] + [vmem] * count,
-        out_specs=(vmem,) * 2,
-    )(z_index.reshape(1), *blocks)
+    )(core.reshape(1), hidden, hidden, norm_gain.reshape(1, -1), routes.T, gate_weights.T)
 
 
 def add_experts(core, hidden, mix, returned):
@@ -213,20 +159,13 @@
     core = lax.axis_index("ep").astype(jnp.int32)
     x_index = lax.axis_index("x").astype(jnp.int32)
 
-    z_index = lax.axis_index("z").astype(jnp.int32)
-    packed, mix = pack_rows(core, hidden, norm_gain, routes, gate_weights)
-    packed, gate_proj, up_proj, down_proj = lax.optimization_barrier(
-        (packed, gate_proj, up_proj, down_proj)
-    )
-    after, before = shifted(packed, "z", 1), shifted(packed, "z", -1)
-    opposite = shifted(packed, "z", 4)
-    upward = shifted(jnp.concatenate([packed, after], axis=0), "z", 2)
-    downward = shifted(jnp.concatenate([packed, before], axis=0), "z", -2)
-    picked = choose_rows(z_index, [packed, after, before, opposite, upward, downward])
-    low, high = [
-        lax.all_to_all(part, "y", split_axis=0, concat_axis=0, tiled=True).reshape(-1, half)
-        for part in picked
-    ]
+    outbound, mix = slot_rows(core, hidden, norm_gain, routes, gate_weights)
+    outbound, gate_proj, up_proj, down_proj = lax.optimization_barrier(
+        (outbound, gate_proj, up_proj, down_proj)
+    )
+    rows = lax.all_to_all(
+        outbound.reshape(EXPERTS, CAP, half), PLANE, split_axis=0, concat_axis=0, tiled=True
+    ).reshape(count, half)
 
     both = jnp.concatenate([gate_proj[0], up_proj[0]], axis=1)
     far_weights = lax.dynamic_slice_in_dim(both, (1 - core) * half, half, 0)
@@ -243,15 +182,13 @@
         return jnp.concatenate(parts, axis=0)
 
     near_down, far_down = down_rows(core), down_rows(1 - core)
-    low, high, mixed, near_down, far_down, queries, latent_cache, movers = (
+    rows, mixed, near_down, far_down, queries, latent_cache, movers = (
         lax.optimization_barrier(
-            (low, high, mixed, near_down, far_down, queries, latent_cache, movers)
+            (rows, mixed, near_down, far_down, queries, latent_cache, movers)
         )
     )
 
-    ahead_low, behind_low = shifted(low, "x", 1), shifted(low, "x", -1)
-    ahead_high, behind_high = shifted(high, "x", 1), shifted(high, "x", -1)
-    across_low, across_high = shifted(ahead_low, "x", 1), shifted(behind_high, "x", -1)
+    ahead, behind = shifted(rows, "x", 1), shifted(rows, "x", -1)
 
     attention = attend(queries, latent_cache, cache_lens, core)
     listed = movers[0]
@@ -272,15 +209,14 @@
         total = jnp.concatenate(totals, axis=0)
         value = total[:, :256] + shifted(total[:, 256:], "ep", 1)
         activated = (jax.nn.silu(value[:, :128]) * value[:, 128:]).astype(BF)
-        activated = jnp.swapaxes(activated.reshape(-1, 2, 4, 4 * CAP, 128), 1, 2)
         return activated.reshape(-1, count, 128)
 
-    own = activate(products([low, high]))
-    ahead_low, ahead_high, behind_low, behind_high, own, served = lax.optimization_barrier(
-        (ahead_low, ahead_high, behind_low, behind_high, own, served)
-    )
-    after_x = products([behind_low, behind_high])
-    before_x = products([ahead_low, ahead_high])
+    own = activate(products([rows]))
+    ahead, behind, own, served = lax.optimization_barrier((ahead, behind, own, served))
+    middle = count // 2
+    across_low = shifted(ahead[:middle], "x", 1)
+    across_high = shifted(behind[middle:], "x", -1)
+    after_x, before_x = products([behind]), products([ahead])
     across_low, across_high, after_x, before_x = lax.optimization_barrier(
         (across_low, across_high, after_x, before_x)
     )
@@ -296,7 +232,7 @@
     ).astype(BF)
     returned = lax.all_to_all(
         expert_out.reshape(4 * EXPERTS, CAP, -1),
-        ("x", "y", "z"),
+        ("x",) + PLANE,
         split_axis=0,
         concat_axis=0,
         tiled=True,

time: 252 us -> 212 us (0.84)
  starting transfers between devices: 41.5 us -> 25.1 us
  waiting for transfers between devices: 102 us -> 85.9 us
    ppermute x21 -> x14, waiting for transfers between devices: 88.2 us -> 53.2 us  [shifted(): lax.ppermute(x, axis, [(i, (i + by) % devices) for i in range(devices)])]
    all_to_all x2 -> x1, waiting for transfers between devices: 13.6 us -> 32.7 us  [local(): lax.all_to_all(outbound.reshape(EXPERTS, CAP, half), PLANE, split_axis=0,...]
    ppermute x21 -> x14, starting transfers between devices: 32.8 us -> 13.7 us  [shifted(): lax.ppermute(x, axis, [(i, (i + by) % devices) for i in range(devices)])]
    all_to_all x2 -> x1, starting transfers between devices: 8.67 us -> 11.4 us  [local(): lax.all_to_all(outbound.reshape(EXPERTS, CAP, half), PLANE, split_axis=0,...]
    pallas_call x2 -> x1, Pallas kernels: 5.45 us -> 3.22 us  [slot_rows(): pl.pallas_call(kernel, out_shape=(jax.ShapeDtypeStruct((slots, half), BF)...]
    dot_general x8 -> x5, matrix products: 9.77 us -> 7.58 us  [products(): return [jnp.dot(b, mixed, preferred_element_type=F32) for b in blocks]]
  transfers between devices with their start and end apart: 23 -> 15, of which waited for: 15 -> 12; matrix products, arithmetic and copies ran while one was open for 11% -> 13% of each run, Pallas kernels for 1% -> 0%
where the time goes in v2:
time: 212 us
  waiting for transfers between devices  85.9 us (41%)
  blocking collectives  59.2 us (28%)
  starting transfers between devices  25.1 us (12%)
  matrix products  13.5 us (6%)
  other arithmetic  11.3 us (5%)
  local copies, waits for them, and re-layouts  8.51 us (4%)
  Pallas kernels  6.97 us (3%)
    all_to_all x1, blocking collectives, local(): lax.all_to_all(expert_out.reshape(4 * EXPERTS, CAP, -1), ('x',) + PLANE,...  59.2 us
    ppermute x14, waiting for transfers between devices, shifted(): lax.ppermute(x, axis, [(i, (i + by) % devices) for i in range(devices)])  53.2 us
    all_to_all x1, waiting for transfers between devices, local(): lax.all_to_all(outbound.reshape(EXPERTS, CAP, half), PLANE, split_axis=0,...  32.7 us
    ppermute x14, starting transfers between devices, shifted(): lax.ppermute(x, axis, [(i, (i + by) % devices) for i in range(devices)])  13.7 us
    all_to_all x1, starting transfers between devices, local(): lax.all_to_all(outbound.reshape(EXPERTS, CAP, half), PLANE, split_axis=0,...  11.4 us
    dot_general x5, matrix products, products(): return [jnp.dot(b, mixed, preferred_element_type=F32) for b in blocks]  7.58 us
    optimization_barrier x1, local copies, waits for them, and re-layouts, local(): lax.optimization_barrier((rows, mixed, near_down, far_down, queries, late...  4.33 us
  transfers between devices with their start and end apart: 15, of which 12 were waited for; matrix products, arithmetic and copies ran while one was open for 13% of the time, Pallas kernels for 0%

profile of v2, /device:TPU:32, one launch (start us, length us, event | category | flops | bytes accessed | tf_op | source)
XLA Modules:
  0.0 211.5 jit_solution(9008670023265946132)
XLA Ops:
  0.7 3.2 %shard_map.122 = (bf16[256,3584]{1,0:T(8,128)(2,1)}, bf16[256,16]{1,0:T(8,128)(2,1)}) custom-call(s32[1]{0:T(128)} %bitcast.core_ref, bf16[16,7168]{1,0:T(8,128)(2,1)} %hidden_ref.1, bf16[16,7168]{1,0:T(8,128)(2,1)} %hidden_ref.1, f32[1,7168]{1,0:T(1,128)} %bitcast.100, s32[8,16]{1,0:T(8,128)} %bitcast.101, bf16[8,16]{1,0:T(8,128)(2,1)} %bitcast.102), custom_call_target="tpu_custom_call" | custom-call | tf_op jit(solution)/shard_map/pallas_call | solution.py:89
  3.9 11.4 %all-to-all-start = ((bf16[32,8,3584]{2,1,0:T(8,128)(2,1)}), bf16[32,8,3584]{2,1,0:T(8,128)(2,1)}, u32[]{:S(2)}, u32[]{:S(2)}) async-start(bf16[32,8,3584]{2,1,0:T(8,128)(2,1)} %bitcast.94), calls=%async_computation | async-start | bytes 3670016 | tf_op jit(solution)/shard_map/all_to_all | solution.py:166
  15.3 3.7 %fusion.4 = (bf16[3584,256]{1,0:T(8,128)(2,1)S(1)}, bf16[3584,256]{1,0:T(8,128)(2,1)}) fusion(s32[]{:T(128)S(6)} %select_n.85, bf16[7168,128]{1,0:T(8,128)(2,1)} %bitcast.95, bf16[7168,128]{1,0:T(8,128)(2,1)} %bitcast.96, s32[]{:T(128)S(6)} %select_n.86), kind=kLoop, calls=%fused_computation.10 | loop fusion | flops 7340032 | bytes 7340040 | tf_op jit(solution)/shard_map/concatenate | solution.py:170
  19.0 1.7 dynamic-slice_bitcast_fusion.3
  20.7 1.4 pad_maximum_fusion.2
  23.1 3.5 %pad_maximum_fusion = bf16[3584,512]{1,0:T(8,128)(2,1)} fusion(bf16[3584,256]{1,0:T(8,128)(2,1)} %collective-permute-done, bf16[3584,256]{1,0:T(8,128)(2,1)S(1)} %get-tuple-element.49), kind=kLoop, calls=%fused_computation.4 | loop fusion | flops 7340032 | bytes 7340032 | tf_op jit(solution)/shard_map/concatenate | solution.py:173
  26.6 32.7 %all-to-all-done = bf16[32,8,3584]{2,1,0:T(8,128)(2,1)} async-done(((bf16[32,8,3584]{2,1,0:T(8,128)(2,1)}), bf16[32,8,3584]{2,1,0:T(8,128)(2,1)}, u32[]{:S(2)}, u32[]{:S(2)}) %all-to-all-start) | async-done | bytes 1835040 | tf_op jit(solution)/shard_map/all_to_all | solution.py:166
  59.4 1.5 collective-permute-start.1
  60.9 1.7 collective-permute-start.2
  62.6 4.3 %copy.16 = bf16[16,128,576]{2,1,0:T(8,128)(2,1)} copy(bf16[16,128,576]{1,2,0:T(8,128)(2,1)} %param.12) | data formatting | bytes 4718592 | tf_op jit(solution)/shard_map/optimization_barrier | solution.py:186
  67.0 2.5 %fusion.35 = (f32[16,64]{1,0:T(8,128)S(1)}, f32[16,64,128]{2,1,0:T(8,128)S(1)}) fusion(bf16[16,64,576]{2,1,0:T(8,128)(2,1)S(1)} %copy-done, bf16[16,128,576]{1,2,0:T(8,128)(2,1)} %param.12, pred[16,128]{1,0:T(8,128)(4,1)S(1)} %broadcast_compare_fusion), kind=kOutput, calls=%fused_computation.88 | convolution fusion | flops 151387136 | bytes 4069376 | tf_op jit(solution)/shard_map/shc,stc->sht/dot_general | solution.py:25
  71.9 2.6 %fusion.36 = f32[256,512]{1,0:T(8,128)S(1)} fusion(bf16[256,3584]{1,0:T(8,128)(2,1)} %bitcast.5, bf16[3584,512]{1,0:T(8,128)(2,1)S(1)} %copy-done.1), kind=kOutput, calls=%fused_computation.89 | convolution fusion | flops 939524096 | bytes 6029312 | tf_op jit(solution)/shard_map/dot_general | solution.py:206
  74.8 1.3 collective-permute-done.3
  77.0 1.5 collective-permute-start.6
  78.6 10.7 %collective-permute-done.6 = bf16[4,32,512]{2,1,0:T(8,128)(2,1)S(1)} collective-permute-done((bf16[4,32,512]{2,1,0:T(8,128)(2,1)S(1)}, bf16[4,32,512]{2,1,0:T(8,128)(2,1)S(1)}, u32[]{:S(2)}, u32[]{:S(2)}) %collective-permute-start.6) | collective-permute-done | bytes 131104 | tf_op jit(solution)/shard_map/ppermute | solution.py:19
  90.3 9.4 %collective-permute-done.1 = bf16[256,3584]{1,0:T(8,128)(2,1)S(1)} collective-permute-done((bf16[256,3584]{1,0:T(8,128)(2,1)}, bf16[256,3584]{1,0:T(8,128)(2,1)S(1)}, u32[]{:S(2)}, u32[]{:S(2)}) %collective-permute-start.1) | collective-permute-done | bytes 1835040 | tf_op jit(solution)/shard_map/ppermute | solution.py:19
  99.8 1.6 collective-permute-start.7
  101.4 1.2 slice.95
  102.6 2.0 collective-permute-start.8
  104.6 1.1 fusion.38
  105.7 2.6 %fusion.37 = f32[256,512]{1,0:T(8,128)S(1)} fusion(bf16[256,3584]{1,0:T(8,128)(2,1)} %collective-permute-done.2, bf16[3584,512]{1,0:T(8,128)(2,1)S(1)} %copy-done.1), kind=kOutput, calls=%fused_computation.90 | convolution fusion | flops 939524096 | bytes 6029312 | tf_op jit(solution)/shard_map/dot_general | solution.py:206
  108.3 11.0 %collective-permute-done.7 = bf16[128,3584]{1,0:T(8,128)(2,1)S(1)} collective-permute-done((bf16[128,3584]{1,0:T(8,128)(2,1)S(1)}, bf16[128,3584]{1,0:T(8,128)(2,1)S(1)}, u32[]{:S(2)}, u32[]{:S(2)}) %collective-permute-start.7) | collective-permute-done | bytes 917536 | tf_op jit(solution)/shard_map/ppermute | solution.py:19
  119.3 1.3 collective-permute-done.8
  122.1 2.3 %collective-permute-done.9 = f32[768,256]{1,0:T(8,128)S(1)} collective-permute-done((f32[768,256]{1,0:T(8,128)S(1)}, f32[768,256]{1,0:T(8,128)S(1)}, u32[]{:S(2)}, u32[]{:S(2)}) %collective-permute-start.9) | collective-permute-done | bytes 786464 | tf_op jit(solution)/shard_map/ppermute | solution.py:19
  124.8 3.2 %collective-permute-start.10 = (bf16[4,256,128]{2,1,0:T(8,128)(2,1)S(1)}, bf16[4,256,128]{2,1,0:T(8,128)(2,1)S(1)}, u32[]{:S(2)}, u32[]{:S(2)}) collective-permute-start(bf16[4,256,128]{2,1,0:T(8,128)(2,1)S(1)} %pad_maximum_fusion.5), channel_id=1, source_target_pairs={{0,6},{2,0},{4,2},{6,4},{1,7},{3,1},{5,3},{7,5},{8,14},{10,8},{12,... | collective-permute-start | bytes 786440 | tf_op jit(solution)/shard_map/ppermute | solution.py:19
  129.2 10.2 %collective-permute-done.10 = bf16[4,256,128]{2,1,0:T(8,128)(2,1)S(1)} collective-permute-done((bf16[4,256,128]{2,1,0:T(8,128)(2,1)S(1)}, bf16[4,256,128]{2,1,0:T(8,128)(2,1)S(1)}, u32[]{:S(2)}, u32[]{:S(2)}) %collective-permute-start.10) | collective-permute-done | bytes 262176 | tf_op jit(solution)/shard_map/ppermute | solution.py:19
  139.5 3.4 %collective-permute-done.12 = bf16[4,256,128]{2,1,0:T(8,128)(2,1)S(1)} collective-permute-done((bf16[4,256,128]{2,1,0:T(8,128)(2,1)S(1)}, bf16[4,256,128]{2,1,0:T(8,128)(2,1)S(1)}, u32[]{:S(2)}, u32[]{:S(2)}) %collective-permute-start.12) | collective-permute-done | bytes 262176 | tf_op jit(solution)/shard_map/ppermute | solution.py:19
  143.4 2.6 %collective-permute-done.13 = bf16[1024,512]{1,0:T(8,128)(2,1)S(1)} collective-permute-done((bf16[1024,512]{1,0:T(8,128)(2,1)S(1)}, bf16[1024,512]{1,0:T(8,128)(2,1)S(1)}, u32[]{:S(2)}, u32[]{:S(2)}) %collective-permute-start.13) | collective-permute-done | bytes 1048608 | tf_op jit(solution)/shard_map/ppermute | solution.py:19
  146.0 1.2 fusion.41
  147.3 1.3 fusion.2
  148.6 59.2 %all_to_all.10 = bf16[128,8,896]{2,1,0:T(8,128)(2,1)} all-to-all(bf16[128,8,896]{2,1,0:T(8,128)(2,1)S(1)} %fusion.2), channel_id=1, replica_groups=mesh['z'=8,'y'=4,'x'=4,'ep'=2] {'x','z','y'}, dimensions={0} | all-to-all | bytes 3670016 | tf_op jit(solution)/shard_map/all_to_all | solution.py:233
  207.8 3.7 %shard_map.123 = bf16[16,3584]{1,0:T(8,128)(2,1)} custom-call(s32[1]{0:T(128)} %bitcast.core_ref, bf16[16,7168]{1,0:T(8,128)(2,1)} %hidden_ref.1, bf16[256,16]{1,0:T(8,128)(2,1)} %get-tuple-element.34.mix_ref, bf16[4,256,896]{2,1,0:T(8,128)(2,1)} %bitcast.93), custom_call_target="tpu_custom_call" | custom-call | tf_op jit(solution)/shard_map/pallas_call | solution.py:127
  (64 shorter events, 9.2 us)
Async XLA Ops:
  0.6 66.3 %copy-start = (bf16[16,64,576]{2,1,0:T(8,128)(2,1)S(1)}, bf16[16,64,576]{2,1,0:T(8,128)(2,1)}, u32[]{:S(2)}) copy-start(bf16[16,64,576]{2,1,0:T(8,128)(2,1)} %param.11) | copy-start | bytes 3538948
  3.9 55.5 %all-to-all-start = ((bf16[32,8,3584]{2,1,0:T(8,128)(2,1)}), bf16[32,8,3584]{2,1,0:T(8,128)(2,1)}, u32[]{:S(2)}, u32[]{:S(2)}) async-start(bf16[32,8,3584]{2,1,0:T(8,128)(2,1)} %bitcast.94), calls=%async_computation | async-start | bytes 3670016 | tf_op jit(solution)/shard_map/all_to_all | solution.py:166
  19.0 4.1 %collective-permute-start = (bf16[3584,256]{1,0:T(8,128)(2,1)}, bf16[3584,256]{1,0:T(8,128)(2,1)}, u32[]{:S(2)}, u32[]{:S(2)}) collective-permute-start(bf16[3584,256]{1,0:T(8,128)(2,1)} %get-tuple-element.50), channel_id=1, source_target_pairs={{0,1},{1,0},{2,3},{3,2},{4,5},{5,4},{6,7},{7,6},{8,9},{9,8},{10,11... | collective-permute-start | bytes 5505032 | tf_op jit(solution)/shard_map/ppermute | solution.py:19
  20.7 1.4 copy-start.5
  59.4 40.2 %collective-permute-start.1 = (bf16[256,3584]{1,0:T(8,128)(2,1)}, bf16[256,3584]{1,0:T(8,128)(2,1)S(1)}, u32[]{:S(2)}, u32[]{:S(2)}) collective-permute-start(bf16[256,3584]{1,0:T(8,128)(2,1)} %bitcast.5), channel_id=1, source_target_pairs={{0,2},{2,4},{4,6},{6,0},{1,3},{3,5},{5,7},{7,1},{8,10},{10,12},{12... | collective-permute-start | bytes 5505032 | tf_op jit(solution)/shard_map/ppermute | solution.py:19
  60.9 38.9 %collective-permute-start.2 = (bf16[256,3584]{1,0:T(8,128)(2,1)}, bf16[256,3584]{1,0:T(8,128)(2,1)}, u32[]{:S(2)}, u32[]{:S(2)}) collective-permute-start(bf16[256,3584]{1,0:T(8,128)(2,1)} %bitcast.5), channel_id=1, source_target_pairs={{0,6},{2,0},{4,2},{6,4},{1,7},{3,1},{5,3},{7,5},{8,14},{10,8},{12,... | collective-permute-start | bytes 5505032 | tf_op jit(solution)/shard_map/ppermute | solution.py:19
  67.0 2.9 %copy-start.2 = (bf16[16,128,576]{2,1,0:T(8,128)(2,1)S(1)}, bf16[16,128,576]{2,1,0:T(8,128)(2,1)}, u32[]{:S(2)}) copy-start(bf16[16,128,576]{2,1,0:T(8,128)(2,1)} %copy.16) | copy-start | bytes 7077892
  69.9 2.0 copy-start.1
  70.5 5.7 %collective-permute-start.5 = (bf16[16,32,512]{2,1,0:T(8,128)(2,1)S(1)}, bf16[16,32,512]{2,1,0:T(8,128)(2,1)S(1)}, u32[]{:S(2)}, u32[]{:S(2)}) collective-permute-start(bf16[16,32,512]{2,1,0:T(8,128)(2,1)S(1)} %dynamic-slice_convert_fusion), channel_id=1, source_target_pairs={{0,1},{1,0},{2,3},{3,2},{4,5},{5,4},{6,7},{7,6},{8,9},{9,8},{10,11... | collective-permute-start | bytes 1572872 | tf_op jit(solution)/shard_map/ppermute | solution.py:19
  70.7 3.9 %copy-start.6 = (s32[1,4]{1,0:T(1,128)S(1)}, s32[1,4]{1,0:T(1,128)}, u32[]{:S(2)}) copy-start(s32[1,4]{1,0:T(1,128)} %param.14) | copy-start | bytes 52
  70.7 4.0 %collective-permute-start.4 = (f32[2,16,32]{2,1,0:T(8,128)S(1)}, f32[2,16,32]{2,1,0:T(8,128)S(1)}, u32[]{:S(2)}, u32[]{:S(2)}) collective-permute-start(f32[2,16,32]{2,1,0:T(8,128)S(1)} %pad_maximum_fusion.9), channel_id=1, source_target_pairs={{0,1},{1,0},{2,3},{3,2},{4,5},{5,4},{6,7},{7,6},{8,9},{9,8},{10,11... | collective-permute-start | bytes 12296 | tf_op jit(solution)/shard_map/ppermute | solution.py:19
  74.6 1.6 collective-permute-start.3
  77.0 12.3 %collective-permute-start.6 = (bf16[4,32,512]{2,1,0:T(8,128)(2,1)S(1)}, bf16[4,32,512]{2,1,0:T(8,128)(2,1)S(1)}, u32[]{:S(2)}, u32[]{:S(2)}) collective-permute-start(bf16[4,32,512]{2,1,0:T(8,128)(2,1)S(1)} %copy.22), channel_id=1, source_target_pairs={{0,128},{32,160},{64,192},{96,224},{128,0},{160,32},{192,64},{224,... | collective-permute-start | bytes 393224 | tf_op jit(solution)/shard_map/ppermute | solution.py:19
  99.8 19.5 %collective-permute-start.7 = (bf16[128,3584]{1,0:T(8,128)(2,1)S(1)}, bf16[128,3584]{1,0:T(8,128)(2,1)S(1)}, u32[]{:S(2)}, u32[]{:S(2)}) collective-permute-start(bf16[128,3584]{1,0:T(8,128)(2,1)S(1)} %slice.94), channel_id=1, source_target_pairs={{0,2},{2,4},{4,6},{6,0},{1,3},{3,5},{5,7},{7,1},{8,10},{10,12},{12... | collective-permute-start | bytes 2752520 | tf_op jit(solution)/shard_map/ppermute | solution.py:19
  102.6 17.9 %collective-permute-start.8 = (bf16[128,3584]{1,0:T(8,128)(2,1)S(1)}, bf16[128,3584]{1,0:T(8,128)(2,1)S(1)}, u32[]{:S(2)}, u32[]{:S(2)}) collective-permute-start(bf16[128,3584]{1,0:T(8,128)(2,1)S(1)} %slice.95), channel_id=1, source_target_pairs={{0,6},{2,0},{4,2},{6,4},{1,7},{3,1},{5,3},{7,5},{8,14},{10,8},{12,... | collective-permute-start | bytes 2752520 | tf_op jit(solution)/shard_map/ppermute | solution.py:19
  122.0 2.4 %collective-permute-start.9 = (f32[768,256]{1,0:T(8,128)S(1)}, f32[768,256]{1,0:T(8,128)S(1)}, u32[]{:S(2)}, u32[]{:S(2)}) collective-permute-start(f32[768,256]{1,0:T(8,128)S(1)} %slice.123), channel_id=1, source_target_pairs={{0,1},{1,0},{2,3},{3,2},{4,5},{5,4},{6,7},{7,6},{8,9},{9,8},{10,11... | collective-permute-start | bytes 2359304 | tf_op jit(solution)/shard_map/ppermute | solution.py:19
  124.8 14.7 %collective-permute-start.10 = (bf16[4,256,128]{2,1,0:T(8,128)(2,1)S(1)}, bf16[4,256,128]{2,1,0:T(8,128)(2,1)S(1)}, u32[]{:S(2)}, u32[]{:S(2)}) collective-permute-start(bf16[4,256,128]{2,1,0:T(8,128)(2,1)S(1)} %pad_maximum_fusion.5), channel_id=1, source_target_pairs={{0,6},{2,0},{4,2},{6,4},{1,7},{3,1},{5,3},{7,5},{8,14},{10,8},{12,... | collective-permute-start | bytes 786440 | tf_op jit(solution)/shard_map/ppermute | solution.py:19
  128.0 11.5 %collective-permute-start.11 = (bf16[4,256,128]{2,1,0:T(8,128)(2,1)S(1)}, bf16[4,256,128]{2,1,0:T(8,128)(2,1)S(1)}, u32[]{:S(2)}, u32[]{:S(2)}) collective-permute-start(bf16[4,256,128]{2,1,0:T(8,128)(2,1)S(1)} %pad_maximum_fusion.5), channel_id=1, source_target_pairs={{0,4},{2,6},{4,0},{6,2},{1,5},{3,7},{5,1},{7,3},{8,12},{10,14},{12... | collective-permute-start | bytes 786440 | tf_op jit(solution)/shard_map/ppermute | solution.py:19
  128.1 14.8 %collective-permute-start.12 = (bf16[4,256,128]{2,1,0:T(8,128)(2,1)S(1)}, bf16[4,256,128]{2,1,0:T(8,128)(2,1)S(1)}, u32[]{:S(2)}, u32[]{:S(2)}) collective-permute-start(bf16[4,256,128]{2,1,0:T(8,128)(2,1)S(1)} %pad_maximum_fusion.5), channel_id=1, source_target_pairs={{0,2},{2,4},{4,6},{6,0},{1,3},{3,5},{5,7},{7,1},{8,10},{10,12},{12... | collective-permute-start | bytes 786440 | tf_op jit(solution)/shard_map/ppermute | solution.py:19
  143.1 3.0 %copy-start.4 = (bf16[512,896]{1,0:T(8,128)(2,1)S(1)}, bf16[512,896]{1,0:T(8,128)(2,1)}, u32[]{:S(2)}) copy-start(bf16[512,896]{1,0:T(8,128)(2,1)} %get-tuple-element.43) | copy-start | bytes 2752516
  143.3 4.0 %copy-start.3 = (bf16[512,896]{1,0:T(8,128)(2,1)S(1)}, bf16[512,896]{1,0:T(8,128)(2,1)}, u32[]{:S(2)}) copy-start(bf16[512,896]{1,0:T(8,128)(2,1)} %get-tuple-element.42) | copy-start | bytes 2752516
  143.3 2.7 %collective-permute-start.13 = (bf16[1024,512]{1,0:T(8,128)(2,1)S(1)}, bf16[1024,512]{1,0:T(8,128)(2,1)S(1)}, u32[]{:S(2)}, u32[]{:S(2)}) collective-permute-start(bf16[1024,512]{1,0:T(8,128)(2,1)S(1)} %constant_dynamic-slice_fusion), channel_id=1, source_target_pairs={{0,1},{1,0},{2,3},{3,2},{4,5},{5,4},{6,7},{7,6},{8,9},{9,8},{10,11... | collective-permute-start | bytes 3145736 | tf_op jit(solution)/shard_map/ppermute | solution.py:19

commit v3 on v2

--- a/solution.py
+++ b/solution.py
@@ -58,7 +58,9 @@
     slots = EXPERTS * CAP
     top = routes.shape[1]
 
-    def kernel(core_ref, all_ref, half_ref, gain_ref, routes_ref, gates_ref, out_ref, mix_ref):
+    part = half // 2
+
+    def kernel(core_ref, all_ref, half_ref, gain_ref, routes_ref, gates_ref, *out_refs):
         del core_ref
         ids = routes_ref[...].astype(F32)
         gates = gates_ref[...].astype(F32)
@@ -75,21 +77,22 @@
         before = jnp.where(left < right, 1.0, 0.0).astype(BF)
         earlier = jnp.dot(member.astype(BF), before, preferred_element_type=F32)
         fits = (member > 0.5) & (earlier == (place & 7).astype(F32))
-        mix_ref[...] = jnp.where(fits, weight, 0.0).astype(BF)
+        out_refs[2][...] = jnp.where(fits, weight, 0.0).astype(BF)
         chosen = jnp.where(fits, 1.0, 0.0).astype(BF)
         wide = all_ref[...].astype(F32)
         inverse = lax.rsqrt(jnp.mean(wide * wide, axis=1, keepdims=True) + 1e-06)
-        for start in range(0, half, 512):
-            columns = slice(start, start + 512)
+        for start in range(0, half, 256):
+            columns = slice(start, start + 256)
             normed = half_ref[:, columns].astype(F32) * inverse * gain_ref[:, columns]
-            out_ref[:, columns] = jnp.dot(
+            out_refs[start // part][:, start % part : start % part + 256] = jnp.dot(
                 chosen, normed.astype(BF), preferred_element_type=F32
             ).astype(BF)
 
     return pl.pallas_call(
         kernel,
         out_shape=(
-            jax.ShapeDtypeStruct((slots, half), BF),
+            jax.ShapeDtypeStruct((slots, part), BF),
+            jax.ShapeDtypeStruct((slots, part), BF),
             jax.ShapeDtypeStruct((slots, requests), BF),
         ),
         grid_spec=pltpu.PrefetchScalarGridSpec(
@@ -103,7 +106,8 @@
                 pl.BlockSpec((top, requests), lambda i, c: (0, 0)),
             ],
             out_specs=(
-                pl.BlockSpec((slots, half), lambda i, c: (0, 0)),
+                pl.BlockSpec((slots, part), lambda i, c: (0, 0)),
+                pl.BlockSpec((slots, part), lambda i, c: (0, 0)),
                 pl.BlockSpec((slots, requests), lambda i, c: (0, 0)),
             ),
         ),
@@ -113,30 +117,26 @@
 def add_experts(core, hidden, mix, returned):
     requests = hidden.shape[0]
     blocks, slots, width = returned.shape
+    half = blocks * width
 
     def kernel(core_ref, hidden_ref, mix_ref, returned_ref, out_ref):
-        del core_ref
-        weighted = lax.dot_general(
-            mix_ref[...],
-            returned_ref[0],
-            (((0,), (0,)), ((), ())),
-            preferred_element_type=F32,
-        )
-        out_ref[...] = (hidden_ref[...].astype(F32) + weighted).astype(BF)
-
+        own = hidden_ref[:, pl.ds(pl.multiple_of(core_ref[0] * half, 128), half)]
+        for n in range(blocks):
+            columns = slice(n * width, (n + 1) * width)
+            weighted = lax.dot_general(
+                mix_ref[...],
+                returned_ref[n],
+                (((0,), (0,)), ((), ())),
+                preferred_element_type=F32,
+            )
+            out_ref[:, columns] = (own[:, columns].astype(F32) + weighted).astype(BF)
+
+    vmem = pl.BlockSpec(memory_space=pltpu.VMEM)
     return pl.pallas_call(
         kernel,
-        out_shape=jax.ShapeDtypeStruct((requests, blocks * width), BF),
-        grid_spec=pltpu.PrefetchScalarGridSpec(
-            num_scalar_prefetch=1,
-            grid=(blocks,),
-            in_specs=[
-                pl.BlockSpec((requests, width), lambda i, c: (0, c[0] * blocks + i)),
-                pl.BlockSpec((slots, requests), lambda i, c: (0, 0)),
-                pl.BlockSpec((1, slots, width), lambda i, c: (i, 0, 0)),
-            ],
-            out_specs=pl.BlockSpec((requests, width), lambda i, c: (0, i)),
-        ),
+        out_shape=jax.ShapeDtypeStruct((requests, half), BF),
+        in_specs=[pl.BlockSpec(memory_space=pltpu.SMEM)] + [vmem] * 3,
+        out_specs=vmem,
     )(core.reshape(1), hidden, mix, returned)
 
 
@@ -159,13 +159,18 @@
     core = lax.axis_index("ep").astype(jnp.int32)
     x_index = lax.axis_index("x").astype(jnp.int32)
 
-    outbound, mix = slot_rows(core, hidden, norm_gain, routes, gate_weights)
-    outbound, gate_proj, up_proj, down_proj = lax.optimization_barrier(
-        (outbound, gate_proj, up_proj, down_proj)
-    )
-    rows = lax.all_to_all(
-        outbound.reshape(EXPERTS, CAP, half), PLANE, split_axis=0, concat_axis=0, tiled=True
-    ).reshape(count, half)
+    first, second, mix = slot_rows(core, hidden, norm_gain, routes, gate_weights)
+    first, second, gate_proj, up_proj, down_proj = lax.optimization_barrier(
+        (first, second, gate_proj, up_proj, down_proj)
+    )
+
+    def along_plane(part):
+        part = part.reshape(EXPERTS, CAP, -1)
+        part = lax.all_to_all(part, PLANE, split_axis=0, concat_axis=0, tiled=True)
+        return part.reshape(count, -1)
+
+    first = along_plane(first)
+    first, second = lax.optimization_barrier((first, second))
 
     both = jnp.concatenate([gate_proj[0], up_proj[0]], axis=1)
     far_weights = lax.dynamic_slice_in_dim(both, (1 - core) * half, half, 0)
@@ -182,13 +187,14 @@
         return jnp.concatenate(parts, axis=0)
 
     near_down, far_down = down_rows(core), down_rows(1 - core)
-    rows, mixed, near_down, far_down, queries, latent_cache, movers = (
+    gathered = lax.all_gather(first, "x", axis=0, tiled=True)
+    second = along_plane(second)
+    second, mixed, near_down, far_down, queries, latent_cache, movers = (
         lax.optimization_barrier(
-            (rows, mixed, near_down, far_down, queries, latent_cache, movers)
+            (second, mixed, near_down, far_down, queries, latent_cache, movers)
         )
     )
-
-    ahead, behind = shifted(rows, "x", 1), shifted(rows, "x", -1)
+    ahead, behind = shifted(second, "x", 1), shifted(second, "x", -1)
 
     attention = attend(queries, latent_cache, cache_lens, core)
     listed = movers[0]
@@ -202,8 +208,10 @@
         [jnp.where(flagged[:, None, None], nothing, attention), arrived_contexts], axis=0
     )
 
-    def products(blocks):
-        return [jnp.dot(b, mixed, preferred_element_type=F32) for b in blocks]
+    def product(rows, features):
+        return jnp.dot(rows, mixed[features], preferred_element_type=F32)
+
+    early, late = slice(0, half // 2), slice(half // 2, half)
 
     def activate(totals):
         total = jnp.concatenate(totals, axis=0)
@@ -211,16 +219,24 @@
         activated = (jax.nn.silu(value[:, :128]) * value[:, 128:]).astype(BF)
         return activated.reshape(-1, count, 128)
 
-    own = activate(products([rows]))
-    ahead, behind, own, served = lax.optimization_barrier((ahead, behind, own, served))
+    own = activate([product(first, early) + product(second, late)])
+    ahead, behind, own = lax.optimization_barrier((ahead, behind, own))
     middle = count // 2
     across_low = shifted(ahead[:middle], "x", 1)
     across_high = shifted(behind[middle:], "x", -1)
-    after_x, before_x = products([behind]), products([ahead])
-    across_low, across_high, after_x, before_x = lax.optimization_barrier(
-        (across_low, across_high, after_x, before_x)
-    )
-    others = activate(after_x + products([across_low, across_high]) + before_x)
+    after_x, before_x = product(behind, late), product(ahead, late)
+    across_low, across_high, after_x, before_x, served = lax.optimization_barrier(
+        (across_low, across_high, after_x, before_x, served)
+    )
+    in_order = product(gathered, early)
+
+    def early_part(by):
+        return lax.dynamic_slice_in_dim(in_order, (x_index + by) % 4 * count, count, 0)
+
+    opposite = jnp.concatenate([product(across_low, late), product(across_high, late)], axis=0)
+    others = activate(
+        [early_part(1) + after_x, early_part(2) + opposite, early_part(3) + before_x]
+    )
     acts = jnp.concatenate([own, others], axis=0)
     held = [acts] + [shifted(acts, "x", -by) for by in (1, 2, 3)]
     stripes = [jnp.concatenate([held[s][(r - s) % 4] for s in range(4)], axis=1) for r in range(4)]

time: 212 us -> 233 us (1.099)
  between operations: 1 us -> 14.5 us
  starting transfers between devices: 25.1 us -> 30.7 us
  matrix products: 13.5 us -> 17.5 us
  waiting for transfers between devices: 85.9 us -> 82.4 us
    ppermute x14, waiting for transfers between devices: 53.2 us -> 46.9 us  [shifted(): lax.ppermute(x, axis, [(i, (i + by) % devices) for i in range(devices)])]
    all_to_all x1 -> x2, starting transfers between devices: 11.4 us -> 17.5 us  [along_plane(): part = lax.all_to_all(part, PLANE, split_axis=0, concat_axis=0, tiled=True)]
    dot_general x5 -> x7, matrix products: 7.58 us -> 11.5 us  [product(): return jnp.dot(rows, mixed[features], preferred_element_type=F32)]
    all_to_all x1 -> x2, waiting for transfers between devices: 32.7 us -> 35.4 us  [along_plane(): part = lax.all_to_all(part, PLANE, split_axis=0, concat_axis=0, tiled=True)]
  transfers between devices with their start and end apart: 15 -> 17, of which waited for: 12 -> 12; matrix products, arithmetic and copies ran while one was open for 13% -> 13% of each run, Pallas kernels for 0% -> 0%
where the time goes in v3:
time: 233 us; the launch traced here: 232 us
  waiting for transfers between devices  82.4 us (35%)
  blocking collectives  59 us (25%)
  starting transfers between devices  30.7 us (13%)
  matrix products  17.5 us (8%)
  between operations  14.5 us (6%)
  other arithmetic  13.1 us (6%)
  local copies, waits for them, and re-layouts  8.99 us (4%)
  Pallas kernels  5.73 us (2%)
    all_to_all x1, blocking collectives, local(): lax.all_to_all(expert_out.reshape(4 * EXPERTS, CAP, -1), ('x',) + PLANE,...  59 us
    ppermute x14, waiting for transfers between devices, shifted(): lax.ppermute(x, axis, [(i, (i + by) % devices) for i in range(devices)])  46.9 us
    all_to_all x2, waiting for transfers between devices, along_plane(): part = lax.all_to_all(part, PLANE, split_axis=0, concat_axis=0, tiled=True)  35.4 us
    all_to_all x2, starting transfers between devices, along_plane(): part = lax.all_to_all(part, PLANE, split_axis=0, concat_axis=0, tiled=True)  17.5 us
    ppermute x14, starting transfers between devices, shifted(): lax.ppermute(x, axis, [(i, (i + by) % devices) for i in range(devices)])  13.1 us
    dot_general x7, matrix products, product(): return jnp.dot(rows, mixed[features], preferred_element_type=F32)  11.5 us
  transfers between devices with their start and end apart: 17, of which 12 were waited for; matrix products, arithmetic and copies ran while one was open for 13% of the time, Pallas kernels for 0%

profile of v3, /device:TPU:32, one launch (start us, length us, event | category | flops | bytes accessed | tf_op | source)
XLA Modules:
  0.0 231.9 jit_solution(14144044217526045170)
XLA Ops:
  7.2 3.0 %shard_map.122 = (bf16[256,1792]{1,0:T(8,128)(2,1)}, bf16[256,1792]{1,0:T(8,128)(2,1)}, bf16[256,16]{1,0:T(8,128)(2,1)}) custom-call(s32[1]{0:T(128)} %bitcast.core_ref, bf16[16,7168]{1,0:T(8,128)(2,1)} %hidden_ref.1, bf16[16,7168]{1,0:T(8,128)(2,1)} %hidden_ref.1, f32[1,7168]{1,0:T(1,128)} %bitcast.100, s32[8,16]{1,0:T(8,128)} %bitcast.101, ...), custom_call_target="tpu_custom_call" | custom-call | tf_op jit(solution)/shard_map/pallas_call | solution.py:91
  10.2 11.4 %all-to-all-start = ((bf16[32,8,1792]{2,1,0:T(8,128)(2,1)}), bf16[32,8,1792]{2,1,0:T(8,128)(2,1)}, u32[]{:S(2)}, u32[]{:S(2)}) async-start(bf16[32,8,1792]{2,1,0:T(8,128)(2,1)} %bitcast.99), calls=%async_computation | async-start | bytes 1835008 | tf_op jit(solution)/shard_map/all_to_all | solution.py:169
  21.6 3.7 %fusion.4 = (bf16[3584,256]{1,0:T(8,128)(2,1)S(1)}, bf16[3584,256]{1,0:T(8,128)(2,1)}) fusion(s32[]{:T(128)S(6)} %select_n.100, bf16[7168,128]{1,0:T(8,128)(2,1)} %bitcast.93, bf16[7168,128]{1,0:T(8,128)(2,1)} %bitcast.94, s32[]{:T(128)S(6)} %select_n.101), kind=kLoop, calls=%fused_computation.10 | loop fusion | flops 7340032 | bytes 7340040 | tf_op jit(solution)/shard_map/concatenate | solution.py:175
  25.3 21.1 %all-to-all-done = bf16[32,8,1792]{2,1,0:T(8,128)(2,1)} async-done(((bf16[32,8,1792]{2,1,0:T(8,128)(2,1)}), bf16[32,8,1792]{2,1,0:T(8,128)(2,1)}, u32[]{:S(2)}, u32[]{:S(2)}) %all-to-all-start) | async-done | bytes 917536 | tf_op jit(solution)/shard_map/all_to_all | solution.py:169
  46.4 6.1 %all-to-all-start.1 = ((bf16[32,8,1792]{2,1,0:T(8,128)(2,1)}), bf16[32,8,1792]{2,1,0:T(8,128)(2,1)}, u32[]{:S(2)}, u32[]{:S(2)}) async-start(bf16[32,8,1792]{2,1,0:T(8,128)(2,1)} %bitcast.98), calls=%async_computation.1 | async-start | bytes 1835008 | tf_op jit(solution)/shard_map/all_to_all | solution.py:169
  52.7 2.7 %dynamic-slice_bitcast_fusion.3 = (bf16[128,896]{1,0:T(8,128)(2,1)S(1)}, bf16[128,896]{1,0:T(8,128)(2,1)}, bf16[128,896]{1,0:T(8,128)(2,1)}, bf16[128,896]{1,0:T...) fusion(bf16[1,1024,896]{2,1,0:T(8,128)(2,1)} %param.21, ...), kind=kLoop, calls=%fused_computation.59 | loop fusion | bytes 3670048 | tf_op jit(solution)/shard_map/dynamic_slice | solution.py:185
  55.5 2.9 %pad_maximum_fusion.2 = (bf16[512,896]{1,0:T(8,128)(2,1)}, bf16[512,896]{1,0:T(8,128)(2,1)}) fusion(bf16[128,896]{1,0:T(8,128)(2,1)} %get-tuple-element.66, bf16[128,896]{1,0:T(8,128)(2,1)} %get-tuple-element.67, bf16[128,896]{1,0:T(8,128)(2,1)} %get-tuple-element.68, bf16[128,896]{1,0:T(8,128)(2,1)} %get-tuple-element.69, ...), kind=kLoop, calls=%fused_computation.31 | loop fusion | flops 7340032 | bytes 3670016 | tf_op jit(solution)/shard_map/concatenate | solution.py:187
  58.5 3.6 %pad_maximum_fusion = bf16[3584,512]{1,0:T(8,128)(2,1)} fusion(bf16[3584,256]{1,0:T(8,128)(2,1)} %collective-permute-done, bf16[3584,256]{1,0:T(8,128)(2,1)S(1)} %get-tuple-element.57), kind=kLoop, calls=%fused_computation.4 | loop fusion | flops 7340032 | bytes 7340032 | tf_op jit(solution)/shard_map/concatenate | solution.py:178
  62.1 14.3 %all-to-all-done.1 = bf16[32,8,1792]{2,1,0:T(8,128)(2,1)} async-done(((bf16[32,8,1792]{2,1,0:T(8,128)(2,1)}), bf16[32,8,1792]{2,1,0:T(8,128)(2,1)}, u32[]{:S(2)}, u32[]{:S(2)}) %all-to-all-start.1) | async-done | bytes 917536 | tf_op jit(solution)/shard_map/all_to_all | solution.py:169
  76.4 1.5 collective-permute-start.1
  77.9 1.7 collective-permute-start.2
  79.6 4.4 %copy.16 = bf16[16,128,576]{2,1,0:T(8,128)(2,1)} copy(bf16[16,128,576]{1,2,0:T(8,128)(2,1)} %param.12) | data formatting | bytes 4718592 | tf_op jit(solution)/shard_map/optimization_barrier | solution.py:193
  84.0 2.6 %fusion.52 = (f32[16,64]{1,0:T(8,128)S(1)}, f32[16,64,128]{2,1,0:T(8,128)S(1)}) fusion(bf16[16,64,576]{2,1,0:T(8,128)(2,1)S(1)} %copy-done, bf16[16,128,576]{1,2,0:T(8,128)(2,1)} %param.12, pred[16,128]{1,0:T(8,128)(4,1)S(1)} %broadcast_compare_fusion), kind=kOutput, calls=%fused_computation.106 | convolution fusion | flops 151387136 | bytes 4069376 | tf_op jit(solution)/shard_map/shc,stc->sht/dot_general | solution.py:25
  88.6 1.8 fusion.21
  90.5 1.8 fusion.10
  94.8 1.9 collective-permute-start.8
  96.7 10.4 %collective-permute-done.8 = bf16[4,32,512]{2,1,0:T(8,128)(2,1)S(1)} collective-permute-done((bf16[4,32,512]{2,1,0:T(8,128)(2,1)S(1)}, bf16[4,32,512]{2,1,0:T(8,128)(2,1)S(1)}, u32[]{:S(2)}, u32[]{:S(2)}) %collective-permute-start.8) | collective-permute-done | bytes 131104 | tf_op jit(solution)/shard_map/ppermute | solution.py:19
  108.0 11.3 %collective-permute-done.1 = bf16[256,1792]{1,0:T(8,128)(2,1)S(1)} collective-permute-done((bf16[256,1792]{1,0:T(8,128)(2,1)}, bf16[256,1792]{1,0:T(8,128)(2,1)S(1)}, u32[]{:S(2)}, u32[]{:S(2)}) %collective-permute-start.1) | collective-permute-done | bytes 917536 | tf_op jit(solution)/shard_map/ppermute | solution.py:19
  119.4 1.6 collective-permute-start.4
  122.0 2.0 collective-permute-start.5
  124.6 1.8 fusion.19
  126.4 5.8 %collective-permute-done.4 = bf16[128,1792]{1,0:T(8,128)(2,1)S(1)} collective-permute-done((bf16[128,1792]{1,0:T(8,128)(2,1)S(1)}, bf16[128,1792]{1,0:T(8,128)(2,1)S(1)}, u32[]{:S(2)}, u32[]{:S(2)}) %collective-permute-start.4) | collective-permute-done | bytes 458784 | tf_op jit(solution)/shard_map/ppermute | solution.py:19
  133.0 4.7 %fusion.5 = f32[1024,512]{1,0:T(8,128)S(1)} fusion(bf16[1024,1792]{1,0:T(8,128)(2,1)} %all-gather.2.cloned.1.call-done, bf16[3584,512]{1,0:T(8,128)(2,1)} %pad_maximum_fusion), kind=kOutput, calls=%fused_computation.11 | convolution fusion | flops 1879048192 | bytes 7602176 | tf_op jit(solution)/shard_map/dot_general | solution.py:212
  138.4 2.3 collective-permute-done.9
  141.0 1.6 collective-permute-start.10
  142.5 1.4 collective-permute-start.11
  144.5 5.7 %collective-permute-done.10 = bf16[4,256,128]{2,1,0:T(8,128)(2,1)S(1)} collective-permute-done((bf16[4,256,128]{2,1,0:T(8,128)(2,1)S(1)}, bf16[4,256,128]{2,1,0:T(8,128)(2,1)S(1)}, u32[]{:S(2)}, u32[]{:S(2)}) %collective-permute-start.10) | collective-permute-done | bytes 262176 | tf_op jit(solution)/shard_map/ppermute | solution.py:19
  150.2 3.0 %collective-permute-done.11 = bf16[4,256,128]{2,1,0:T(8,128)(2,1)S(1)} collective-permute-done((bf16[4,256,128]{2,1,0:T(8,128)(2,1)S(1)}, bf16[4,256,128]{2,1,0:T(8,128)(2,1)S(1)}, u32[]{:S(2)}, u32[]{:S(2)}) %collective-permute-start.11) | collective-permute-done | bytes 262176 | tf_op jit(solution)/shard_map/ppermute | solution.py:19
  153.3 4.4 %collective-permute-done.12 = bf16[4,256,128]{2,1,0:T(8,128)(2,1)S(1)} collective-permute-done((bf16[4,256,128]{2,1,0:T(8,128)(2,1)S(1)}, bf16[4,256,128]{2,1,0:T(8,128)(2,1)S(1)}, u32[]{:S(2)}, u32[]{:S(2)}) %collective-permute-start.12) | collective-permute-done | bytes 262176 | tf_op jit(solution)/shard_map/ppermute | solution.py:19
  158.2 2.6 %collective-permute-done.13 = bf16[1024,512]{1,0:T(8,128)(2,1)S(1)} collective-permute-done((bf16[1024,512]{1,0:T(8,128)(2,1)S(1)}, bf16[1024,512]{1,0:T(8,128)(2,1)S(1)}, u32[]{:S(2)}, u32[]{:S(2)}) %collective-permute-start.13) | collective-permute-done | bytes 1048608 | tf_op jit(solution)/shard_map/ppermute | solution.py:19
  163.4 59.0 %all_to_all.15 = bf16[128,8,896]{2,1,0:T(8,128)(2,1)} all-to-all(bf16[128,8,896]{2,1,0:T(8,128)(2,1)S(1)} %fusion.2), channel_id=1, replica_groups=mesh['z'=8,'y'=4,'x'=4,'ep'=2] {'x','z','y'}, dimensions={0} | all-to-all | bytes 3670016 | tf_op jit(solution)/shard_map/all_to_all | solution.py:249
  222.3 2.7 %shard_map.123 = bf16[16,3584]{1,0:T(8,128)(2,1)} custom-call(s32[1]{0:T(128)} %bitcast.core_ref, bf16[16,7168]{1,0:T(8,128)(2,1)} %hidden_ref.1, bf16[256,16]{1,0:T(8,128)(2,1)} %get-tuple-element.44.mix_ref, bf16[4,256,896]{2,1,0:T(8,128)(2,1)} %bitcast.92), custom_call_target="tpu_custom_call" | custom-call | tf_op jit(solution)/shard_map/pallas_call | solution.py:135
  (72 shorter events, 12.7 us)
Async XLA Ops:
  7.2 76.8 %copy-start = (bf16[16,64,576]{2,1,0:T(8,128)(2,1)S(1)}, bf16[16,64,576]{2,1,0:T(8,128)(2,1)}, u32[]{:S(2)}) copy-start(bf16[16,64,576]{2,1,0:T(8,128)(2,1)} %param.11) | copy-start | bytes 3538948
  10.2 36.2 %all-to-all-start = ((bf16[32,8,1792]{2,1,0:T(8,128)(2,1)}), bf16[32,8,1792]{2,1,0:T(8,128)(2,1)}, u32[]{:S(2)}, u32[]{:S(2)}) async-start(bf16[32,8,1792]{2,1,0:T(8,128)(2,1)} %bitcast.99), calls=%async_computation | async-start | bytes 1835008 | tf_op jit(solution)/shard_map/all_to_all | solution.py:169
  25.3 33.2 %collective-permute-start = (bf16[3584,256]{1,0:T(8,128)(2,1)}, bf16[3584,256]{1,0:T(8,128)(2,1)}, u32[]{:S(2)}, u32[]{:S(2)}) collective-permute-start(bf16[3584,256]{1,0:T(8,128)(2,1)} %get-tuple-element.58), channel_id=1, source_target_pairs={{0,1},{1,0},{2,3},{3,2},{4,5},{5,4},{6,7},{7,6},{8,9},{9,8},{10,11... | collective-permute-start | bytes 5505032 | tf_op jit(solution)/shard_map/ppermute | solution.py:19
  46.4 29.9 %all-to-all-start.1 = ((bf16[32,8,1792]{2,1,0:T(8,128)(2,1)}), bf16[32,8,1792]{2,1,0:T(8,128)(2,1)}, u32[]{:S(2)}, u32[]{:S(2)}) async-start(bf16[32,8,1792]{2,1,0:T(8,128)(2,1)} %bitcast.98), calls=%async_computation.1 | async-start | bytes 1835008 | tf_op jit(solution)/shard_map/all_to_all | solution.py:169
  52.6 80.5 %all-gather.2.cloned.1.call-start = ((), (), s32[]{:S(2)}) async-start(), calls=%async_computation.3 | async-start | bytes 4587520 | tf_op jit(solution)/shard_map/all_gather | solution.py:190
  55.5 2.9 %copy-start.5 = (s32[16]{0:T(128)S(1)}, s32[16]{0:T(128)}, u32[]{:S(2)}) copy-start(s32[16]{0:T(128)} %param.13) | copy-start | bytes 196
  76.4 42.9 %collective-permute-start.1 = (bf16[256,1792]{1,0:T(8,128)(2,1)}, bf16[256,1792]{1,0:T(8,128)(2,1)S(1)}, u32[]{:S(2)}, u32[]{:S(2)}) collective-permute-start(bf16[256,1792]{1,0:T(8,128)(2,1)} %bitcast.7), channel_id=1, source_target_pairs={{0,2},{2,4},{4,6},{6,0},{1,3},{3,5},{5,7},{7,1},{8,10},{10,12},{12... | collective-permute-start | bytes 2752520 | tf_op jit(solution)/shard_map/ppermute | solution.py:19
  77.9 41.5 %collective-permute-start.2 = (bf16[256,1792]{1,0:T(8,128)(2,1)}, bf16[256,1792]{1,0:T(8,128)(2,1)}, u32[]{:S(2)}, u32[]{:S(2)}) collective-permute-start(bf16[256,1792]{1,0:T(8,128)(2,1)} %bitcast.7), channel_id=1, source_target_pairs={{0,6},{2,0},{4,2},{6,4},{1,7},{3,1},{5,3},{7,5},{8,14},{10,8},{12,... | collective-permute-start | bytes 2752520 | tf_op jit(solution)/shard_map/ppermute | solution.py:19
  84.0 2.6 %copy-start.1 = (bf16[16,128,576]{2,1,0:T(8,128)(2,1)S(1)}, bf16[16,128,576]{2,1,0:T(8,128)(2,1)}, u32[]{:S(2)}) copy-start(bf16[16,128,576]{2,1,0:T(8,128)(2,1)} %copy.16) | copy-start | bytes 7077892
  86.6 2.0 copy-start.3
  87.2 6.8 %collective-permute-start.7 = (bf16[16,32,512]{2,1,0:T(8,128)(2,1)S(1)}, bf16[16,32,512]{2,1,0:T(8,128)(2,1)S(1)}, u32[]{:S(2)}, u32[]{:S(2)}) collective-permute-start(bf16[16,32,512]{2,1,0:T(8,128)(2,1)S(1)} %dynamic-slice_convert_fusion), channel_id=1, source_target_pairs={{0,1},{1,0},{2,3},{3,2},{4,5},{5,4},{6,7},{7,6},{8,9},{9,8},{10,11... | collective-permute-start | bytes 1572872 | tf_op jit(solution)/shard_map/ppermute | solution.py:19
  87.8 4.7 %collective-permute-start.6 = (f32[2,16,32]{2,1,0:T(8,128)S(1)}, f32[2,16,32]{2,1,0:T(8,128)S(1)}, u32[]{:S(2)}, u32[]{:S(2)}) collective-permute-start(f32[2,16,32]{2,1,0:T(8,128)S(1)} %pad_maximum_fusion.9), channel_id=1, source_target_pairs={{0,1},{1,0},{2,3},{3,2},{4,5},{5,4},{6,7},{7,6},{8,9},{9,8},{10,11... | collective-permute-start | bytes 12296 | tf_op jit(solution)/shard_map/ppermute | solution.py:19
  90.4 2.0 copy-start.6
  92.3 1.6 collective-permute-start.3
  94.8 12.3 %collective-permute-start.8 = (bf16[4,32,512]{2,1,0:T(8,128)(2,1)S(1)}, bf16[4,32,512]{2,1,0:T(8,128)(2,1)S(1)}, u32[]{:S(2)}, u32[]{:S(2)}) collective-permute-start(bf16[4,32,512]{2,1,0:T(8,128)(2,1)S(1)} %copy.22), channel_id=1, source_target_pairs={{0,128},{32,160},{64,192},{96,224},{128,0},{160,32},{192,64},{224,... | collective-permute-start | bytes 393224 | tf_op jit(solution)/shard_map/ppermute | solution.py:19
  119.4 12.8 %collective-permute-start.4 = (bf16[128,1792]{1,0:T(8,128)(2,1)S(1)}, bf16[128,1792]{1,0:T(8,128)(2,1)S(1)}, u32[]{:S(2)}, u32[]{:S(2)}) collective-permute-start(bf16[128,1792]{1,0:T(8,128)(2,1)S(1)} %slice.104), channel_id=1, source_target_pairs={{0,2},{2,4},{4,6},{6,0},{1,3},{3,5},{5,7},{7,1},{8,10},{10,12},{12... | collective-permute-start | bytes 1376264 | tf_op jit(solution)/shard_map/ppermute | solution.py:19
  122.0 10.2 %collective-permute-start.5 = (bf16[128,1792]{1,0:T(8,128)(2,1)S(1)}, bf16[128,1792]{1,0:T(8,128)(2,1)S(1)}, u32[]{:S(2)}, u32[]{:S(2)}) collective-permute-start(bf16[128,1792]{1,0:T(8,128)(2,1)S(1)} %slice.105), channel_id=1, source_target_pairs={{0,6},{2,0},{4,2},{6,4},{1,7},{3,1},{5,3},{7,5},{8,14},{10,8},{12,... | collective-permute-start | bytes 1376264 | tf_op jit(solution)/shard_map/ppermute | solution.py:19
  138.3 2.4 %collective-permute-start.9 = (f32[768,256]{1,0:T(8,128)S(1)}, f32[768,256]{1,0:T(8,128)S(1)}, u32[]{:S(2)}, u32[]{:S(2)}) collective-permute-start(f32[768,256]{1,0:T(8,128)S(1)} %slice.136), channel_id=1, source_target_pairs={{0,1},{1,0},{2,3},{3,2},{4,5},{5,4},{6,7},{7,6},{8,9},{9,8},{10,11... | collective-permute-start | bytes 2359304 | tf_op jit(solution)/shard_map/ppermute | solution.py:19
  141.0 9.2 %collective-permute-start.10 = (bf16[4,256,128]{2,1,0:T(8,128)(2,1)S(1)}, bf16[4,256,128]{2,1,0:T(8,128)(2,1)S(1)}, u32[]{:S(2)}, u32[]{:S(2)}) collective-permute-start(bf16[4,256,128]{2,1,0:T(8,128)(2,1)S(1)} %pad_maximum_fusion.5), channel_id=1, source_target_pairs={{0,6},{2,0},{4,2},{6,4},{1,7},{3,1},{5,3},{7,5},{8,14},{10,8},{12,... | collective-permute-start | bytes 786440 | tf_op jit(solution)/shard_map/ppermute | solution.py:19
  142.5 10.7 %collective-permute-start.11 = (bf16[4,256,128]{2,1,0:T(8,128)(2,1)S(1)}, bf16[4,256,128]{2,1,0:T(8,128)(2,1)S(1)}, u32[]{:S(2)}, u32[]{:S(2)}) collective-permute-start(bf16[4,256,128]{2,1,0:T(8,128)(2,1)S(1)} %pad_maximum_fusion.5), channel_id=1, source_target_pairs={{0,4},{2,6},{4,0},{6,2},{1,5},{3,7},{5,1},{7,3},{8,12},{10,14},{12... | collective-permute-start | bytes 786440 | tf_op jit(solution)/shard_map/ppermute | solution.py:19
  143.9 13.8 %collective-permute-start.12 = (bf16[4,256,128]{2,1,0:T(8,128)(2,1)S(1)}, bf16[4,256,128]{2,1,0:T(8,128)(2,1)S(1)}, u32[]{:S(2)}, u32[]{:S(2)}) collective-permute-start(bf16[4,256,128]{2,1,0:T(8,128)(2,1)S(1)} %pad_maximum_fusion.5), channel_id=1, source_target_pairs={{0,2},{2,4},{4,6},{6,0},{1,3},{3,5},{5,7},{7,1},{8,10},{10,12},{12... | collective-permute-start | bytes 786440 | tf_op jit(solution)/shard_map/ppermute | solution.py:19
  157.9 3.0 %copy-start.4 = (bf16[512,896]{1,0:T(8,128)(2,1)S(1)}, bf16[512,896]{1,0:T(8,128)(2,1)}, u32[]{:S(2)}) copy-start(bf16[512,896]{1,0:T(8,128)(2,1)} %get-tuple-element.51) | copy-start | bytes 2752516
  158.1 4.0 %copy-start.2 = (bf16[512,896]{1,0:T(8,128)(2,1)S(1)}, bf16[512,896]{1,0:T(8,128)(2,1)}, u32[]{:S(2)}) copy-start(bf16[512,896]{1,0:T(8,128)(2,1)} %get-tuple-element.50) | copy-start | bytes 2752516
  158.1 2.7 %collective-permute-start.13 = (bf16[1024,512]{1,0:T(8,128)(2,1)S(1)}, bf16[1024,512]{1,0:T(8,128)(2,1)S(1)}, u32[]{:S(2)}, u32[]{:S(2)}) collective-permute-start(bf16[1024,512]{1,0:T(8,128)(2,1)S(1)} %constant_dynamic-slice_fusion), channel_id=1, source_target_pairs={{0,1},{1,0},{2,3},{3,2},{4,5},{5,4},{6,7},{7,6},{8,9},{9,8},{10,11... | collective-permute-start | bytes 3145736 | tf_op jit(solution)/shard_map/ppermute | solution.py:19
Sparse Core Ops, SparseCore 0:
  55.6 69.1 all-gather.1

commit v4 on v3

--- a/solution.py
+++ b/solution.py
@@ -57,10 +57,9 @@
     half = model_width // 2
     slots = EXPERTS * CAP
     top = routes.shape[1]
-
-    part = half // 2
-
-    def kernel(core_ref, all_ref, half_ref, gain_ref, routes_ref, gates_ref, *out_refs):
+    width = half // 4
+
+    def kernel(core_ref, all_ref, half_ref, gain_ref, routes_ref, gates_ref, out_ref, mix_ref):
         del core_ref
         ids = routes_ref[...].astype(F32)
         gates = gates_ref[...].astype(F32)
@@ -77,22 +76,21 @@
         before = jnp.where(left < right, 1.0, 0.0).astype(BF)
         earlier = jnp.dot(member.astype(BF), before, preferred_element_type=F32)
         fits = (member > 0.5) & (earlier == (place & 7).astype(F32))
-        out_refs[2][...] = jnp.where(fits, weight, 0.0).astype(BF)
+        mix_ref[...] = jnp.where(fits, weight, 0.0).astype(BF)
         chosen = jnp.where(fits, 1.0, 0.0).astype(BF)
         wide = all_ref[...].astype(F32)
         inverse = lax.rsqrt(jnp.mean(wide * wide, axis=1, keepdims=True) + 1e-06)
-        for start in range(0, half, 256):
-            columns = slice(start, start + 256)
+        for n in range(4):
+            columns = slice(n * width, (n + 1) * width)
             normed = half_ref[:, columns].astype(F32) * inverse * gain_ref[:, columns]
-            out_refs[start // part][:, start % part : start % part + 256] = jnp.dot(
+            out_ref[n] = jnp.dot(
                 chosen, normed.astype(BF), preferred_element_type=F32
             ).astype(BF)
 
     return pl.pallas_call(
         kernel,
         out_shape=(
-            jax.ShapeDtypeStruct((slots, part), BF),
-            jax.ShapeDtypeStruct((slots, part), BF),
+            jax.ShapeDtypeStruct((4, slots, width), BF),
             jax.ShapeDtypeStruct((slots, requests), BF),
         ),
         grid_spec=pltpu.PrefetchScalarGridSpec(
@@ -106,8 +104,7 @@
                 pl.BlockSpec((top, requests), lambda i, c: (0, 0)),
             ],
             out_specs=(
-                pl.BlockSpec((slots, part), lambda i, c: (0, 0)),
-                pl.BlockSpec((slots, part), lambda i, c: (0, 0)),
+                pl.BlockSpec((4, slots, width), lambda i, c: (0, 0, 0)),
                 pl.BlockSpec((slots, requests), lambda i, c: (0, 0)),
             ),
         ),
@@ -159,23 +156,29 @@
     core = lax.axis_index("ep").astype(jnp.int32)
     x_index = lax.axis_index("x").astype(jnp.int32)
 
-    first, second, mix = slot_rows(core, hidden, norm_gain, routes, gate_weights)
-    first, second, gate_proj, up_proj, down_proj = lax.optimization_barrier(
-        (first, second, gate_proj, up_proj, down_proj)
-    )
-
-    def along_plane(part):
-        part = part.reshape(EXPERTS, CAP, -1)
-        part = lax.all_to_all(part, PLANE, split_axis=0, concat_axis=0, tiled=True)
-        return part.reshape(count, -1)
-
-    first = along_plane(first)
-    first, second = lax.optimization_barrier((first, second))
+    outbound, mix = slot_rows(core, hidden, norm_gain, routes, gate_weights)
+    outbound, gate_proj, up_proj, down_proj = lax.optimization_barrier(
+        (outbound, gate_proj, up_proj, down_proj)
+    )
+    rows = lax.all_to_all(
+        outbound.reshape(4 * EXPERTS, CAP, -1),
+        ("x",) + PLANE,
+        split_axis=0,
+        concat_axis=0,
+        tiled=True,
+    ).reshape(4 * count, -1)
 
     both = jnp.concatenate([gate_proj[0], up_proj[0]], axis=1)
     far_weights = lax.dynamic_slice_in_dim(both, (1 - core) * half, half, 0)
     near_weights = lax.dynamic_slice_in_dim(both, core * half, half, 0)
     mixed = jnp.concatenate([near_weights, shifted(far_weights, "ep", 1)], axis=1)
+
+    quarter = half // 4
+
+    def features_of(by):
+        return lax.dynamic_slice_in_dim(mixed, (x_index + 4 - by) % 4 * quarter, quarter, 0)
+
+    weights = [features_of(0)] + [shifted(features_of(by), "x", -by) for by in (1, 2, 3)]
 
     def down_rows(which):
         parts = []
@@ -187,14 +190,19 @@
         return jnp.concatenate(parts, axis=0)
 
     near_down, far_down = down_rows(core), down_rows(1 - core)
-    gathered = lax.all_gather(first, "x", axis=0, tiled=True)
-    second = along_plane(second)
-    second, mixed, near_down, far_down, queries, latent_cache, movers = (
+    rows, weights, near_down, far_down, queries, latent_cache, movers = (
         lax.optimization_barrier(
-            (second, mixed, near_down, far_down, queries, latent_cache, movers)
+            (rows, weights, near_down, far_down, queries, latent_cache, movers)
         )
     )
-    ahead, behind = shifted(second, "x", 1), shifted(second, "x", -1)
+
+    partial = [jnp.dot(rows, w, preferred_element_type=F32) for w in weights]
+    other_core = shifted(jnp.concatenate([p[:, 256:].astype(BF) for p in partial], axis=1), "ep", 1)
+    sums = [
+        p[:, :256] + other_core[:, n * 256 : (n + 1) * 256].astype(F32)
+        for n, p in enumerate(partial)
+    ]
+    arrived = [shifted(sums[by].astype(BF), "x", by) for by in (1, 2, 3)]
 
     attention = attend(queries, latent_cache, cache_lens, core)
     listed = movers[0]
@@ -208,40 +216,11 @@
         [jnp.where(flagged[:, None, None], nothing, attention), arrived_contexts], axis=0
     )
 
-    def product(rows, features):
-        return jnp.dot(rows, mixed[features], preferred_element_type=F32)
-
-    early, late = slice(0, half // 2), slice(half // 2, half)
-
-    def activate(totals):
-        total = jnp.concatenate(totals, axis=0)
-        value = total[:, :256] + shifted(total[:, 256:], "ep", 1)
-        activated = (jax.nn.silu(value[:, :128]) * value[:, 128:]).astype(BF)
-        return activated.reshape(-1, count, 128)
-
-    own = activate([product(first, early) + product(second, late)])
-    ahead, behind, own = lax.optimization_barrier((ahead, behind, own))
-    middle = count // 2
-    across_low = shifted(ahead[:middle], "x", 1)
-    across_high = shifted(behind[middle:], "x", -1)
-    after_x, before_x = product(behind, late), product(ahead, late)
-    across_low, across_high, after_x, before_x, served = lax.optimization_barrier(
-        (across_low, across_high, after_x, before_x, served)
-    )
-    in_order = product(gathered, early)
-
-    def early_part(by):
-        return lax.dynamic_slice_in_dim(in_order, (x_index + by) % 4 * count, count, 0)
-
-    opposite = jnp.concatenate([product(across_low, late), product(across_high, late)], axis=0)
-    others = activate(
-        [early_part(1) + after_x, early_part(2) + opposite, early_part(3) + before_x]
-    )
-    acts = jnp.concatenate([own, others], axis=0)
+    value = sums[0] + sum(part.astype(F32) for part in arrived)
+    acts = (jax.nn.silu(value[:, :128]) * value[:, 128:]).astype(BF)
+    acts, served = lax.optimization_barrier((acts, served))
     held = [acts] + [shifted(acts, "x", -by) for by in (1, 2, 3)]
-    stripes = [jnp.concatenate([held[s][(r - s) % 4] for s in range(4)], axis=1) for r in range(4)]
-    twice = jnp.concatenate(stripes + stripes[:3], axis=0)
-    joined = lax.dynamic_slice_in_dim(twice, (4 - x_index) % 4 * count, 4 * count, 0)
+    joined = jnp.concatenate(held, axis=1)
     expert_out = (
         jnp.dot(joined, near_down, preferred_element_type=F32)
         + jnp.dot(shifted(joined, "ep", 1), far_down, preferred_element_type=F32)

time: 233 us -> 229 us (0.983)
  between operations: 14.5 us -> 0.94 us
  waiting for transfers between devices: 82.4 us -> 90.4 us
  matrix products: 17.5 us -> 20.4 us
    ppermute x14 -> x15, waiting for transfers between devices: 46.9 us -> 90.4 us  [shifted(): lax.ppermute(x, axis, [(i, (i + by) % devices) for i in range(devices)])]
    all_to_all x2 -> x1, waiting for transfers between devices: 35.4 us -> 0.01 us  [local(): lax.all_to_all(outbound.reshape(4 * EXPERTS, CAP, -1), ('x',) + PLANE, sp...]
    dot_general x7 -> x4, matrix products: 11.5 us -> 14.3 us  [local(): partial = [jnp.dot(rows, w, preferred_element_type=F32) for w in weights]]
    concatenate x1, other arithmetic: 2.87 us -> 0.15 us  [down_rows(): return jnp.concatenate(parts, axis=0)]
    all_to_all x2 -> x1, starting transfers between devices: 17.5 us -> 15.4 us  [local(): lax.all_to_all(outbound.reshape(4 * EXPERTS, CAP, -1), ('x',) + PLANE, sp...]
    ppermute x14 -> x15, starting transfers between devices: 13.1 us -> 14.5 us  [shifted(): lax.ppermute(x, axis, [(i, (i + by) % devices) for i in range(devices)])]
  transfers between devices with their start and end apart: 17 -> 16, of which waited for: 12 -> 10; matrix products, arithmetic and copies ran while one was open for 13% -> 9% of each run, Pallas kernels for 0% -> 0%
where the time goes in v4:
time: 229 us; the launch traced here: 228 us
  waiting for transfers between devices  90.4 us (39%)
  blocking collectives  57.8 us (25%)
  starting transfers between devices  29.9 us (13%)
  matrix products  20.4 us (9%)
  other arithmetic  14.1 us (6%)
  local copies, waits for them, and re-layouts  9.05 us (4%)
  Pallas kernels  5.87 us (3%)
    ppermute x15, waiting for transfers between devices, shifted(): lax.ppermute(x, axis, [(i, (i + by) % devices) for i in range(devices)])  90.4 us
    all_to_all x1, blocking collectives, local(): lax.all_to_all(expert_out.reshape(4 * EXPERTS, CAP, -1), ('x',) + PLANE,...  57.8 us
    all_to_all x1, starting transfers between devices, local(): lax.all_to_all(outbound.reshape(4 * EXPERTS, CAP, -1), ('x',) + PLANE, sp...  15.4 us
    ppermute x15, starting transfers between devices, shifted(): lax.ppermute(x, axis, [(i, (i + by) % devices) for i in range(devices)])  14.5 us
    dot_general x4, matrix products, local(): partial = [jnp.dot(rows, w, preferred_element_type=F32) for w in weights]  14.3 us
  transfers between devices with their start and end apart: 16, of which 10 were waited for; matrix products, arithmetic and copies ran while one was open for 9% of the time, Pallas kernels for 0%

profile of v4, /device:TPU:32, one launch (start us, length us, event | category | flops | bytes accessed | tf_op | source)
XLA Modules:
  0.0 228.5 jit_solution(5743303354665744805)
XLA Ops:
  0.7 3.2 %shard_map.122 = (bf16[4,256,896]{2,1,0:T(8,128)(2,1)}, bf16[256,16]{1,0:T(8,128)(2,1)}) custom-call(s32[1]{0:T(128)} %bitcast.core_ref, bf16[16,7168]{1,0:T(8,128)(2,1)} %hidden_ref.1, bf16[16,7168]{1,0:T(8,128)(2,1)} %hidden_ref.1, f32[1,7168]{1,0:T(1,128)} %bitcast.67, s32[8,16]{1,0:T(8,128)} %bitcast.68, bf16[8,16]{1,0:T(8,128)(2,1)} %bitcast.69), custom_call_target="tpu_custom_call" | custom-call | tf_op jit(solution)/shard_map/pallas_call | solution.py:90
  3.8 15.4 %all-to-all-start = ((bf16[128,8,896]{2,1,0:T(8,128)(2,1)}), bf16[128,8,896]{2,1,0:T(8,128)(2,1)}, u32[]{:S(2)}, u32[]{:S(2)}) async-start(bf16[128,8,896]{2,1,0:T(8,128)(2,1)} %bitcast.64), calls=%async_computation | async-start | bytes 3670016 | tf_op jit(solution)/shard_map/all_to_all | solution.py:163
  19.3 3.7 %fusion.2 = (bf16[3584,256]{1,0:T(8,128)(2,1)}, bf16[3584,256]{1,0:T(8,128)(2,1)S(1)}) fusion(s32[]{:T(128)S(6)} %select_n.101, bf16[7168,128]{1,0:T(8,128)(2,1)} %bitcast.65, bf16[7168,128]{1,0:T(8,128)(2,1)} %bitcast.66, s32[]{:T(128)S(6)} %select_n.100), kind=kLoop, calls=%fused_computation.16 | loop fusion | flops 7340032 | bytes 7340040 | tf_op jit(solution)/shard_map/concatenate | solution.py:171
  22.9 4.1 %collective-permute-done = bf16[3584,256]{1,0:T(8,128)(2,1)} collective-permute-done((bf16[3584,256]{1,0:T(8,128)(2,1)}, bf16[3584,256]{1,0:T(8,128)(2,1)}, u32[]{:S(2)}, u32[]{:S(2)}) %collective-permute-start) | collective-permute-done | bytes 1835040 | tf_op jit(solution)/shard_map/ppermute | solution.py:19
  27.0 3.3 %fusion.10 = (bf16[896,512]{1,0:T(8,128)(2,1)}, bf16[896,512]{1,0:T(8,128)(2,1)}, bf16[896,512]{1,0:T(8,128)(2,1)}, bf16[896,512]{1,0:T(8,128)(2,1)}) fusion(s32[]{:T(128)S(6)} %select_n.109, bf16[3584,256]{1,0:T(8,128)(2,1)S(1)} %get-tuple-element.48, bf16[3584,256]{1,0:T(8,128)(2,1)} %collective-permute-done, s32[]{:T(128)S(6)} %select_n.103, ...), kind=kLoop, calls=%fused_computation.35 | loop fusion | flops 7340032 | bytes 7340048 | tf_op jit(solution)/shard_map/concatenate | solution.py:174
  30.4 3.2 %collective-permute-start.1 = (bf16[896,512]{1,0:T(8,128)(2,1)}, bf16[896,512]{1,0:T(8,128)(2,1)}, u32[]{:S(2)}, u32[]{:S(2)}) collective-permute-start(bf16[896,512]{1,0:T(8,128)(2,1)} %get-tuple-element.45), channel_id=1, source_target_pairs={{0,6},{2,0},{4,2},{6,4},{1,7},{3,1},{5,3},{7,5},{8,14},{10,8},{12,... | collective-permute-start | bytes 2752520 | tf_op jit(solution)/shard_map/ppermute | solution.py:19
  34.0 1.1 collective-permute-start.3
  35.1 1.7 dynamic-slice_bitcast_fusion.3
  37.0 47.5 %collective-permute-done.1 = bf16[896,512]{1,0:T(8,128)(2,1)} collective-permute-done((bf16[896,512]{1,0:T(8,128)(2,1)}, bf16[896,512]{1,0:T(8,128)(2,1)}, u32[]{:S(2)}, u32[]{:S(2)}) %collective-permute-start.1) | collective-permute-done | bytes 917536 | tf_op jit(solution)/shard_map/ppermute | solution.py:19
  84.4 3.5 %collective-permute-done.3 = bf16[896,512]{1,0:T(8,128)(2,1)} collective-permute-done((bf16[896,512]{1,0:T(8,128)(2,1)}, bf16[896,512]{1,0:T(8,128)(2,1)}, u32[]{:S(2)}, u32[]{:S(2)}) %collective-permute-start.3) | collective-permute-done | bytes 917536 | tf_op jit(solution)/shard_map/ppermute | solution.py:19
  87.9 3.0 %fusion.35 = f32[1024,512]{0,1:T(8,128)S(1)} fusion(bf16[1024,896]{1,0:T(8,128)(2,1)} %bitcast.5, bf16[896,512]{1,0:T(8,128)(2,1)} %get-tuple-element.26), kind=kOutput, calls=%fused_computation.86 | convolution fusion | flops 939524096 | bytes 4849664 | tf_op jit(solution)/shard_map/dot_general | solution.py:199
  90.9 3.8 %fusion.36 = f32[1024,512]{0,1:T(8,128)S(1)} fusion(bf16[1024,896]{1,0:T(8,128)(2,1)} %bitcast.5, bf16[896,512]{1,0:T(8,128)(2,1)} %collective-permute-done.1), kind=kOutput, calls=%fused_computation.87 | convolution fusion | flops 939524096 | bytes 4849664 | tf_op jit(solution)/shard_map/dot_general | solution.py:199
  94.7 3.8 %fusion.38 = f32[1024,512]{0,1:T(8,128)S(1)} fusion(bf16[1024,896]{1,0:T(8,128)(2,1)} %bitcast.5, bf16[896,512]{1,0:T(8,128)(2,1)} %collective-permute-done.3), kind=kOutput, calls=%fused_computation.89 | convolution fusion | flops 939524096 | bytes 4849664 | tf_op jit(solution)/shard_map/dot_general | solution.py:199
  98.6 3.7 %fusion.37 = f32[1024,512]{0,1:T(8,128)S(1)} fusion(bf16[1024,896]{1,0:T(8,128)(2,1)} %bitcast.5, bf16[896,512]{1,0:T(8,128)(2,1)} %collective-permute-done.2), kind=kOutput, calls=%fused_computation.88 | convolution fusion | flops 939524096 | bytes 4849664 | tf_op jit(solution)/shard_map/dot_general | solution.py:199
  102.3 1.4 copy-done.8
  104.0 1.5 pad_maximum_fusion
  105.5 4.3 %copy.16 = bf16[16,128,576]{2,1,0:T(8,128)(2,1)} copy(bf16[16,128,576]{1,2,0:T(8,128)(2,1)} %param.12) | data formatting | bytes 4718592 | tf_op jit(solution)/shard_map/optimization_barrier | solution.py:194
  109.9 2.5 %fusion.34 = (f32[16,64]{1,0:T(8,128)S(1)}, f32[16,64,128]{2,1,0:T(8,128)S(1)}) fusion(bf16[16,64,576]{2,1,0:T(8,128)(2,1)S(1)} %copy-done, bf16[16,128,576]{1,2,0:T(8,128)(2,1)} %param.12, pred[16,128]{1,0:T(8,128)(4,1)S(1)} %broadcast_compare_fusion), kind=kOutput, calls=%fused_computation.85 | convolution fusion | flops 151387136 | bytes 4069376 | tf_op jit(solution)/shard_map/shc,stc->sht/dot_general | solution.py:25
  115.5 2.0 fusion.8
  120.5 4.2 %collective-permute-start.10 = (bf16[4,32,512]{2,1,0:T(8,128)(2,1)S(1)}, bf16[4,32,512]{2,1,0:T(8,128)(2,1)S(1)}, u32[]{:S(2)}, u32[]{:S(2)}) collective-permute-start(bf16[4,32,512]{2,1,0:T(8,128)(2,1)S(1)} %copy.22), channel_id=1, source_target_pairs={{0,128},{32,160},{64,192},{96,224},{128,0},{160,32},{192,64},{224,... | collective-permute-start | bytes 393224 | tf_op jit(solution)/shard_map/ppermute | solution.py:19
  124.7 7.8 %collective-permute-done.10 = bf16[4,32,512]{2,1,0:T(8,128)(2,1)S(1)} collective-permute-done((bf16[4,32,512]{2,1,0:T(8,128)(2,1)S(1)}, bf16[4,32,512]{2,1,0:T(8,128)(2,1)S(1)}, u32[]{:S(2)}, u32[]{:S(2)}) %collective-permute-start.10) | collective-permute-done | bytes 131104 | tf_op jit(solution)/shard_map/ppermute | solution.py:19
  133.4 1.1 collective-permute-done.6
  134.6 10.5 %collective-permute-done.5 = bf16[1024,256]{0,1:T(8,128)(2,1)S(1)} collective-permute-done((bf16[1024,256]{0,1:T(8,128)(2,1)S(1)}, bf16[1024,256]{0,1:T(8,128)(2,1)S(1)}, u32[]{:S(2)}, u32[]{:S(2)}) %collective-permute-start.5) | collective-permute-done | bytes 524320 | tf_op jit(solution)/shard_map/ppermute | solution.py:19
  145.0 1.4 fusion.9
  148.9 7.0 %collective-permute-done.11 = bf16[1024,128]{0,1:T(8,128)(2,1)S(1)} collective-permute-done((bf16[1024,128]{0,1:T(8,128)(2,1)S(1)}, bf16[1024,128]{0,1:T(8,128)(2,1)S(1)}, u32[]{:S(2)}, u32[]{:S(2)}) %collective-permute-start.11) | collective-permute-done | bytes 262176 | tf_op jit(solution)/shard_map/ppermute | solution.py:19
  155.9 2.4 %collective-permute-done.12 = bf16[1024,128]{0,1:T(8,128)(2,1)S(1)} collective-permute-done((bf16[1024,128]{0,1:T(8,128)(2,1)S(1)}, bf16[1024,128]{0,1:T(8,128)(2,1)S(1)}, u32[]{:S(2)}, u32[]{:S(2)}) %collective-permute-start.12) | collective-permute-done | bytes 262176 | tf_op jit(solution)/shard_map/ppermute | solution.py:19
  158.3 4.0 %collective-permute-done.13 = bf16[1024,128]{0,1:T(8,128)(2,1)S(1)} collective-permute-done((bf16[1024,128]{0,1:T(8,128)(2,1)S(1)}, bf16[1024,128]{0,1:T(8,128)(2,1)S(1)}, u32[]{:S(2)}, u32[]{:S(2)}) %collective-permute-start.13) | collective-permute-done | bytes 262176 | tf_op jit(solution)/shard_map/ppermute | solution.py:19
  162.6 2.6 %collective-permute-done.14 = bf16[1024,512]{0,1:T(8,128)(2,1)S(1)} collective-permute-done((bf16[1024,512]{0,1:T(8,128)(2,1)S(1)}, bf16[1024,512]{0,1:T(8,128)(2,1)S(1)}, u32[]{:S(2)}, u32[]{:S(2)}) %collective-permute-start.14) | collective-permute-done | bytes 1048608 | tf_op jit(solution)/shard_map/ppermute | solution.py:19
  165.3 1.3 fusion.39
  166.6 1.4 fusion.4
  167.9 57.8 %all_to_all.10 = bf16[128,8,896]{2,1,0:T(8,128)(2,1)} all-to-all(bf16[128,8,896]{2,1,0:T(8,128)(2,1)S(1)} %fusion.4), channel_id=1, replica_groups=mesh['z'=8,'y'=4,'x'=4,'ep'=2] {'x','z','y'}, dimensions={0} | all-to-all | bytes 3670016 | tf_op jit(solution)/shard_map/all_to_all | solution.py:228
  225.8 2.7 %shard_map.123 = bf16[16,3584]{1,0:T(8,128)(2,1)} custom-call(s32[1]{0:T(128)} %bitcast.core_ref, bf16[16,7168]{1,0:T(8,128)(2,1)} %hidden_ref.1, bf16[256,16]{1,0:T(8,128)(2,1)} %get-tuple-element.34.mix_ref, bf16[4,256,896]{2,1,0:T(8,128)(2,1)} %bitcast.63), custom_call_target="tpu_custom_call" | custom-call | tf_op jit(solution)/shard_map/pallas_call | solution.py:132
  (65 shorter events, 10.7 us)
Async XLA Ops:
  0.6 109.2 %copy-start = (bf16[16,64,576]{2,1,0:T(8,128)(2,1)S(1)}, bf16[16,64,576]{2,1,0:T(8,128)(2,1)}, u32[]{:S(2)}) copy-start(bf16[16,64,576]{2,1,0:T(8,128)(2,1)} %param.11) | copy-start | bytes 3538948
  3.8 84.0 %all-to-all-start = ((bf16[128,8,896]{2,1,0:T(8,128)(2,1)}), bf16[128,8,896]{2,1,0:T(8,128)(2,1)}, u32[]{:S(2)}, u32[]{:S(2)}) async-start(bf16[128,8,896]{2,1,0:T(8,128)(2,1)} %bitcast.64), calls=%async_computation | async-start | bytes 3670016 | tf_op jit(solution)/shard_map/all_to_all | solution.py:163
  22.9 4.1 %collective-permute-start = (bf16[3584,256]{1,0:T(8,128)(2,1)}, bf16[3584,256]{1,0:T(8,128)(2,1)}, u32[]{:S(2)}, u32[]{:S(2)}) collective-permute-start(bf16[3584,256]{1,0:T(8,128)(2,1)} %get-tuple-element.47), channel_id=1, source_target_pairs={{0,1},{1,0},{2,3},{3,2},{4,5},{5,4},{6,7},{7,6},{8,9},{9,8},{10,11... | collective-permute-start | bytes 5505032 | tf_op jit(solution)/shard_map/ppermute | solution.py:19
  30.4 54.1 %collective-permute-start.1 = (bf16[896,512]{1,0:T(8,128)(2,1)}, bf16[896,512]{1,0:T(8,128)(2,1)}, u32[]{:S(2)}, u32[]{:S(2)}) collective-permute-start(bf16[896,512]{1,0:T(8,128)(2,1)} %get-tuple-element.45), channel_id=1, source_target_pairs={{0,6},{2,0},{4,2},{6,4},{1,7},{3,1},{5,3},{7,5},{8,14},{10,8},{12,... | collective-permute-start | bytes 2752520 | tf_op jit(solution)/shard_map/ppermute | solution.py:19
  33.6 50.8 %collective-permute-start.2 = (bf16[896,512]{1,0:T(8,128)(2,1)}, bf16[896,512]{1,0:T(8,128)(2,1)}, u32[]{:S(2)}, u32[]{:S(2)}) collective-permute-start(bf16[896,512]{1,0:T(8,128)(2,1)} %get-tuple-element.46), channel_id=1, source_target_pairs={{0,4},{2,6},{4,0},{6,2},{1,5},{3,7},{5,1},{7,3},{8,12},{10,14},{12... | collective-permute-start | bytes 2752520 | tf_op jit(solution)/shard_map/ppermute | solution.py:19
  34.0 53.9 %collective-permute-start.3 = (bf16[896,512]{1,0:T(8,128)(2,1)}, bf16[896,512]{1,0:T(8,128)(2,1)}, u32[]{:S(2)}, u32[]{:S(2)}) collective-permute-start(bf16[896,512]{1,0:T(8,128)(2,1)} %get-tuple-element.43), channel_id=1, source_target_pairs={{0,2},{2,4},{4,6},{6,0},{1,3},{3,5},{5,7},{7,1},{8,10},{10,12},{12... | collective-permute-start | bytes 2752520 | tf_op jit(solution)/shard_map/ppermute | solution.py:19
  90.9 13.0 %copy-start.2 = (f32[1024,512]{0,1:T(8,128)}, f32[1024,512]{0,1:T(8,128)S(1)}, u32[]{:S(2)}) copy-start(f32[1024,512]{0,1:T(8,128)S(1)} %fusion.35) | copy-start | bytes 6291460
  94.7 9.1 %copy-start.4 = (f32[1024,512]{0,1:T(8,128)}, f32[1024,512]{0,1:T(8,128)S(1)}, u32[]{:S(2)}) copy-start(f32[1024,512]{0,1:T(8,128)S(1)} %fusion.36) | copy-start | bytes 6291460
  98.5 3.8 %copy-start.6 = (f32[1024,512]{0,1:T(8,128)}, f32[1024,512]{0,1:T(8,128)S(1)}, u32[]{:S(2)}) copy-start(f32[1024,512]{0,1:T(8,128)S(1)} %fusion.38) | copy-start | bytes 6291460
  102.3 1.4 copy-start.8
  104.0 1.5 copy-start.10
  105.5 9.1 %collective-permute-start.4 = (bf16[1024,1024]{0,1:T(8,128)(2,1)}, bf16[1024,1024]{0,1:T(8,128)(2,1)}, u32[]{:S(2)}, u32[]{:S(2)}) collective-permute-start(bf16[1024,1024]{0,1:T(8,128)(2,1)} %pad_maximum_fusion), channel_id=1, source_target_pairs={{0,1},{1,0},{2,3},{3,2},{4,5},{5,4},{6,7},{7,6},{8,9},{9,8},{10,11... | collective-permute-start | bytes 6291464 | tf_op jit(solution)/shard_map/ppermute | solution.py:19
  109.9 3.7 %copy-start.1 = (bf16[16,128,576]{2,1,0:T(8,128)(2,1)S(1)}, bf16[16,128,576]{2,1,0:T(8,128)(2,1)}, u32[]{:S(2)}) copy-start(bf16[16,128,576]{2,1,0:T(8,128)(2,1)} %copy.16) | copy-start | bytes 7077892
  112.5 2.0 copy-start.9
  113.0 1.2 copy-start.11
  113.0 1.9 copy-start.5
  113.0 2.5 %copy-start.7 = (f32[1024,512]{0,1:T(8,128)S(1)}, f32[1024,512]{0,1:T(8,128)}, u32[]{:S(2)}) copy-start(f32[1024,512]{0,1:T(8,128)} %copy-done.6) | copy-start | bytes 6291460
  113.0 1.4 collective-permute-start.8
  114.3 5.5 %collective-permute-start.9 = (bf16[16,32,512]{2,1,0:T(8,128)(2,1)S(1)}, bf16[16,32,512]{2,1,0:T(8,128)(2,1)S(1)}, u32[]{:S(2)}, u32[]{:S(2)}) collective-permute-start(bf16[16,32,512]{2,1,0:T(8,128)(2,1)S(1)} %dynamic-slice_convert_fusion), channel_id=1, source_target_pairs={{0,1},{1,0},{2,3},{3,2},{4,5},{5,4},{6,7},{7,6},{8,9},{9,8},{10,11... | collective-permute-start | bytes 1572872 | tf_op jit(solution)/shard_map/ppermute | solution.py:19
  117.5 16.0 %collective-permute-start.7 = (bf16[1024,256]{0,1:T(8,128)(2,1)S(1)}, bf16[1024,256]{0,1:T(8,128)(2,1)S(1)}, u32[]{:S(2)}, u32[]{:S(2)}) collective-permute-start(bf16[1024,256]{0,1:T(8,128)(2,1)S(1)} %get-tuple-element.50), channel_id=1, source_target_pairs={{0,6},{2,0},{4,2},{6,4},{1,7},{3,1},{5,3},{7,5},{8,14},{10,8},{12,... | collective-permute-start | bytes 1572872 | tf_op jit(solution)/shard_map/ppermute | solution.py:19
  118.2 16.3 %collective-permute-start.6 = (bf16[1024,256]{0,1:T(8,128)(2,1)S(1)}, bf16[1024,256]{0,1:T(8,128)(2,1)S(1)}, u32[]{:S(2)}, u32[]{:S(2)}) collective-permute-start(bf16[1024,256]{0,1:T(8,128)(2,1)S(1)} %get-tuple-element.51), channel_id=1, source_target_pairs={{0,4},{2,6},{4,0},{6,2},{1,5},{3,7},{5,1},{7,3},{8,12},{10,14},{12... | collective-permute-start | bytes 1572872 | tf_op jit(solution)/shard_map/ppermute | solution.py:19
  119.0 26.1 %collective-permute-start.5 = (bf16[1024,256]{0,1:T(8,128)(2,1)S(1)}, bf16[1024,256]{0,1:T(8,128)(2,1)S(1)}, u32[]{:S(2)}, u32[]{:S(2)}) collective-permute-start(bf16[1024,256]{0,1:T(8,128)(2,1)S(1)} %get-tuple-element.49), channel_id=1, source_target_pairs={{0,2},{2,4},{4,6},{6,0},{1,3},{3,5},{5,7},{7,1},{8,10},{10,12},{12... | collective-permute-start | bytes 1572872 | tf_op jit(solution)/shard_map/ppermute | solution.py:19
  119.7 25.3 %copy-start.3 = (f32[1024,512]{0,1:T(8,128)S(1)}, f32[1024,512]{0,1:T(8,128)}, u32[]{:S(2)}) copy-start(f32[1024,512]{0,1:T(8,128)} %copy-done.2) | copy-start | bytes 6291460
  120.5 12.0 %collective-permute-start.10 = (bf16[4,32,512]{2,1,0:T(8,128)(2,1)S(1)}, bf16[4,32,512]{2,1,0:T(8,128)(2,1)S(1)}, u32[]{:S(2)}, u32[]{:S(2)}) collective-permute-start(bf16[4,32,512]{2,1,0:T(8,128)(2,1)S(1)} %copy.22), channel_id=1, source_target_pairs={{0,128},{32,160},{64,192},{96,224},{128,0},{160,32},{192,64},{224,... | collective-permute-start | bytes 393224 | tf_op jit(solution)/shard_map/ppermute | solution.py:19
  146.7 9.2 %collective-permute-start.11 = (bf16[1024,128]{0,1:T(8,128)(2,1)S(1)}, bf16[1024,128]{0,1:T(8,128)(2,1)S(1)}, u32[]{:S(2)}, u32[]{:S(2)}) collective-permute-start(bf16[1024,128]{0,1:T(8,128)(2,1)S(1)} %fusion.14), channel_id=1, source_target_pairs={{0,6},{2,0},{4,2},{6,4},{1,7},{3,1},{5,3},{7,5},{8,14},{10,8},{12,... | collective-permute-start | bytes 786440 | tf_op jit(solution)/shard_map/ppermute | solution.py:19
  147.5 10.8 %collective-permute-start.12 = (bf16[1024,128]{0,1:T(8,128)(2,1)S(1)}, bf16[1024,128]{0,1:T(8,128)(2,1)S(1)}, u32[]{:S(2)}, u32[]{:S(2)}) collective-permute-start(bf16[1024,128]{0,1:T(8,128)(2,1)S(1)} %fusion.14), channel_id=1, source_target_pairs={{0,4},{2,6},{4,0},{6,2},{1,5},{3,7},{5,1},{7,3},{8,12},{10,14},{12... | collective-permute-start | bytes 786440 | tf_op jit(solution)/shard_map/ppermute | solution.py:19
  148.1 14.2 %collective-permute-start.13 = (bf16[1024,128]{0,1:T(8,128)(2,1)S(1)}, bf16[1024,128]{0,1:T(8,128)(2,1)S(1)}, u32[]{:S(2)}, u32[]{:S(2)}) collective-permute-start(bf16[1024,128]{0,1:T(8,128)(2,1)S(1)} %fusion.14), channel_id=1, source_target_pairs={{0,2},{2,4},{4,6},{6,0},{1,3},{3,5},{5,7},{7,1},{8,10},{10,12},{12... | collective-permute-start | bytes 786440 | tf_op jit(solution)/shard_map/ppermute | solution.py:19
  162.3 3.0 %collective-permute-start.14 = (bf16[1024,512]{0,1:T(8,128)(2,1)S(1)}, bf16[1024,512]{0,1:T(8,128)(2,1)S(1)}, u32[]{:S(2)}, u32[]{:S(2)}) collective-permute-start(bf16[1024,512]{0,1:T(8,128)(2,1)S(1)} %constant_dynamic-update-slice_fusion), channel_id=1, source_target_pairs={{0,1},{1,0},{2,3},{3,2},{4,5},{5,4},{6,7},{7,6},{8,9},{9,8},{10,11... | collective-permute-start | bytes 3145736 | tf_op jit(solution)/shard_map/ppermute | solution.py:19

commit v5 on v2

--- a/solution.py
+++ b/solution.py
@@ -58,8 +58,8 @@
     slots = EXPERTS * CAP
     top = routes.shape[1]
 
-    def kernel(core_ref, all_ref, half_ref, gain_ref, routes_ref, gates_ref, out_ref, mix_ref):
-        del core_ref
+    def kernel(core_ref, all_ref, gain_ref, routes_ref, gates_ref, out_ref, mix_ref):
+        base = core_ref[0] * half
         ids = routes_ref[...].astype(F32)
         gates = gates_ref[...].astype(F32)
         place = lax.broadcasted_iota(jnp.int32, (slots, requests), 0)
@@ -81,62 +81,47 @@
         inverse = lax.rsqrt(jnp.mean(wide * wide, axis=1, keepdims=True) + 1e-06)
         for start in range(0, half, 512):
             columns = slice(start, start + 512)
-            normed = half_ref[:, columns].astype(F32) * inverse * gain_ref[:, columns]
+            own = pl.ds(pl.multiple_of(base + start, 128), 512)
+            normed = all_ref[:, own].astype(F32) * inverse * gain_ref[:, own]
             out_ref[:, columns] = jnp.dot(
                 chosen, normed.astype(BF), preferred_element_type=F32
             ).astype(BF)
 
+    vmem = pl.BlockSpec(memory_space=pltpu.VMEM)
     return pl.pallas_call(
         kernel,
         out_shape=(
             jax.ShapeDtypeStruct((slots, half), BF),
             jax.ShapeDtypeStruct((slots, requests), BF),
         ),
-        grid_spec=pltpu.PrefetchScalarGridSpec(
-            num_scalar_prefetch=1,
-            grid=(1,),
-            in_specs=[
-                pl.BlockSpec((requests, model_width), lambda i, c: (0, 0)),
-                pl.BlockSpec((requests, half), lambda i, c: (0, c[0])),
-                pl.BlockSpec((1, half), lambda i, c: (0, c[0])),
-                pl.BlockSpec((top, requests), lambda i, c: (0, 0)),
-                pl.BlockSpec((top, requests), lambda i, c: (0, 0)),
-            ],
-            out_specs=(
-                pl.BlockSpec((slots, half), lambda i, c: (0, 0)),
-                pl.BlockSpec((slots, requests), lambda i, c: (0, 0)),
-            ),
-        ),
-    )(core.reshape(1), hidden, hidden, norm_gain.reshape(1, -1), routes.T, gate_weights.T)
+        in_specs=[pl.BlockSpec(memory_space=pltpu.SMEM)] + [vmem] * 4,
+        out_specs=(vmem, vmem),
+    )(core.reshape(1), hidden, norm_gain.reshape(1, -1), routes.T, gate_weights.T)
 
 
 def add_experts(core, hidden, mix, returned):
     requests = hidden.shape[0]
     blocks, slots, width = returned.shape
+    half = blocks * width
 
     def kernel(core_ref, hidden_ref, mix_ref, returned_ref, out_ref):
-        del core_ref
-        weighted = lax.dot_general(
-            mix_ref[...],
-            returned_ref[0],
-            (((0,), (0,)), ((), ())),
-            preferred_element_type=F32,
-        )
-        out_ref[...] = (hidden_ref[...].astype(F32) + weighted).astype(BF)
-
+        own = hidden_ref[:, pl.ds(pl.multiple_of(core_ref[0] * half, 128), half)]
+        for n in range(blocks):
+            columns = slice(n * width, (n + 1) * width)
+            weighted = lax.dot_general(
+                mix_ref[...],
+                returned_ref[n],
+                (((0,), (0,)), ((), ())),
+                preferred_element_type=F32,
+            )
+            out_ref[:, columns] = (own[:, columns].astype(F32) + weighted).astype(BF)
+
+    vmem = pl.BlockSpec(memory_space=pltpu.VMEM)
     return pl.pallas_call(
         kernel,
-        out_shape=jax.ShapeDtypeStruct((requests, blocks * width), BF),
-        grid_spec=pltpu.PrefetchScalarGridSpec(
-            num_scalar_prefetch=1,
-            grid=(blocks,),
-            in_specs=[
-                pl.BlockSpec((requests, width), lambda i, c: (0, c[0] * blocks + i)),
-                pl.BlockSpec((slots, requests), lambda i, c: (0, 0)),
-                pl.BlockSpec((1, slots, width), lambda i, c: (i, 0, 0)),
-            ],
-            out_specs=pl.BlockSpec((requests, width), lambda i, c: (0, i)),
-        ),
+        out_shape=jax.ShapeDtypeStruct((requests, half), BF),
+        in_specs=[pl.BlockSpec(memory_space=pltpu.SMEM)] + [vmem] * 3,
+        out_specs=vmem,
     )(core.reshape(1), hidden, mix, returned)
 
 

time: 212 us -> 211 us (level)
  no operation moved by 1% of the time
where the time goes in v5:
time: 211 us; the launch traced here: 210 us
  waiting for transfers between devices  86 us (41%)
  blocking collectives  59.2 us (28%)
  starting transfers between devices  25.1 us (12%)
  matrix products  13.5 us (6%)
  other arithmetic  11.3 us (5%)
  local copies, waits for them, and re-layouts  8.5 us (4%)
  Pallas kernels  5.86 us (3%)
    all_to_all x1, blocking collectives, local(): lax.all_to_all(expert_out.reshape(4 * EXPERTS, CAP, -1), ('x',) + PLANE,...  59.2 us
    ppermute x14, waiting for transfers between devices, shifted(): lax.ppermute(x, axis, [(i, (i + by) % devices) for i in range(devices)])  53.2 us
    all_to_all x1, waiting for transfers between devices, local(): lax.all_to_all(outbound.reshape(EXPERTS, CAP, half), PLANE, split_axis=0,...  32.7 us
    ppermute x14, starting transfers between devices, shifted(): lax.ppermute(x, axis, [(i, (i + by) % devices) for i in range(devices)])  13.7 us
    all_to_all x1, starting transfers between devices, local(): lax.all_to_all(outbound.reshape(EXPERTS, CAP, half), PLANE, split_axis=0,...  11.4 us
    dot_general x5, matrix products, products(): return [jnp.dot(b, mixed, preferred_element_type=F32) for b in blocks]  7.59 us
    optimization_barrier x1, local copies, waits for them, and re-layouts, local(): lax.optimization_barrier((rows, mixed, near_down, far_down, queries, late...  4.33 us
  transfers between devices with their start and end apart: 15, of which 12 were waited for; matrix products, arithmetic and copies ran while one was open for 13% of the time, Pallas kernels for 0%

profile of v5, /device:TPU:32, one launch (start us, length us, event | category | flops | bytes accessed | tf_op | source)
XLA Modules:
  0.0 210.4 jit_solution(620339022247092636)
XLA Ops:
  0.7 3.2 %shard_map.122 = (bf16[256,3584]{1,0:T(8,128)(2,1)}, bf16[256,16]{1,0:T(8,128)(2,1)}) custom-call(s32[1]{0:T(128)} %bitcast.core_ref, bf16[16,7168]{1,0:T(8,128)(2,1)} %hidden_ref.1, f32[1,7168]{1,0:T(1,128)} %bitcast.100, s32[8,16]{1,0:T(8,128)} %bitcast.101, bf16[8,16]{1,0:T(8,128)(2,1)} %bitcast.102), custom_call_target="tpu_custom_call" | custom-call | tf_op jit(solution)/shard_map/pallas_call | solution.py:91
  3.8 11.4 %all-to-all-start = ((bf16[32,8,3584]{2,1,0:T(8,128)(2,1)}), bf16[32,8,3584]{2,1,0:T(8,128)(2,1)}, u32[]{:S(2)}, u32[]{:S(2)}) async-start(bf16[32,8,3584]{2,1,0:T(8,128)(2,1)} %bitcast.94), calls=%async_computation | async-start | bytes 3670016 | tf_op jit(solution)/shard_map/all_to_all | solution.py:151
  15.2 3.7 %fusion.4 = (bf16[3584,256]{1,0:T(8,128)(2,1)S(1)}, bf16[3584,256]{1,0:T(8,128)(2,1)}) fusion(s32[]{:T(128)S(6)} %select_n.85, bf16[7168,128]{1,0:T(8,128)(2,1)} %bitcast.95, bf16[7168,128]{1,0:T(8,128)(2,1)} %bitcast.96, s32[]{:T(128)S(6)} %select_n.86), kind=kLoop, calls=%fused_computation.10 | loop fusion | flops 7340032 | bytes 7340040 | tf_op jit(solution)/shard_map/concatenate | solution.py:155
  18.9 1.7 dynamic-slice_bitcast_fusion.3
  20.7 1.4 pad_maximum_fusion.2
  23.0 3.5 %pad_maximum_fusion = bf16[3584,512]{1,0:T(8,128)(2,1)} fusion(bf16[3584,256]{1,0:T(8,128)(2,1)} %collective-permute-done, bf16[3584,256]{1,0:T(8,128)(2,1)S(1)} %get-tuple-element.49), kind=kLoop, calls=%fused_computation.4 | loop fusion | flops 7340032 | bytes 7340032 | tf_op jit(solution)/shard_map/concatenate | solution.py:158
  26.6 32.7 %all-to-all-done = bf16[32,8,3584]{2,1,0:T(8,128)(2,1)} async-done(((bf16[32,8,3584]{2,1,0:T(8,128)(2,1)}), bf16[32,8,3584]{2,1,0:T(8,128)(2,1)}, u32[]{:S(2)}, u32[]{:S(2)}) %all-to-all-start) | async-done | bytes 1835040 | tf_op jit(solution)/shard_map/all_to_all | solution.py:151
  59.3 1.5 collective-permute-start.1
  60.8 1.7 collective-permute-start.2
  62.6 4.3 %copy.16 = bf16[16,128,576]{2,1,0:T(8,128)(2,1)} copy(bf16[16,128,576]{1,2,0:T(8,128)(2,1)} %param.12) | data formatting | bytes 4718592 | tf_op jit(solution)/shard_map/optimization_barrier | solution.py:171
  66.9 2.5 %fusion.35 = (f32[16,64]{1,0:T(8,128)S(1)}, f32[16,64,128]{2,1,0:T(8,128)S(1)}) fusion(bf16[16,64,576]{2,1,0:T(8,128)(2,1)S(1)} %copy-done, bf16[16,128,576]{1,2,0:T(8,128)(2,1)} %param.12, pred[16,128]{1,0:T(8,128)(4,1)S(1)} %broadcast_compare_fusion), kind=kOutput, calls=%fused_computation.88 | convolution fusion | flops 151387136 | bytes 4069376 | tf_op jit(solution)/shard_map/shc,stc->sht/dot_general | solution.py:25
  71.9 2.6 %fusion.36 = f32[256,512]{1,0:T(8,128)S(1)} fusion(bf16[256,3584]{1,0:T(8,128)(2,1)} %bitcast.5, bf16[3584,512]{1,0:T(8,128)(2,1)S(1)} %copy-done.1), kind=kOutput, calls=%fused_computation.89 | convolution fusion | flops 939524096 | bytes 6029312 | tf_op jit(solution)/shard_map/dot_general | solution.py:191
  74.8 1.3 collective-permute-done.3
  77.0 1.5 collective-permute-start.6
  78.6 10.8 %collective-permute-done.6 = bf16[4,32,512]{2,1,0:T(8,128)(2,1)S(1)} collective-permute-done((bf16[4,32,512]{2,1,0:T(8,128)(2,1)S(1)}, bf16[4,32,512]{2,1,0:T(8,128)(2,1)S(1)}, u32[]{:S(2)}, u32[]{:S(2)}) %collective-permute-start.6) | collective-permute-done | bytes 131104 | tf_op jit(solution)/shard_map/ppermute | solution.py:19
  90.2 9.4 %collective-permute-done.1 = bf16[256,3584]{1,0:T(8,128)(2,1)S(1)} collective-permute-done((bf16[256,3584]{1,0:T(8,128)(2,1)}, bf16[256,3584]{1,0:T(8,128)(2,1)S(1)}, u32[]{:S(2)}, u32[]{:S(2)}) %collective-permute-start.1) | collective-permute-done | bytes 1835040 | tf_op jit(solution)/shard_map/ppermute | solution.py:19
  99.7 1.6 collective-permute-start.7
  101.3 1.2 slice.95
  102.6 2.0 collective-permute-start.8
  104.6 1.1 fusion.38
  105.7 2.6 %fusion.37 = f32[256,512]{1,0:T(8,128)S(1)} fusion(bf16[256,3584]{1,0:T(8,128)(2,1)} %collective-permute-done.2, bf16[3584,512]{1,0:T(8,128)(2,1)S(1)} %copy-done.1), kind=kOutput, calls=%fused_computation.90 | convolution fusion | flops 939524096 | bytes 6029312 | tf_op jit(solution)/shard_map/dot_general | solution.py:191
  108.3 11.0 %collective-permute-done.7 = bf16[128,3584]{1,0:T(8,128)(2,1)S(1)} collective-permute-done((bf16[128,3584]{1,0:T(8,128)(2,1)S(1)}, bf16[128,3584]{1,0:T(8,128)(2,1)S(1)}, u32[]{:S(2)}, u32[]{:S(2)}) %collective-permute-start.7) | collective-permute-done | bytes 917536 | tf_op jit(solution)/shard_map/ppermute | solution.py:19
  119.2 1.3 collective-permute-done.8
  122.1 2.3 %collective-permute-done.9 = f32[768,256]{1,0:T(8,128)S(1)} collective-permute-done((f32[768,256]{1,0:T(8,128)S(1)}, f32[768,256]{1,0:T(8,128)S(1)}, u32[]{:S(2)}, u32[]{:S(2)}) %collective-permute-start.9) | collective-permute-done | bytes 786464 | tf_op jit(solution)/shard_map/ppermute | solution.py:19
  124.7 3.2 %collective-permute-start.10 = (bf16[4,256,128]{2,1,0:T(8,128)(2,1)S(1)}, bf16[4,256,128]{2,1,0:T(8,128)(2,1)S(1)}, u32[]{:S(2)}, u32[]{:S(2)}) collective-permute-start(bf16[4,256,128]{2,1,0:T(8,128)(2,1)S(1)} %pad_maximum_fusion.5), channel_id=1, source_target_pairs={{0,6},{2,0},{4,2},{6,4},{1,7},{3,1},{5,3},{7,5},{8,14},{10,8},{12,... | collective-permute-start | bytes 786440 | tf_op jit(solution)/shard_map/ppermute | solution.py:19
  129.2 10.3 %collective-permute-done.10 = bf16[4,256,128]{2,1,0:T(8,128)(2,1)S(1)} collective-permute-done((bf16[4,256,128]{2,1,0:T(8,128)(2,1)S(1)}, bf16[4,256,128]{2,1,0:T(8,128)(2,1)S(1)}, u32[]{:S(2)}, u32[]{:S(2)}) %collective-permute-start.10) | collective-permute-done | bytes 262176 | tf_op jit(solution)/shard_map/ppermute | solution.py:19
  139.5 3.4 %collective-permute-done.12 = bf16[4,256,128]{2,1,0:T(8,128)(2,1)S(1)} collective-permute-done((bf16[4,256,128]{2,1,0:T(8,128)(2,1)S(1)}, bf16[4,256,128]{2,1,0:T(8,128)(2,1)S(1)}, u32[]{:S(2)}, u32[]{:S(2)}) %collective-permute-start.12) | collective-permute-done | bytes 262176 | tf_op jit(solution)/shard_map/ppermute | solution.py:19
  143.3 2.6 %collective-permute-done.13 = bf16[1024,512]{1,0:T(8,128)(2,1)S(1)} collective-permute-done((bf16[1024,512]{1,0:T(8,128)(2,1)S(1)}, bf16[1024,512]{1,0:T(8,128)(2,1)S(1)}, u32[]{:S(2)}, u32[]{:S(2)}) %collective-permute-start.13) | collective-permute-done | bytes 1048608 | tf_op jit(solution)/shard_map/ppermute | solution.py:19
  146.0 1.2 fusion.41
  147.2 1.3 fusion.2
  148.5 59.2 %all_to_all.10 = bf16[128,8,896]{2,1,0:T(8,128)(2,1)} all-to-all(bf16[128,8,896]{2,1,0:T(8,128)(2,1)S(1)} %fusion.2), channel_id=1, replica_groups=mesh['z'=8,'y'=4,'x'=4,'ep'=2] {'x','z','y'}, dimensions={0} | all-to-all | bytes 3670016 | tf_op jit(solution)/shard_map/all_to_all | solution.py:218
  207.7 2.7 %shard_map.123 = bf16[16,3584]{1,0:T(8,128)(2,1)} custom-call(s32[1]{0:T(128)} %bitcast.core_ref, bf16[16,7168]{1,0:T(8,128)(2,1)} %hidden_ref.1, bf16[256,16]{1,0:T(8,128)(2,1)} %get-tuple-element.34.mix_ref, bf16[4,256,896]{2,1,0:T(8,128)(2,1)} %bitcast.93), custom_call_target="tpu_custom_call" | custom-call | tf_op jit(solution)/shard_map/pallas_call | solution.py:120
  (64 shorter events, 9.2 us)
Async XLA Ops:
  0.6 66.3 %copy-start = (bf16[16,64,576]{2,1,0:T(8,128)(2,1)S(1)}, bf16[16,64,576]{2,1,0:T(8,128)(2,1)}, u32[]{:S(2)}) copy-start(bf16[16,64,576]{2,1,0:T(8,128)(2,1)} %param.11) | copy-start | bytes 3538948
  3.8 55.5 %all-to-all-start = ((bf16[32,8,3584]{2,1,0:T(8,128)(2,1)}), bf16[32,8,3584]{2,1,0:T(8,128)(2,1)}, u32[]{:S(2)}, u32[]{:S(2)}) async-start(bf16[32,8,3584]{2,1,0:T(8,128)(2,1)} %bitcast.94), calls=%async_computation | async-start | bytes 3670016 | tf_op jit(solution)/shard_map/all_to_all | solution.py:151
  18.9 4.1 %collective-permute-start = (bf16[3584,256]{1,0:T(8,128)(2,1)}, bf16[3584,256]{1,0:T(8,128)(2,1)}, u32[]{:S(2)}, u32[]{:S(2)}) collective-permute-start(bf16[3584,256]{1,0:T(8,128)(2,1)} %get-tuple-element.50), channel_id=1, source_target_pairs={{0,1},{1,0},{2,3},{3,2},{4,5},{5,4},{6,7},{7,6},{8,9},{9,8},{10,11... | collective-permute-start | bytes 5505032 | tf_op jit(solution)/shard_map/ppermute | solution.py:19
  20.7 1.4 copy-start.5
  59.3 40.2 %collective-permute-start.1 = (bf16[256,3584]{1,0:T(8,128)(2,1)}, bf16[256,3584]{1,0:T(8,128)(2,1)S(1)}, u32[]{:S(2)}, u32[]{:S(2)}) collective-permute-start(bf16[256,3584]{1,0:T(8,128)(2,1)} %bitcast.5), channel_id=1, source_target_pairs={{0,2},{2,4},{4,6},{6,0},{1,3},{3,5},{5,7},{7,1},{8,10},{10,12},{12... | collective-permute-start | bytes 5505032 | tf_op jit(solution)/shard_map/ppermute | solution.py:19
  60.8 38.9 %collective-permute-start.2 = (bf16[256,3584]{1,0:T(8,128)(2,1)}, bf16[256,3584]{1,0:T(8,128)(2,1)}, u32[]{:S(2)}, u32[]{:S(2)}) collective-permute-start(bf16[256,3584]{1,0:T(8,128)(2,1)} %bitcast.5), channel_id=1, source_target_pairs={{0,6},{2,0},{4,2},{6,4},{1,7},{3,1},{5,3},{7,5},{8,14},{10,8},{12,... | collective-permute-start | bytes 5505032 | tf_op jit(solution)/shard_map/ppermute | solution.py:19
  66.9 2.9 %copy-start.2 = (bf16[16,128,576]{2,1,0:T(8,128)(2,1)S(1)}, bf16[16,128,576]{2,1,0:T(8,128)(2,1)}, u32[]{:S(2)}) copy-start(bf16[16,128,576]{2,1,0:T(8,128)(2,1)} %copy.16) | copy-start | bytes 7077892
  69.8 2.0 copy-start.1
  70.5 5.7 %collective-permute-start.5 = (bf16[16,32,512]{2,1,0:T(8,128)(2,1)S(1)}, bf16[16,32,512]{2,1,0:T(8,128)(2,1)S(1)}, u32[]{:S(2)}, u32[]{:S(2)}) collective-permute-start(bf16[16,32,512]{2,1,0:T(8,128)(2,1)S(1)} %dynamic-slice_convert_fusion), channel_id=1, source_target_pairs={{0,1},{1,0},{2,3},{3,2},{4,5},{5,4},{6,7},{7,6},{8,9},{9,8},{10,11... | collective-permute-start | bytes 1572872 | tf_op jit(solution)/shard_map/ppermute | solution.py:19
  70.7 3.9 %copy-start.6 = (s32[1,4]{1,0:T(1,128)S(1)}, s32[1,4]{1,0:T(1,128)}, u32[]{:S(2)}) copy-start(s32[1,4]{1,0:T(1,128)} %param.14) | copy-start | bytes 52
  70.7 4.0 %collective-permute-start.4 = (f32[2,16,32]{2,1,0:T(8,128)S(1)}, f32[2,16,32]{2,1,0:T(8,128)S(1)}, u32[]{:S(2)}, u32[]{:S(2)}) collective-permute-start(f32[2,16,32]{2,1,0:T(8,128)S(1)} %pad_maximum_fusion.9), channel_id=1, source_target_pairs={{0,1},{1,0},{2,3},{3,2},{4,5},{5,4},{6,7},{7,6},{8,9},{9,8},{10,11... | collective-permute-start | bytes 12296 | tf_op jit(solution)/shard_map/ppermute | solution.py:19
  74.5 1.6 collective-permute-start.3
  77.0 12.3 %collective-permute-start.6 = (bf16[4,32,512]{2,1,0:T(8,128)(2,1)S(1)}, bf16[4,32,512]{2,1,0:T(8,128)(2,1)S(1)}, u32[]{:S(2)}, u32[]{:S(2)}) collective-permute-start(bf16[4,32,512]{2,1,0:T(8,128)(2,1)S(1)} %copy.22), channel_id=1, source_target_pairs={{0,128},{32,160},{64,192},{96,224},{128,0},{160,32},{192,64},{224,... | collective-permute-start | bytes 393224 | tf_op jit(solution)/shard_map/ppermute | solution.py:19
  99.7 19.5 %collective-permute-start.7 = (bf16[128,3584]{1,0:T(8,128)(2,1)S(1)}, bf16[128,3584]{1,0:T(8,128)(2,1)S(1)}, u32[]{:S(2)}, u32[]{:S(2)}) collective-permute-start(bf16[128,3584]{1,0:T(8,128)(2,1)S(1)} %slice.94), channel_id=1, source_target_pairs={{0,2},{2,4},{4,6},{6,0},{1,3},{3,5},{5,7},{7,1},{8,10},{10,12},{12... | collective-permute-start | bytes 2752520 | tf_op jit(solution)/shard_map/ppermute | solution.py:19
  102.6 17.9 %collective-permute-start.8 = (bf16[128,3584]{1,0:T(8,128)(2,1)S(1)}, bf16[128,3584]{1,0:T(8,128)(2,1)S(1)}, u32[]{:S(2)}, u32[]{:S(2)}) collective-permute-start(bf16[128,3584]{1,0:T(8,128)(2,1)S(1)} %slice.95), channel_id=1, source_target_pairs={{0,6},{2,0},{4,2},{6,4},{1,7},{3,1},{5,3},{7,5},{8,14},{10,8},{12,... | collective-permute-start | bytes 2752520 | tf_op jit(solution)/shard_map/ppermute | solution.py:19
  122.0 2.4 %collective-permute-start.9 = (f32[768,256]{1,0:T(8,128)S(1)}, f32[768,256]{1,0:T(8,128)S(1)}, u32[]{:S(2)}, u32[]{:S(2)}) collective-permute-start(f32[768,256]{1,0:T(8,128)S(1)} %slice.123), channel_id=1, source_target_pairs={{0,1},{1,0},{2,3},{3,2},{4,5},{5,4},{6,7},{7,6},{8,9},{9,8},{10,11... | collective-permute-start | bytes 2359304 | tf_op jit(solution)/shard_map/ppermute | solution.py:19
  124.7 14.7 %collective-permute-start.10 = (bf16[4,256,128]{2,1,0:T(8,128)(2,1)S(1)}, bf16[4,256,128]{2,1,0:T(8,128)(2,1)S(1)}, u32[]{:S(2)}, u32[]{:S(2)}) collective-permute-start(bf16[4,256,128]{2,1,0:T(8,128)(2,1)S(1)} %pad_maximum_fusion.5), channel_id=1, source_target_pairs={{0,6},{2,0},{4,2},{6,4},{1,7},{3,1},{5,3},{7,5},{8,14},{10,8},{12,... | collective-permute-start | bytes 786440 | tf_op jit(solution)/shard_map/ppermute | solution.py:19
  127.9 11.5 %collective-permute-start.11 = (bf16[4,256,128]{2,1,0:T(8,128)(2,1)S(1)}, bf16[4,256,128]{2,1,0:T(8,128)(2,1)S(1)}, u32[]{:S(2)}, u32[]{:S(2)}) collective-permute-start(bf16[4,256,128]{2,1,0:T(8,128)(2,1)S(1)} %pad_maximum_fusion.5), channel_id=1, source_target_pairs={{0,4},{2,6},{4,0},{6,2},{1,5},{3,7},{5,1},{7,3},{8,12},{10,14},{12... | collective-permute-start | bytes 786440 | tf_op jit(solution)/shard_map/ppermute | solution.py:19
  128.1 14.8 %collective-permute-start.12 = (bf16[4,256,128]{2,1,0:T(8,128)(2,1)S(1)}, bf16[4,256,128]{2,1,0:T(8,128)(2,1)S(1)}, u32[]{:S(2)}, u32[]{:S(2)}) collective-permute-start(bf16[4,256,128]{2,1,0:T(8,128)(2,1)S(1)} %pad_maximum_fusion.5), channel_id=1, source_target_pairs={{0,2},{2,4},{4,6},{6,0},{1,3},{3,5},{5,7},{7,1},{8,10},{10,12},{12... | collective-permute-start | bytes 786440 | tf_op jit(solution)/shard_map/ppermute | solution.py:19
  143.0 3.0 %copy-start.4 = (bf16[512,896]{1,0:T(8,128)(2,1)S(1)}, bf16[512,896]{1,0:T(8,128)(2,1)}, u32[]{:S(2)}) copy-start(bf16[512,896]{1,0:T(8,128)(2,1)} %get-tuple-element.43) | copy-start | bytes 2752516
  143.2 4.0 %copy-start.3 = (bf16[512,896]{1,0:T(8,128)(2,1)S(1)}, bf16[512,896]{1,0:T(8,128)(2,1)}, u32[]{:S(2)}) copy-start(bf16[512,896]{1,0:T(8,128)(2,1)} %get-tuple-element.42) | copy-start | bytes 2752516
  143.2 2.7 %collective-permute-start.13 = (bf16[1024,512]{1,0:T(8,128)(2,1)S(1)}, bf16[1024,512]{1,0:T(8,128)(2,1)S(1)}, u32[]{:S(2)}, u32[]{:S(2)}) collective-permute-start(bf16[1024,512]{1,0:T(8,128)(2,1)S(1)} %constant_dynamic-slice_fusion), channel_id=1, source_target_pairs={{0,1},{1,0},{2,3},{3,2},{4,5},{5,4},{6,7},{7,6},{8,9},{9,8},{10,11... | collective-permute-start | bytes 3145736 | tf_op jit(solution)/shard_map/ppermute | solution.py:19
